TPU v7x, 32 devices: a whole 2x2x4 slice. The times are simulated.
32 devices in a mesh: ctx: 4 (over x, core), kv: 4 (over z), rep: 2 (over y).
Axes of the slice: x: 2, y: 2, z: 4, core: 2. Of those that a mesh axis runs over, the one named last changes fastest.
Arguments:
- queries: bfloat16 [2048, 8, 12, 128], P(('rep', 'ctx'), 'kv'), parts along dimension 0, may hold values from -100 to 100
- keys: bfloat16 [2048, 8, 128], P(('rep', 'ctx'), 'kv'), parts along dimension 0, may hold values from -4 to 4
- values: bfloat16 [2048, 8, 128], P(('rep', 'ctx'), 'kv'), parts along dimension 0, may hold values from -6 to 6
- output_gradient: bfloat16 [2048, 8, 12, 128], P(('rep', 'ctx'), 'kv'), parts along dimension 0, may hold values from -60 to 60
- band_start: int32 [2048], P(('rep', 'ctx')), parts along dimension 0, may hold values from 0 to 1023, as said below
Outputs:
- grad_query: float32 [2048, 8, 12, 128], P(('rep', 'ctx'), 'kv'), parts along dimension 0
- grad_key: float32 [2048, 8, 128], P(('rep', 'ctx'), 'kv'), parts along dimension 0
- grad_value: float32 [2048, 8, 128], P(('rep', 'ctx'), 'kv'), parts along dimension 0
There are 2 independent parts, one for each index of `rep`. A program takes and returns all parts, laid end to end along the dimension named above; each array names one. Nothing has to cross between parts.
Inputs may be any that keep to these rules, and one draw needn't show every extreme that they name: For every row i, i - 2047 <= band_start[i] <= i and band_start[i] >= 0; the lower end i - 2047 is reached at some rows wherever i >= 2047.
All inputs are finite; a program needn't handle non-finite values.
Results may differ from a plain program's by a relative error of at most 0.003.
Values may be sent and summed in bfloat16 or wider, within the bound.
No kernel may reach another device: no remote copies, remote signals or barrier semaphores. Data moves between devices by JAX's collectives and lax.ppermute only.
A program may use at most 256 MiB of HBM per device.

v0:
```python
import jax
import jax.numpy as jnp
from jax import lax
from jax.sharding import PartitionSpec as P

WINDOW = 2048


def passed_along(block, axis, distance):
    devices = range(lax.axis_size(axis))
    route = [(i - distance, i) for i in devices if i - distance in devices]
    return lax.ppermute(block, axis, route)


def shards(queries, keys, values, output_gradient, band_start):
    rows_here = queries.shape[0]
    head_size = queries.shape[3]
    scaling = head_size ** (-0.5)
    ctx_count = lax.axis_size("ctx")
    reach = min(WINDOW // rows_here, ctx_count - 1)
    position = lax.axis_index("ctx") * rows_here + jnp.arange(rows_here, dtype=jnp.int32)
    own_pair = jnp.stack([keys, values], 0)
    pairs = [own_pair]
    moving = own_pair
    for offset in range(1, reach + 1):
        moving = passed_along(moving, "ctx", 1)
        pairs.append(moving)

    def tile_mask(offset):
        key_pos = position - offset * rows_here
        allowed = (key_pos[None, :] >= band_start[:, None]) & (
            key_pos[None, :] <= position[:, None]
        )
        return allowed[:, None, None, :]

    def tile_products(pair):
        scores = (
            jnp.einsum("rhgd,khd->rhgk", queries, pair[0], preferred_element_type=jnp.float32)
            * scaling
        )
        grad_probs = jnp.einsum(
            "rhgd,khd->rhgk", output_gradient, pair[1], preferred_element_type=jnp.float32
        )
        return (scores, grad_probs)

    stat_shape = queries.shape[:3]
    running_max = jnp.full(stat_shape, -1e30, jnp.float32)
    running_total = jnp.zeros(stat_shape, jnp.float32)
    running_dot = jnp.zeros(stat_shape, jnp.float32)
    for offset in range(reach + 1):
        allowed = tile_mask(offset)
        scores, grad_probs = tile_products(pairs[offset])
        new_max = jnp.maximum(running_max, jnp.max(jnp.where(allowed, scores, -1e30), -1))
        rescale = jnp.exp(running_max - new_max)
        shifted = jnp.where(allowed, jnp.exp(scores - new_max[..., None]), 0.0)
        running_total = running_total * rescale + jnp.sum(shifted, -1)
        running_dot = running_dot * rescale + jnp.sum(shifted * grad_probs, -1)
        running_max = new_max
    log_total = running_max + jnp.log(running_total)
    dot_sum = running_dot / running_total
    query_grad = jnp.zeros(queries.shape, jnp.float32)
    partials = []
    for offset in range(reach + 1):
        allowed = tile_mask(offset)
        scores, grad_probs = tile_products(pairs[offset])
        weights = jnp.where(allowed, jnp.exp(scores - log_total[..., None]), 0.0)
        weights_bf = weights.astype(jnp.bfloat16)
        grad_scores = (weights * (grad_probs - dot_sum[..., None])).astype(jnp.bfloat16)
        query_grad = query_grad + jnp.einsum(
            "rhgk,khd->rhgd", grad_scores, pairs[offset][0], preferred_element_type=jnp.float32
        )
        key_part = jnp.einsum(
            "rhgk,rhgd->khd", grad_scores, queries, preferred_element_type=jnp.float32
        )
        value_part = jnp.einsum(
            "rhgk,rhgd->khd", weights_bf, output_gradient, preferred_element_type=jnp.float32
        )
        partials.append(jnp.stack([key_part, value_part], 0))
    gathered = partials[0]
    for offset in range(1, reach + 1):
        gathered = gathered + passed_along(
            partials[offset].astype(jnp.bfloat16), "ctx", -offset
        ).astype(jnp.float32)
    return (query_grad * scaling, gathered[0] * scaling, gathered[1])


def solution(mesh):
    placed = (
        P(("rep", "ctx"), "kv", None, None),
        P(("rep", "ctx"), "kv", None),
        P(("rep", "ctx"), "kv", None),
        P(("rep", "ctx"), "kv", None, None),
        P(("rep", "ctx")),
    )
    return jax.shard_map(
        shards,
        mesh=mesh,
        in_specs=placed,
        out_specs=(
            P(("rep", "ctx"), "kv", None, None),
            P(("rep", "ctx"), "kv", None),
            P(("rep", "ctx"), "kv", None),
        ),
        check_vma=False,
    )
```

profile of v0, /device:TPU:0, one launch (start us, length us, event | category | flops | bytes accessed | tf_op | source)
XLA Modules:
  0.0 106.2 jit_solution(6316799328690191177)
XLA Ops:
  0.6 0.0 copy-start
  0.6 0.0 copy-start.5
  0.7 1.2 %copy_bitcast_fusion = (bf16[1,256,2,128]{3,1,2,0:T(8,128)(2,1)S(1)}, bf16[1,256,2,128]{3,1,2,0:T(8,128)(2,1)S(1)}) fusion(bf16[256,2,128]{2,1,0:T(2,128)(2,1)} %param.7, bf16[256,2,128]{2,1,0:T(2,128)(2,1)} %param.6), kind=kLoop, calls=%fused_computation.137 | loop fusion | bytes 524288 | tf_op jit(solution)/shard_map/stack | solution.py:22
  1.8 0.7 pad_maximum_fusion
  2.5 2.4 %collective-permute-start = (bf16[2,256,2,128]{3,1,2,0:T(8,128)(2,1)}, bf16[2,256,2,128]{3,1,2,0:T(8,128)(2,1)S(1)}, u32[]{:S(2)}, u32[]{:S(2)}) collective-permute-start(bf16[2,256,2,128]{3,1,2,0:T(8,128)(2,1)} %pad_maximum_fusion), channel_id=1, source_target_pairs={{0,8},{8,16},{16,24},{1,9},{9,17},{17,25},{2,10},{10,18},{18,26},{... | collective-permute-start | bytes 786440 | tf_op jit(solution)/shard_map/ppermute | solution.py:12
  4.9 1.0 compare_and_fusion.3
  5.9 2.7 %fusion.27 = (f32[256,2,12]{0,2,1:T(8,128)S(1)}, f32[2,256,256,12]{2,1,3,0:T(8,128)S(1)}) fusion(pred[256,256]{0,1:T(8,128)(4,1)S(1)} %get-tuple-element.26, bf16[256,2,12,128]{3,1,2,0:T(2,128)(2,1)} %param.5, bf16[256,2,128,1]{2,1,0,3:T(2,128)(2,1)} %bitcast.324), kind=kOutput, calls=%fused_computation.47 | convolution fusion | flops 407365632 | bytes 8085504 | tf_op jit(solution)/shard_map/rhgd,khd->rhgk/dot_general | solution.py:38
  8.6 0.0 collective-permute-done
  8.7 4.5 %collective-permute-start.1 = (bf16[2,256,2,128]{3,1,2,0:T(8,128)(2,1)S(1)}, bf16[2,256,2,128]{3,1,2,0:T(8,128)(2,1)S(1)}, u32[]{:S(2)}, u32[]{:S(2)}) collective-permute-start(bf16[2,256,2,128]{3,1,2,0:T(8,128)(2,1)S(1)} %collective-permute-done), channel_id=1, source_target_pairs={{0,8},{8,16},{16,24},{1,9},{9,17},{17,25},{2,10},{10,18},{18,26},{... | collective-permute-start | bytes 786440 | tf_op jit(solution)/shard_map/ppermute | solution.py:12
  13.2 0.0 copy-done.5
  13.2 1.2 %fusion.22 = (f32[256,2,12]{0,2,1:T(8,128)S(1)}, f32[2,256,256,12]{2,1,3,0:T(8,128)S(1)}) fusion(pred[256,256]{0,1:T(8,128)(4,1)S(1)} %get-tuple-element.29, bf16[256,2,12,128]{3,1,2,0:T(2,128)(2,1)S(1)} %copy-done.5, bf16[2,256,2,128]{3,1,2,0:T(8,128)(2,1)S(1)} %collective-permute-done), kind=kOutput, calls=%fused_computation.39 | convolution fusion | flops 407365632 | bytes 8085504 | tf_op jit(solution)/shard_map/rhgd,khd->rhgk/dot_general | solution.py:38
  14.4 0.0 copy-start.2
  14.4 0.0 collective-permute-done.1
  14.4 6.2 %collective-permute-start.2 = (bf16[2,256,2,128]{3,1,2,0:T(8,128)(2,1)S(1)}, bf16[2,256,2,128]{3,1,2,0:T(8,128)(2,1)S(1)}, u32[]{:S(2)}, u32[]{:S(2)}) collective-permute-start(bf16[2,256,2,128]{3,1,2,0:T(8,128)(2,1)S(1)} %collective-permute-done.1), channel_id=1, source_target_pairs={{0,8},{8,16},{16,24},{1,9},{9,17},{17,25},{2,10},{10,18},{18,26},{... | collective-permute-start | bytes 786440 | tf_op jit(solution)/shard_map/ppermute | solution.py:12
  20.6 0.0 copy-start.11
  20.6 1.2 %fusion.17 = (f32[256,2,12]{0,2,1:T(8,128)S(1)}, f32[2,256,256,12]{2,1,3,0:T(8,128)S(1)}) fusion(pred[256,256]{0,1:T(8,128)(4,1)S(1)} %get-tuple-element.28, bf16[256,2,12,128]{3,1,2,0:T(2,128)(2,1)S(1)} %copy-done.5, bf16[2,256,2,128]{3,1,2,0:T(8,128)(2,1)S(1)} %collective-permute-done.1), kind=kOutput, calls=%fused_computation.31 | convolution fusion | flops 407365632 | bytes 8085504 | tf_op jit(solution)/shard_map/rhgd,khd->rhgk/dot_general | solution.py:38
  21.8 0.0 copy-start.3
  21.8 0.0 collective-permute-done.2
  21.9 1.2 %fusion.12 = (f32[256,2,12]{0,2,1:T(8,128)S(1)}, f32[2,256,256,12]{2,1,3,0:T(8,128)S(1)}) fusion(pred[256,256]{0,1:T(8,128)(4,1)S(1)} %get-tuple-element.27, bf16[256,2,12,128]{3,1,2,0:T(2,128)(2,1)S(1)} %copy-done.5, bf16[2,256,2,128]{3,1,2,0:T(8,128)(2,1)S(1)} %collective-permute-done.2), kind=kOutput, calls=%fused_computation.23 | convolution fusion | flops 407365632 | bytes 8085504 | tf_op jit(solution)/shard_map/rhgd,khd->rhgk/dot_general | solution.py:38
  23.1 0.0 copy-start.4
  23.1 0.0 copy-done
  23.1 0.0 copy-done.11
  23.1 4.9 %fusion.33 = (f32[256,2,12]{0,2,1:T(8,128)S(1)}, f32[256,2,12]{0,2,1:T(8,128)S(1)}, f32[2,256,256,12]{2,1,3,0:T(8,128)}) fusion(f32[2,256,256,12]{2,1,3,0:T(8,128)S(1)} %get-tuple-element.37, f32[256,2,12]{0,2,1:T(8,128)S(1)} %get-tuple-element.25, pred[256,256]{0,1:T(8,128)(4,1)S(1)} %get-tuple-element.26, bf16[256,2,12,128]{3,1,2,0:T(2,128)(2,1)S(1)} %copy-done, ...), kind=kOutput, calls=%fused_computation.53 | convolution fusion | flops 412078080 | bytes 14426112 | tf_op jit(solution)/shard_map/rhgd,khd->rhgk/dot_general | solution.py:41
  28.1 4.0 %fusion.39 = (f32[256,2,12]{0,2,1:T(8,128)S(1)}, f32[256,2,12]{0,2,1:T(8,128)S(1)}, f32[2,256,256,12]{2,1,3,0:T(8,128)}) fusion(f32[2,256,256,12]{2,1,3,0:T(8,128)S(1)} %get-tuple-element.31, f32[256,2,12]{0,2,1:T(8,128)S(1)} %get-tuple-element.14, pred[256,256]{0,1:T(8,128)(4,1)S(1)} %get-tuple-element.27, bf16[256,2,12,128]{3,1,2,0:T(2,128)(2,1)S(1)} %copy-done, ...), kind=kOutput, calls=%fused_computation.59 | convolution fusion | flops 412078080 | bytes 14434304 | tf_op jit(solution)/shard_map/rhgd,khd->rhgk/dot_general | solution.py:41
  32.1 4.0 %fusion.37 = (f32[256,2,12]{0,2,1:T(8,128)S(1)}, f32[256,2,12]{0,2,1:T(8,128)S(1)}, f32[2,256,256,12]{2,1,3,0:T(8,128)}) fusion(f32[2,256,256,12]{2,1,3,0:T(8,128)S(1)} %get-tuple-element.33, f32[256,2,12]{0,2,1:T(8,128)S(1)} %get-tuple-element.15, pred[256,256]{0,1:T(8,128)(4,1)S(1)} %get-tuple-element.28, bf16[256,2,12,128]{3,1,2,0:T(2,128)(2,1)S(1)} %copy-done, ...), kind=kOutput, calls=%fused_computation.57 | convolution fusion | flops 412078080 | bytes 14434304 | tf_op jit(solution)/shard_map/rhgd,khd->rhgk/dot_general | solution.py:41
  36.1 4.0 %fusion.35 = (f32[256,2,12]{0,2,1:T(8,128)S(1)}, f32[256,2,12]{0,2,1:T(8,128)S(1)}, f32[2,256,256,12]{2,1,3,0:T(8,128)}) fusion(f32[2,256,256,12]{2,1,3,0:T(8,128)S(1)} %get-tuple-element.35, f32[256,2,12]{0,2,1:T(8,128)S(1)} %get-tuple-element.16, pred[256,256]{0,1:T(8,128)(4,1)S(1)} %get-tuple-element.29, bf16[256,2,12,128]{3,1,2,0:T(2,128)(2,1)S(1)} %copy-done, ...), kind=kOutput, calls=%fused_computation.55 | convolution fusion | flops 412078080 | bytes 14434304 | tf_op jit(solution)/shard_map/rhgd,khd->rhgk/dot_general | solution.py:41
  40.1 0.1 log_add_fusion
  40.1 0.0 copy-done.2
  40.2 1.6 %fusion.80 = bf16[1,256,2,128]{3,1,2,0:T(8,128)(2,1)S(1)} fusion(f32[2,256,256,12]{2,1,3,0:T(8,128)S(1)} %get-tuple-element.35, f32[256,2,12]{0,2,1:T(8,128)S(1)} %get-tuple-element.19, pred[256,256]{0,1:T(8,128)(4,1)S(1)} %get-tuple-element.29, bf16[256,2,12,128]{3,1,2,0:T(2,128)(2,1)S(1)} %copy-done), kind=kOutput, calls=%fused_computation.89 | convolution fusion | flops 409010176 | bytes 8085504 | tf_op jit(solution)/shard_map/rhgk,rhgd->khd/dot_general | solution.py:75
  41.8 0.0 copy-done.3
  41.8 1.6 %fusion.83 = bf16[1,256,2,128]{3,1,2,0:T(8,128)(2,1)S(1)} fusion(f32[2,256,256,12]{2,1,3,0:T(8,128)S(1)} %get-tuple-element.33, f32[256,2,12]{0,2,1:T(8,128)S(1)} %get-tuple-element.19, pred[256,256]{0,1:T(8,128)(4,1)S(1)} %get-tuple-element.28, bf16[256,2,12,128]{3,1,2,0:T(2,128)(2,1)S(1)} %copy-done), kind=kOutput, calls=%fused_computation.90 | convolution fusion | flops 409010176 | bytes 8085504 | tf_op jit(solution)/shard_map/rhgk,rhgd->khd/dot_general | solution.py:75
  43.5 0.0 copy-done.4
  43.5 1.6 %fusion.86 = bf16[1,256,2,128]{3,1,2,0:T(8,128)(2,1)S(1)} fusion(f32[2,256,256,12]{2,1,3,0:T(8,128)S(1)} %get-tuple-element.31, f32[256,2,12]{0,2,1:T(8,128)S(1)} %get-tuple-element.19, pred[256,256]{0,1:T(8,128)(4,1)S(1)} %get-tuple-element.27, bf16[256,2,12,128]{3,1,2,0:T(2,128)(2,1)S(1)} %copy-done), kind=kOutput, calls=%fused_computation.91 | convolution fusion | flops 409010176 | bytes 8085504 | tf_op jit(solution)/shard_map/rhgk,rhgd->khd/dot_general | solution.py:75
  45.1 1.6 %fusion.53 = f32[1,256,2,128]{3,1,2,0:T(8,128)S(1)} fusion(f32[2,256,256,12]{2,1,3,0:T(8,128)S(1)} %get-tuple-element.37, f32[256,2,12]{0,2,1:T(8,128)S(1)} %get-tuple-element.19, pred[256,256]{0,1:T(8,128)(4,1)S(1)} %get-tuple-element.26, bf16[256,2,12,128]{3,1,2,0:T(2,128)(2,1)S(1)} %copy-done), kind=kOutput, calls=%fused_computation.76 | convolution fusion | flops 408944640 | bytes 8216576 | tf_op jit(solution)/shard_map/rhgk,rhgd->khd/dot_general | solution.py:75
  46.8 21.3 %fusion.2 = (bf16[256,2,12,256]{0,3,2,1:T(8,128)(2,1)}, bf16[256,2,12,256]{0,3,2,1:T(8,128)(2,1)}, bf16[256,2,12,256]{0,3,2,1:T(8,128)(2,1)}, bf16[256,2,12,256]{0,3,2,1:T(8,128)(2,1)}) fusion(f32[2,256,256,12]{2,1,3,0:T(8,128)} %get-tuple-element.38, f32[2,256,256,12]{2,1,3,0:T(8,128)} %copy-done.4, f32[256,2,12]{0,2,1:T(8,128)S(1)} %get-tuple-element.20, ...), kind=kLoop, calls=%fused_computation.4 | loop fusion | flops 37748736 | bytes 63225856 | tf_op jit(solution)/shard_map/convert_element_type | solution.py:68
  68.1 3.0 %fusion.77 = bf16[1,256,2,128]{3,1,2,0:T(8,128)(2,1)S(1)} fusion(bf16[256,2,12,256]{0,3,2,1:T(8,128)(2,1)} %get-tuple-element.21, bf16[256,2,12,128]{3,1,2,0:T(2,128)(2,1)S(1)} %copy-done.5), kind=kOutput, calls=%fused_computation.86 | convolution fusion | flops 402718720 | bytes 4849664 | tf_op jit(solution)/shard_map/rhgk,rhgd->khd/dot_general | solution.py:72
  71.1 0.0 copy-start.6
  71.1 0.0 copy-start.10
  71.1 3.0 %fusion.79 = bf16[1,256,2,128]{3,1,2,0:T(8,128)(2,1)S(1)} fusion(bf16[256,2,12,256]{0,3,2,1:T(8,128)(2,1)} %get-tuple-element.22, bf16[256,2,12,128]{3,1,2,0:T(2,128)(2,1)S(1)} %copy-done.5), kind=kOutput, calls=%fused_computation.88 | convolution fusion | flops 402718720 | bytes 4849664 | tf_op jit(solution)/shard_map/rhgk,rhgd->khd/dot_general | solution.py:72
  74.2 0.0 copy-start.8
  74.2 0.0 copy-done.7
  74.2 1.0 fusion.78
  75.1 0.0 copy-done.6
  75.2 0.0 copy-done.10
  75.2 1.4 %fusion.119 = f32[2,256,12,128]{3,1,2,0:T(8,128)S(1)} fusion(bf16[256,2,12,256]{0,3,2,1:T(8,128)(2,1)S(1)} %copy-done.6, bf16[256,2,128,1]{2,1,0,3:T(2,128)(2,1)S(1)} %bitcast.325), kind=kOutput, calls=%fused_computation.141 | convolution fusion | flops 402653184 | bytes 6422528 | tf_op jit(solution)/shard_map/rhgk,khd->rhgd/dot_general | solution.py:69
  76.6 0.0 copy-done.8
  76.6 0.0 copy-start.9
  76.6 1.3 %fusion.117 = f32[2,128,256,12]{1,2,3,0:T(8,128)S(1)} fusion(bf16[256,2,12,256]{0,3,2,1:T(8,128)(2,1)S(1)} %copy-done.8, bf16[2,256,2,128]{3,1,2,0:T(8,128)(2,1)S(1)} %collective-permute-done), kind=kOutput, calls=%fused_computation.139 | convolution fusion | flops 402653184 | bytes 6422528 | tf_op jit(solution)/shard_map/rhgk,khd->rhgd/dot_general | solution.py:69
  77.9 1.3 %fusion.118 = f32[2,128,256,12]{1,2,3,0:T(8,128)S(1)} fusion(bf16[256,2,12,256]{0,3,2,1:T(8,128)(2,1)S(1)} %copy-done.7, bf16[2,256,2,128]{3,1,2,0:T(8,128)(2,1)S(1)} %collective-permute-done.1), kind=kOutput, calls=%fused_computation.140 | convolution fusion | flops 402653184 | bytes 6422528 | tf_op jit(solution)/shard_map/rhgk,khd->rhgd/dot_general | solution.py:69
  79.2 0.0 copy-done.9
  79.3 1.7 %fusion.40 = f32[256,2,12,128]{3,0,2,1:T(8,128)S(1)} fusion(f32[2,128,256,12]{1,2,3,0:T(8,128)S(1)} %fusion.118, f32[2,128,256,12]{1,2,3,0:T(8,128)S(1)} %fusion.117, f32[2,256,12,128]{3,1,2,0:T(8,128)S(1)} %fusion.119, bf16[256,2,12,256]{0,3,2,1:T(8,128)(2,1)S(1)} %copy-done.9, bf16[2,256,2,128]{3,1,2,0:T(8,128)(2,1)S(1)} %collective-permute-done.2), kind=kOutput, calls=%fused_computation.61 | convolution fusion | flops 405798912 | bytes 15859712 | tf_op jit(solution)/shard_map/rhgk,khd->rhgd/dot_general | solution.py:69
  80.9 0.0 copy-start.1
  80.9 4.1 %copy.39 = f32[256,2,12,128]{3,1,2,0:T(2,128)} copy(f32[256,2,12,128]{3,0,2,1:T(8,128)S(1)} %fusion.40) | data formatting | bytes 6291456
  85.1 1.3 %collective-permute-start.4 = (bf16[2,256,2,128]{3,1,2,0:T(8,128)(2,1)S(1)}, bf16[2,256,2,128]{3,1,2,0:T(8,128)(2,1)S(1)}, u32[]{:S(2)}, u32[]{:S(2)}) collective-permute-start(bf16[2,256,2,128]{3,1,2,0:T(8,128)(2,1)S(1)} %pad_maximum_fusion.2), channel_id=1, source_target_pairs={{16,0},{24,8},{17,1},{25,9},{18,2},{26,10},{19,3},{27,11},{20,4},{... | collective-permute-start | bytes 786440 | tf_op jit(solution)/shard_map/ppermute | solution.py:12
  86.4 1.3 %collective-permute-start.3 = (bf16[2,256,2,128]{3,1,2,0:T(8,128)(2,1)S(1)}, bf16[2,256,2,128]{3,1,2,0:T(8,128)(2,1)S(1)}, u32[]{:S(2)}, u32[]{:S(2)}) collective-permute-start(bf16[2,256,2,128]{3,1,2,0:T(8,128)(2,1)S(1)} %pad_maximum_fusion.1), channel_id=1, source_target_pairs={{8,0},{16,8},{24,16},{9,1},{17,9},{25,17},{10,2},{18,10},{26,18},{... | collective-permute-start | bytes 786440 | tf_op jit(solution)/shard_map/ppermute | solution.py:12
  87.7 1.3 %collective-permute-start.5 = (bf16[2,256,2,128]{3,1,2,0:T(8,128)(2,1)S(1)}, bf16[2,256,2,128]{3,1,2,0:T(8,128)(2,1)S(1)}, u32[]{:S(2)}, u32[]{:S(2)}) collective-permute-start(bf16[2,256,2,128]{3,1,2,0:T(8,128)(2,1)S(1)} %pad_maximum_fusion.3), channel_id=1, source_target_pairs={{24,0},{25,1},{26,2},{27,3},{28,4},{29,5},{30,6},{31,7}} | collective-permute-start | bytes 786440 | tf_op jit(solution)/shard_map/ppermute | solution.py:12
  89.0 1.0 convolution_bitcast_fusion.3
  90.0 9.9 %collective-permute-done.4 = bf16[2,256,2,128]{3,1,2,0:T(8,128)(2,1)S(1)} collective-permute-done((bf16[2,256,2,128]{3,1,2,0:T(8,128)(2,1)S(1)}, bf16[2,256,2,128]{3,1,2,0:T(8,128)(2,1)S(1)}, u32[]{:S(2)}, u32[]{:S(2)}) %collective-permute-start.4) | collective-permute-done | bytes 262176 | tf_op jit(solution)/shard_map/ppermute | solution.py:12
  99.9 0.0 collective-permute-done.3
  99.9 4.3 %collective-permute-done.5 = bf16[2,256,2,128]{3,1,2,0:T(8,128)(2,1)S(1)} collective-permute-done((bf16[2,256,2,128]{3,1,2,0:T(8,128)(2,1)S(1)}, bf16[2,256,2,128]{3,1,2,0:T(8,128)(2,1)S(1)}, u32[]{:S(2)}, u32[]{:S(2)}) %collective-permute-start.5) | collective-permute-done | bytes 262176 | tf_op jit(solution)/shard_map/ppermute | solution.py:12
  104.2 0.1 fusion.90
  104.4 0.9 copy.41
  105.3 0.9 copy.40
  106.2 0.0 copy-done.1
  (8 shorter events, 0.1 us)
Async XLA Ops:
  0.6 22.5 %copy-start = (bf16[256,2,12,128]{3,1,2,0:T(2,128)(2,1)S(1)}, bf16[256,2,12,128]{3,1,2,0:T(2,128)(2,1)}, u32[]{:S(2)}) copy-start(bf16[256,2,12,128]{3,1,2,0:T(2,128)(2,1)} %param.8) | copy-start | bytes 4718596
  0.6 12.5 %copy-start.5 = (bf16[256,2,12,128]{3,1,2,0:T(2,128)(2,1)S(1)}, bf16[256,2,12,128]{3,1,2,0:T(2,128)(2,1)}, u32[]{:S(2)}) copy-start(bf16[256,2,12,128]{3,1,2,0:T(2,128)(2,1)} %param.5) | copy-start | bytes 4718596
  2.5 6.1 %collective-permute-start = (bf16[2,256,2,128]{3,1,2,0:T(8,128)(2,1)}, bf16[2,256,2,128]{3,1,2,0:T(8,128)(2,1)S(1)}, u32[]{:S(2)}, u32[]{:S(2)}) collective-permute-start(bf16[2,256,2,128]{3,1,2,0:T(8,128)(2,1)} %pad_maximum_fusion), channel_id=1, source_target_pairs={{0,8},{8,16},{16,24},{1,9},{9,17},{17,25},{2,10},{10,18},{18,26},{... | collective-permute-start | bytes 786440 | tf_op jit(solution)/shard_map/ppermute | solution.py:12
  8.7 5.7 %collective-permute-start.1 = (bf16[2,256,2,128]{3,1,2,0:T(8,128)(2,1)S(1)}, bf16[2,256,2,128]{3,1,2,0:T(8,128)(2,1)S(1)}, u32[]{:S(2)}, u32[]{:S(2)}) collective-permute-start(bf16[2,256,2,128]{3,1,2,0:T(8,128)(2,1)S(1)} %collective-permute-done), channel_id=1, source_target_pairs={{0,8},{8,16},{16,24},{1,9},{9,17},{17,25},{2,10},{10,18},{18,26},{... | collective-permute-start | bytes 786440 | tf_op jit(solution)/shard_map/ppermute | solution.py:12
  14.4 25.8 %copy-start.2 = (f32[2,256,256,12]{2,1,3,0:T(8,128)}, f32[2,256,256,12]{2,1,3,0:T(8,128)S(1)}, u32[]{:S(2)}) copy-start(f32[2,256,256,12]{2,1,3,0:T(8,128)S(1)} %get-tuple-element.35) | copy-start | bytes 18874372
  14.4 7.4 %collective-permute-start.2 = (bf16[2,256,2,128]{3,1,2,0:T(8,128)(2,1)S(1)}, bf16[2,256,2,128]{3,1,2,0:T(8,128)(2,1)S(1)}, u32[]{:S(2)}, u32[]{:S(2)}) collective-permute-start(bf16[2,256,2,128]{3,1,2,0:T(8,128)(2,1)S(1)} %collective-permute-done.1), channel_id=1, source_target_pairs={{0,8},{8,16},{16,24},{1,9},{9,17},{17,25},{2,10},{10,18},{18,26},{... | collective-permute-start | bytes 786440 | tf_op jit(solution)/shard_map/ppermute | solution.py:12
  20.6 2.5 %copy-start.11 = (bf16[256,2,128]{2,1,0:T(2,128)(2,1)S(1)}, bf16[256,2,128]{2,1,0:T(2,128)(2,1)}, u32[]{:S(2)}) copy-start(bf16[256,2,128]{2,1,0:T(2,128)(2,1)} %param.7) | copy-start | bytes 393220
  21.8 20.0 %copy-start.3 = (f32[2,256,256,12]{2,1,3,0:T(8,128)}, f32[2,256,256,12]{2,1,3,0:T(8,128)S(1)}, u32[]{:S(2)}) copy-start(f32[2,256,256,12]{2,1,3,0:T(8,128)S(1)} %get-tuple-element.33) | copy-start | bytes 18874372
  23.1 20.4 %copy-start.4 = (f32[2,256,256,12]{2,1,3,0:T(8,128)}, f32[2,256,256,12]{2,1,3,0:T(8,128)S(1)}, u32[]{:S(2)}) copy-start(f32[2,256,256,12]{2,1,3,0:T(8,128)S(1)} %get-tuple-element.31) | copy-start | bytes 18874372
  68.1 6.1 %copy-start.7 = (bf16[256,2,12,256]{0,3,2,1:T(8,128)(2,1)S(1)}, bf16[256,2,12,256]{0,3,2,1:T(8,128)(2,1)}, u32[]{:S(2)}) copy-start(bf16[256,2,12,256]{0,3,2,1:T(8,128)(2,1)} %get-tuple-element.23) | copy-start | bytes 9437188
  71.1 4.0 %copy-start.6 = (bf16[256,2,12,256]{0,3,2,1:T(8,128)(2,1)S(1)}, bf16[256,2,12,256]{0,3,2,1:T(8,128)(2,1)}, u32[]{:S(2)}) copy-start(bf16[256,2,12,256]{0,3,2,1:T(8,128)(2,1)} %get-tuple-element.24) | copy-start | bytes 9437188
  71.1 4.0 %copy-start.10 = (bf16[256,2,128]{2,1,0:T(2,128)(2,1)S(1)}, bf16[256,2,128]{2,1,0:T(2,128)(2,1)}, u32[]{:S(2)}) copy-start(bf16[256,2,128]{2,1,0:T(2,128)(2,1)} %param.6) | copy-start | bytes 393220
  74.2 2.4 %copy-start.8 = (bf16[256,2,12,256]{0,3,2,1:T(8,128)(2,1)S(1)}, bf16[256,2,12,256]{0,3,2,1:T(8,128)(2,1)}, u32[]{:S(2)}) copy-start(bf16[256,2,12,256]{0,3,2,1:T(8,128)(2,1)} %get-tuple-element.22) | copy-start | bytes 9437188
  76.6 2.7 %copy-start.9 = (bf16[256,2,12,256]{0,3,2,1:T(8,128)(2,1)S(1)}, bf16[256,2,12,256]{0,3,2,1:T(8,128)(2,1)}, u32[]{:S(2)}) copy-start(bf16[256,2,12,256]{0,3,2,1:T(8,128)(2,1)} %get-tuple-element.21) | copy-start | bytes 9437188
  80.9 25.3 %copy-start.1 = (bf16[256,2,12,128]{3,1,2,0:T(2,128)(2,1)S(1)}, bf16[256,2,12,128]{3,1,2,0:T(2,128)(2,1)}, u32[]{:S(2)}) copy-start(bf16[256,2,12,128]{3,1,2,0:T(2,128)(2,1)} %param.8) | copy-start | bytes 4718596
  85.1 14.9 %collective-permute-start.4 = (bf16[2,256,2,128]{3,1,2,0:T(8,128)(2,1)S(1)}, bf16[2,256,2,128]{3,1,2,0:T(8,128)(2,1)S(1)}, u32[]{:S(2)}, u32[]{:S(2)}) collective-permute-start(bf16[2,256,2,128]{3,1,2,0:T(8,128)(2,1)S(1)} %pad_maximum_fusion.2), channel_id=1, source_target_pairs={{16,0},{24,8},{17,1},{25,9},{18,2},{26,10},{19,3},{27,11},{20,4},{... | collective-permute-start | bytes 786440 | tf_op jit(solution)/shard_map/ppermute | solution.py:12
  86.4 13.6 %collective-permute-start.3 = (bf16[2,256,2,128]{3,1,2,0:T(8,128)(2,1)S(1)}, bf16[2,256,2,128]{3,1,2,0:T(8,128)(2,1)S(1)}, u32[]{:S(2)}, u32[]{:S(2)}) collective-permute-start(bf16[2,256,2,128]{3,1,2,0:T(8,128)(2,1)S(1)} %pad_maximum_fusion.1), channel_id=1, source_target_pairs={{8,0},{16,8},{24,16},{9,1},{17,9},{25,17},{10,2},{18,10},{26,18},{... | collective-permute-start | bytes 786440 | tf_op jit(solution)/shard_map/ppermute | solution.py:12
  87.7 16.5 %collective-permute-start.5 = (bf16[2,256,2,128]{3,1,2,0:T(8,128)(2,1)S(1)}, bf16[2,256,2,128]{3,1,2,0:T(8,128)(2,1)S(1)}, u32[]{:S(2)}, u32[]{:S(2)}) collective-permute-start(bf16[2,256,2,128]{3,1,2,0:T(8,128)(2,1)S(1)} %pad_maximum_fusion.3), channel_id=1, source_target_pairs={{24,0},{25,1},{26,2},{27,3},{28,4},{29,5},{30,6},{31,7}} | collective-permute-start | bytes 786440 | tf_op jit(solution)/shard_map/ppermute | solution.py:12
where the time goes:
time: 107 us; the launch traced here: 106 us
  matrix products  43.5 us (41%)
  other arithmetic  23.3 us (22%)
  starting transfers between devices  16.9 us (16%)
  waiting for transfers between devices  14.3 us (13%)
  local copies, waits for them, and re-layouts  7.13 us (7%)
    convert_element_type x1, other arithmetic, shards(): (weights * (grad_probs - dot_sum[..., None])).astype(jnp.bfloat16)  21.3 us
    dot_general x4, matrix products, tile_products(): jnp.einsum('rhgd,khd->rhgk', output_gradient, pair[1], preferred_element_...  17 us
    ppermute x6, starting transfers between devices, passed_along(): return lax.ppermute(block, axis, route)  16.9 us
    ppermute x6, waiting for transfers between devices, passed_along(): return lax.ppermute(block, axis, route)  14.3 us
    dot_general x4, matrix products, shards(): jnp.einsum('rhgk,rhgd->khd', grad_scores, queries, preferred_element_type...  7.97 us
    dot_general x4, matrix products, shards(): jnp.einsum('rhgk,rhgd->khd', weights_bf, output_gradient, preferred_eleme...  6.55 us
    dot_general x4, matrix products, tile_products(): jnp.einsum('rhgd,khd->rhgk', queries, pair[0], preferred_element_type=jnp...  6.34 us
    unnamed x27, local copies, waits for them, and re-layouts  5.97 us
  transfers between devices with their start and end apart: 6, of which 2 were waited for; matrix products, arithmetic and copies ran while one was open for 7% of the time, Pallas kernels for 0%

commit v1 on v0

v1 whole, which is shorter than its diff:
```python
import functools

import jax
import jax.numpy as jnp
from jax import lax
from jax.experimental import pallas as pl
from jax.experimental.pallas import tpu as pltpu
from jax.sharding import PartitionSpec as P

WINDOW = 2048
LOG2E = 1.4426950408889634
MASKED = -1e30
f32 = jnp.float32
bf16 = jnp.bfloat16


def moved(block, distance):
    devices = range(lax.axis_size("ctx"))
    route = [(i - distance, i) for i in devices if i - distance in devices]
    return lax.ppermute(block, "ctx", route)


def swapped(block):
    return lax.ppermute(block, "ctx", [(i, i ^ 1) for i in range(lax.axis_size("ctx"))])


def attention_kernel(sizes, place_ref, q_ref, do_ref, start_ref, *refs):
    tokens, groups, heads, slots, width = sizes
    kv_refs = refs[:slots]
    dq_ref = refs[slots]
    part_refs = refs[slots + 1 : 2 * slots + 1]
    wide, q_s, do_s, k_s, v_s, bias, w_s, ds_s = refs[2 * slots + 1 :]
    keys = slots * tokens
    per_token = groups * heads
    scale = width**-0.5
    for source, split in ((q_ref, q_s), (do_ref, do_s)):
        wide[: tokens * per_token] = source[...].astype(f32)
        for h in range(heads):
            for g in range(groups):
                split[h, g * tokens : (g + 1) * tokens, :] = wide[
                    pl.ds(g * heads + h, tokens, stride=per_token), :
                ].astype(bf16)
    for slot in range(slots):
        for source, split in ((0, k_s), (1, v_s)):
            wide[: tokens * heads] = kv_refs[slot][source].astype(f32)
            for h in range(heads):
                split[h, slot * tokens : (slot + 1) * tokens, :] = wide[
                    pl.ds(h, tokens, stride=heads), :
                ].astype(bf16)
    row = place_ref[0] + lax.broadcasted_iota(jnp.int32, (tokens, 1), 0)
    for slot in range(slots):
        key = place_ref[1 + slot] + lax.broadcasted_iota(jnp.int32, (1, tokens), 1)
        bias[:, slot * tokens : (slot + 1) * tokens] = jnp.where(
            (key <= row) & (key >= start_ref[...]), 0.0, MASKED
        )
    across = (((1,), (1,)), ((), ()))
    down = (((0,), (0,)), ((), ()))
    for h in range(heads):

        def one_group(g, _):
            rows = pl.ds(pl.multiple_of(g * tokens, tokens), tokens)
            scores = lax.dot_general(q_s[h, rows, :], k_s[h], across, preferred_element_type=f32)
            probs = lax.dot_general(do_s[h, rows, :], v_s[h], across, preferred_element_type=f32)
            x = scores * (scale * LOG2E) + bias[...]
            p = jnp.exp2(x - jnp.max(x, -1, keepdims=True))
            inverse = 1.0 / jnp.sum(p, -1, keepdims=True)
            dot_sum = jnp.sum(p * probs, -1, keepdims=True) * inverse
            w = p * inverse
            w_s[rows, :] = w.astype(bf16)
            ds_s[rows, :] = (w * (probs - dot_sum)).astype(bf16)
            return 0

        lax.fori_loop(0, groups, one_group, 0, unroll=2)
        for g in range(0, groups, 2):
            dq = jnp.dot(
                ds_s[g * tokens : (g + 2) * tokens, :], k_s[h], preferred_element_type=f32
            )
            for k in range(2):
                dq_ref[pl.ds((g + k) * heads + h, tokens, stride=per_token), :] = (
                    dq[k * tokens : (k + 1) * tokens] * scale
                )
        dk = lax.dot_general(q_s[h], ds_s[...], down, preferred_element_type=f32) * scale
        dv = lax.dot_general(do_s[h], w_s[...], down, preferred_element_type=f32)
        for source, grad in ((0, dk), (1, dv)):
            turned = grad.T
            for slot in range(slots):
                wide[
                    pl.ds((source * slots + slot) * tokens * heads + h, tokens, stride=heads), :
                ] = turned[slot * tokens : (slot + 1) * tokens]
    for slot in range(slots):
        for source in range(2):
            first = (source * slots + slot) * tokens * heads
            part_refs[slot][source] = wide[first : first + tokens * heads].astype(
                part_refs[slot].dtype
            )


def attention(place, q, do, start, pairs, tokens, groups, heads):
    width = q.shape[-1]
    slots = len(pairs)
    rows = groups * tokens
    keys = slots * tokens
    vmem = pl.BlockSpec(memory_space=pltpu.VMEM)
    wide_rows = max(rows * heads, 2 * keys * heads)
    return pl.pallas_call(
        functools.partial(attention_kernel, (tokens, groups, heads, slots, width)),
        in_specs=[pl.BlockSpec(memory_space=pltpu.SMEM)] + [vmem] * (3 + slots),
        out_specs=[vmem] * (1 + slots),
        out_shape=[jax.ShapeDtypeStruct((rows * heads, width), f32)]
        + [
            jax.ShapeDtypeStruct((2, tokens * heads, width), f32 if slot == 0 else bf16)
            for slot in range(slots)
        ],
        scratch_shapes=[
            pltpu.VMEM((wide_rows, width), f32),
            pltpu.VMEM((heads, rows, width), bf16),
            pltpu.VMEM((heads, rows, width), bf16),
            pltpu.VMEM((heads, keys, width), bf16),
            pltpu.VMEM((heads, keys, width), bf16),
            pltpu.VMEM((tokens, keys), f32),
            pltpu.VMEM((rows, keys), bf16),
            pltpu.VMEM((rows, keys), bf16),
        ],
        compiler_params=pltpu.CompilerParams(vmem_limit_bytes=62 * 2**20),
    )(place, q, do, start, *pairs)


def shards(queries, keys, values, output_gradient, band_start):
    tokens, heads, groups, width = queries.shape
    ctx = lax.axis_index("ctx")
    count = lax.axis_size("ctx")
    reach = min(WINDOW // tokens, count - 1)
    hops = min((reach + 1) // 2, count // 2 - 1)
    own = jnp.stack([keys.reshape(tokens * heads, width), values.reshape(tokens * heads, width)], 0)
    same = [own] + [moved(own, 2 * d) for d in range(1, hops + 1)]
    other = [swapped(block) for block in same]
    partner = ctx + 1 - 2 * (ctx % 2)
    blocks = [ctx - 2 * d for d in range(hops + 1)] + [partner - 2 * d for d in range(hops + 1)]
    place = jnp.stack([ctx] + blocks).astype(jnp.int32) * tokens

    def flat(a):
        return a.transpose(0, 2, 1, 3).reshape(tokens * groups * heads, width)

    dq, *parts = attention(
        place,
        flat(queries),
        flat(output_gradient),
        band_start.reshape(tokens, 1),
        same + other,
        tokens,
        groups,
        heads,
    )
    back = [swapped(part) for part in parts[hops + 1 :]]
    total = parts[0] + back[0].astype(f32)
    for d in range(1, hops + 1):
        both = (parts[d].astype(f32) + back[d].astype(f32)).astype(bf16)
        total = total + moved(both, -2 * d).astype(f32)
    return (
        dq.reshape(tokens, groups, heads, width).transpose(0, 2, 1, 3),
        total[0].reshape(tokens, heads, width),
        total[1].reshape(tokens, heads, width),
    )


def solution(mesh):
    rows = P(("rep", "ctx"), "kv", None, None)
    keys = P(("rep", "ctx"), "kv", None)
    return jax.shard_map(
        shards,
        mesh=mesh,
        in_specs=(rows, keys, keys, rows, P(("rep", "ctx"))),
        out_specs=(rows, keys, keys),
        check_vma=False,
    )
```

time: 107 us -> 57.2 us (0.53)
  matrix products: 43.5 us -> 0 us
  Pallas kernels: 0 us -> 26.5 us
  other arithmetic: 23.3 us -> 3.71 us
  starting transfers between devices: 16.9 us -> 6.73 us
  local copies, waits for them, and re-layouts: 7.13 us -> 3.16 us
  waiting for transfers between devices: 14.3 us -> 16.1 us
    dot_general x20 -> x0, matrix products: 43.5 us -> none  [the longest x4 17 us: tile_products(): jnp.einsum('rhgd,khd->rhgk', output_gradient, pair[1], preferred_element_...]
    pallas_call x0 -> x1, Pallas kernels: none -> 26.5 us  [attention(): pl.pallas_call(functools.partial(attention_kernel, (tokens, groups, heads...]
    convert_element_type x1, other arithmetic: 21.3 us -> 1.02 us  [shards(): both = (parts[d].astype(f32) + back[d].astype(f32)).astype(bf16)]
    ppermute x6, starting transfers between devices: 16.9 us -> 6.73 us  [the longest x2 6.15 us: moved(): return lax.ppermute(block, 'ctx', route)]
    unnamed x27 -> x8, local copies, waits for them, and re-layouts: 5.97 us -> 0.76 us
    ppermute x6, waiting for transfers between devices: 14.3 us -> 16.1 us  [the longest x2 14.7 us: moved(): return lax.ppermute(block, 'ctx', route)]
    reshape x0 -> x1, local copies, waits for them, and re-layouts: none -> 1.49 us  [shards(): band_start.reshape(tokens, 1)]
    another operation x1, local copies, waits for them, and re-layouts: 1.16 us -> 0.08 us  [shards(): place = jnp.stack([ctx] + blocks).astype(jnp.int32) * tokens]
  transfers between devices with their start and end apart: 6 -> 6, of which waited for: 2 -> 3; matrix products, arithmetic and copies ran while one was open for 7% -> 6% of each run, Pallas kernels for 0% -> 0%
where the time goes in v1:
time: 57.2 us; the launch traced here: 56.9 us
  Pallas kernels  26.5 us (46%)
  waiting for transfers between devices  16.1 us (28%)
  starting transfers between devices  6.73 us (12%)
  other arithmetic  3.71 us (6%)
  local copies, waits for them, and re-layouts  3.16 us (6%)
  between operations  0.71 us (1%)
    pallas_call x1, Pallas kernels, attention(): pl.pallas_call(functools.partial(attention_kernel, (tokens, groups, heads...  26.5 us
    ppermute x2, waiting for transfers between devices, moved(): return lax.ppermute(block, 'ctx', route)  14.7 us
    ppermute x2, starting transfers between devices, moved(): return lax.ppermute(block, 'ctx', route)  6.15 us
    reshape x1, local copies, waits for them, and re-layouts, shards(): band_start.reshape(tokens, 1)  1.49 us
    ppermute x4, waiting for transfers between devices, swapped(): lax.ppermute(block, 'ctx', [(i, i ^ 1) for i in range(lax.axis_size('ctx'...  1.35 us
  transfers between devices with their start and end apart: 6, of which 3 were waited for; matrix products, arithmetic and copies ran while one was open for 6% of the time, Pallas kernels for 0%

profile of v1, /device:TPU:0, one launch (start us, length us, event | category | flops | bytes accessed | tf_op | source)
XLA Modules:
  0.0 56.9 jit_solution(2188511944064516174)
XLA Ops:
  0.6 1.0 %pad_maximum_fusion.refs_0_ = bf16[2,512,128]{2,1,0:T(8,128)(2,1)S(1)} fusion(bf16[1,512,128]{2,1,0:T(8,128)(2,1)} %bitcast.22, bf16[1,512,128]{2,1,0:T(8,128)(2,1)} %bitcast.23), kind=kLoop, calls=%fused_computation.2 | loop fusion | flops 131072 | bytes 524288 | tf_op jit(solution)/shard_map/stack | solution.py:134
  1.6 0.0 copy-start
  1.6 4.9 %collective-permute-start = (bf16[2,512,128]{2,1,0:T(8,128)(2,1)S(1)}, bf16[2,512,128]{2,1,0:T(8,128)(2,1)S(1)}, u32[]{:S(2)}, u32[]{:S(2)}) collective-permute-start(bf16[2,512,128]{2,1,0:T(8,128)(2,1)S(1)} %pad_maximum_fusion.refs_0_), channel_id=1, source_target_pairs={{0,16},{8,24},{1,17},{9,25},{2,18},{10,26},{3,19},{11,27},{4,20},{... | collective-permute-start | bytes 786440 | tf_op jit(solution)/shard_map/ppermute | solution.py:20
  6.5 0.1 collective-permute-start.1
  6.6 5.5 %collective-permute-done.refs_1_ = bf16[2,512,128]{2,1,0:T(8,128)(2,1)S(1)} collective-permute-done((bf16[2,512,128]{2,1,0:T(8,128)(2,1)S(1)}, bf16[2,512,128]{2,1,0:T(8,128)(2,1)S(1)}, u32[]{:S(2)}, u32[]{:S(2)}) %collective-permute-start) | collective-permute-done | bytes 262176 | tf_op jit(solution)/shard_map/ppermute | solution.py:20
  12.0 0.0 copy-start.1
  12.0 0.0 collective-permute-start.2
  12.0 1.5 %copy.8.start_ref = s32[256,1]{1,0:T(8,128)} copy(s32[256,1]{0,1:T(1,128)} %bitcast.24) | data formatting | bytes 2048 | tf_op jit(solution)/shard_map/reshape | solution.py:148
  13.5 0.1 stack.23
  13.6 0.6 %broadcast_multiply_fusion.place_ref = s32[5]{0:T(128)} fusion(s32[5]{0:T(128)S(1)} %stack.23), kind=kLoop, calls=%fused_computation.3 | loop fusion | flops 5 | bytes 40 | tf_op jit(solution)/shard_map/mul | solution.py:139
  14.2 0.0 collective-permute-done.1.refs_2_
  14.2 0.0 copy-start.2
  14.2 0.0 collective-permute-done.2.refs_3_
  14.2 0.0 copy-start.3
  14.2 0.0 copy-done
  14.2 0.0 copy-done.1
  14.2 0.7 %copy-done.2 = bf16[2,512,128]{2,1,0:T(8,128)(2,1)} copy-done((bf16[2,512,128]{2,1,0:T(8,128)(2,1)}, bf16[2,512,128]{2,1,0:T(8,128)(2,1)S(1)}, u32[]{:S(2)}) %copy-start.2) | copy-done | bytes 262168
  14.9 0.1 copy-done.3
  15.0 26.5 %shard_map.76 = (f32[6144,128]{1,0:T(8,128)}, f32[2,512,128]{2,1,0:T(8,128)}, bf16[2,512,128]{2,1,0:T(8,128)(2,1)}, bf16[2,512,128]{2,1,0:T(8,128)(2,1)}, bf16[2,512,128]{2,1,0:T(8,128)(2,1)}) custom-call(s32[5]{0:T(128)} %broadcast_multiply_fusion.place_ref, bf16[6144,128]{1,0:T(8,128)(2,1)} %bitcast.18, bf16[6144,128]{1,0:T(8,128)(2,1)} %bitcast.19, ...), custom_call_target="tpu_custom_call" | custom-call | tf_op jit(solution)/shard_map/pallas_call | solution.py:105
  41.4 0.5 collective-permute-start.4
  41.9 0.0 collective-permute-start.3
  41.9 1.3 %collective-permute-done.4 = bf16[2,512,128]{2,1,0:T(8,128)(2,1)S(1)} collective-permute-done((bf16[2,512,128]{2,1,0:T(8,128)(2,1)}, bf16[2,512,128]{2,1,0:T(8,128)(2,1)S(1)}, u32[]{:S(2)}, u32[]{:S(2)}) %collective-permute-start.4) | collective-permute-done | bytes 262176 | tf_op jit(solution)/shard_map/ppermute | solution.py:24
  43.3 1.0 %add_convert_fusion = bf16[2,512,128]{2,1,0:T(8,128)(2,1)S(1)} fusion(bf16[2,512,128]{2,1,0:T(8,128)(2,1)S(1)} %collective-permute-done.4, bf16[2,512,128]{2,1,0:T(8,128)(2,1)} %get-tuple-element.11), kind=kLoop, calls=%fused_computation.1 | loop fusion | flops 524288 | bytes 786432 | tf_op jit(solution)/shard_map/convert_element_type | solution.py:157
  44.3 1.3 %collective-permute-start.5 = (bf16[2,512,128]{2,1,0:T(8,128)(2,1)S(1)}, bf16[2,512,128]{2,1,0:T(8,128)(2,1)S(1)}, u32[]{:S(2)}, u32[]{:S(2)}) collective-permute-start(bf16[2,512,128]{2,1,0:T(8,128)(2,1)S(1)} %add_convert_fusion), channel_id=1, source_target_pairs={{16,0},{24,8},{17,1},{25,9},{18,2},{26,10},{19,3},{27,11},{20,4},{... | collective-permute-start | bytes 786440 | tf_op jit(solution)/shard_map/ppermute | solution.py:20
  45.6 0.0 collective-permute-done.3
  45.6 9.3 %collective-permute-done.5 = bf16[2,512,128]{2,1,0:T(8,128)(2,1)S(1)} collective-permute-done((bf16[2,512,128]{2,1,0:T(8,128)(2,1)S(1)}, bf16[2,512,128]{2,1,0:T(8,128)(2,1)S(1)}, u32[]{:S(2)}, u32[]{:S(2)}) %collective-permute-start.5) | collective-permute-done | bytes 262176 | tf_op jit(solution)/shard_map/ppermute | solution.py:20
  54.9 1.1 %convert_add_fusion = f32[2,512,128]{2,1,0:T(8,128)S(1)} fusion(bf16[2,512,128]{2,1,0:T(8,128)(2,1)S(1)} %collective-permute-done.5, f32[2,512,128]{2,1,0:T(8,128)} %get-tuple-element.9, bf16[2,512,128]{2,1,0:T(8,128)(2,1)S(1)} %collective-permute-done.3), kind=kLoop, calls=%fused_computation | loop fusion | flops 524288 | bytes 1572864 | tf_op jit(solution)/shard_map/add | solution.py:158
  56.0 0.8 %fusion = (f32[1,512,128]{2,1,0:T(8,128)}, f32[1,512,128]{2,1,0:T(8,128)}) fusion(f32[2,512,128]{2,1,0:T(8,128)S(1)} %convert_add_fusion), kind=kLoop, calls=%fused_computation.4 | loop fusion | bytes 1048576 | tf_op jit(solution)/shard_map/slice | solution.py:162
Async XLA Ops:
  1.6 12.6 %copy-start = (bf16[2,512,128]{2,1,0:T(8,128)(2,1)}, bf16[2,512,128]{2,1,0:T(8,128)(2,1)S(1)}, u32[]{:S(2)}) copy-start(bf16[2,512,128]{2,1,0:T(8,128)(2,1)S(1)} %pad_maximum_fusion.refs_0_) | copy-start | bytes 786436
  1.6 10.4 %collective-permute-start = (bf16[2,512,128]{2,1,0:T(8,128)(2,1)S(1)}, bf16[2,512,128]{2,1,0:T(8,128)(2,1)S(1)}, u32[]{:S(2)}, u32[]{:S(2)}) collective-permute-start(bf16[2,512,128]{2,1,0:T(8,128)(2,1)S(1)} %pad_maximum_fusion.refs_0_), channel_id=1, source_target_pairs={{0,16},{8,24},{1,17},{9,25},{2,18},{10,26},{3,19},{11,27},{4,20},{... | collective-permute-start | bytes 786440 | tf_op jit(solution)/shard_map/ppermute | solution.py:20
  6.5 7.7 %collective-permute-start.1 = (bf16[2,512,128]{2,1,0:T(8,128)(2,1)S(1)}, bf16[2,512,128]{2,1,0:T(8,128)(2,1)S(1)}, u32[]{:S(2)}, u32[]{:S(2)}) collective-permute-start(bf16[2,512,128]{2,1,0:T(8,128)(2,1)S(1)} %pad_maximum_fusion.refs_0_), channel_id=1, source_target_pairs={{0,8},{8,0},{16,24},{24,16},{1,9},{9,1},{17,25},{25,17},{2,10},{10... | collective-permute-start | bytes 786440 | tf_op jit(solution)/shard_map/ppermute | solution.py:24
  12.0 2.2 %copy-start.1 = (bf16[2,512,128]{2,1,0:T(8,128)(2,1)}, bf16[2,512,128]{2,1,0:T(8,128)(2,1)S(1)}, u32[]{:S(2)}) copy-start(bf16[2,512,128]{2,1,0:T(8,128)(2,1)S(1)} %collective-permute-done.refs_1_) | copy-start | bytes 786436
  12.0 2.2 %collective-permute-start.2 = (bf16[2,512,128]{2,1,0:T(8,128)(2,1)S(1)}, bf16[2,512,128]{2,1,0:T(8,128)(2,1)S(1)}, u32[]{:S(2)}, u32[]{:S(2)}) collective-permute-start(bf16[2,512,128]{2,1,0:T(8,128)(2,1)S(1)} %collective-permute-done.refs_1_), channel_id=1, source_target_pairs={{0,8},{8,0},{16,24},{24,16},{1,9},{9,1},{17,25},{25,17},{2,10},{10... | collective-permute-start | bytes 786440 | tf_op jit(solution)/shard_map/ppermute | solution.py:24
  14.2 0.7 %copy-start.2 = (bf16[2,512,128]{2,1,0:T(8,128)(2,1)}, bf16[2,512,128]{2,1,0:T(8,128)(2,1)S(1)}, u32[]{:S(2)}) copy-start(bf16[2,512,128]{2,1,0:T(8,128)(2,1)S(1)} %collective-permute-done.1.refs_2_) | copy-start | bytes 786436
  14.2 0.8 %copy-start.3 = (bf16[2,512,128]{2,1,0:T(8,128)(2,1)}, bf16[2,512,128]{2,1,0:T(8,128)(2,1)S(1)}, u32[]{:S(2)}) copy-start(bf16[2,512,128]{2,1,0:T(8,128)(2,1)S(1)} %collective-permute-done.2.refs_3_) | copy-start | bytes 786436
  41.4 1.9 %collective-permute-start.4 = (bf16[2,512,128]{2,1,0:T(8,128)(2,1)}, bf16[2,512,128]{2,1,0:T(8,128)(2,1)S(1)}, u32[]{:S(2)}, u32[]{:S(2)}) collective-permute-start(bf16[2,512,128]{2,1,0:T(8,128)(2,1)} %get-tuple-element.12), channel_id=1, source_target_pairs={{0,8},{8,0},{16,24},{24,16},{1,9},{9,1},{17,25},{25,17},{2,10},{10... | collective-permute-start | bytes 786440 | tf_op jit(solution)/shard_map/ppermute | solution.py:24
  41.9 3.7 %collective-permute-start.3 = (bf16[2,512,128]{2,1,0:T(8,128)(2,1)}, bf16[2,512,128]{2,1,0:T(8,128)(2,1)S(1)}, u32[]{:S(2)}, u32[]{:S(2)}) collective-permute-start(bf16[2,512,128]{2,1,0:T(8,128)(2,1)} %get-tuple-element.10), channel_id=1, source_target_pairs={{0,8},{8,0},{16,24},{24,16},{1,9},{9,1},{17,25},{25,17},{2,10},{10... | collective-permute-start | bytes 786440 | tf_op jit(solution)/shard_map/ppermute | solution.py:24
  44.3 10.6 %collective-permute-start.5 = (bf16[2,512,128]{2,1,0:T(8,128)(2,1)S(1)}, bf16[2,512,128]{2,1,0:T(8,128)(2,1)S(1)}, u32[]{:S(2)}, u32[]{:S(2)}) collective-permute-start(bf16[2,512,128]{2,1,0:T(8,128)(2,1)S(1)} %add_convert_fusion), channel_id=1, source_target_pairs={{16,0},{24,8},{17,1},{25,9},{18,2},{26,10},{19,3},{27,11},{20,4},{... | collective-permute-start | bytes 786440 | tf_op jit(solution)/shard_map/ppermute | solution.py:20

commit v2 on v1

v2 whole, which is shorter than its diff:
```python
import functools

import jax
import jax.numpy as jnp
from jax import lax
from jax.experimental import pallas as pl
from jax.experimental.pallas import tpu as pltpu
from jax.sharding import PartitionSpec as P

WINDOW = 2048
LOG2E = 1.4426950408889634
MASKED = -1e30
f32 = jnp.float32
bf16 = jnp.bfloat16
ACROSS = (((1,), (1,)), ((), ()))
DOWN = (((0,), (0,)), ((), ()))
VMEM = pl.BlockSpec(memory_space=pltpu.VMEM)


def moved(block, distance):
    devices = range(lax.axis_size("ctx"))
    route = [(i - distance, i) for i in devices if i - distance in devices]
    return lax.ppermute(block, "ctx", route)


def swapped(block):
    return lax.ppermute(block, "ctx", [(i, i ^ 1) for i in range(lax.axis_size("ctx"))])


def split_heads(pair_refs, k_s, v_s, wide, tokens, heads):
    for slot, pair in enumerate(pair_refs):
        for source, split in ((0, k_s), (1, v_s)):
            wide[: tokens * heads] = pair[source].astype(f32)
            for h in range(heads):
                split[h, slot * tokens : (slot + 1) * tokens, :] = wide[
                    pl.ds(h, tokens, stride=heads), :
                ].astype(bf16)


def join_heads(dk, dv, part_refs, wide, tokens, heads, scale):
    for source, grad in ((0, dk), (1, dv)):
        for slot, part in enumerate(part_refs):
            for h in range(heads):
                block = grad[h, :, slot * tokens : (slot + 1) * tokens].T
                wide[pl.ds(h, tokens, stride=heads), :] = block * scale if source == 0 else block
            part[source] = wide[: tokens * heads].astype(part.dtype)


def fill_bias(bias, start_ref, first_keys, tokens):
    down = lax.broadcasted_iota(jnp.int32, (tokens, tokens), 0)
    along = lax.broadcasted_iota(jnp.int32, (tokens, tokens), 1)
    start = jnp.sum(
        jnp.where(down == along, start_ref[...].astype(f32), 0.0), -1, keepdims=True
    ).astype(jnp.int32)
    row = lax.axis_index("ctx") * tokens + lax.broadcasted_iota(jnp.int32, (tokens, 1), 0)
    for slot, first in enumerate(first_keys):
        key = first + lax.broadcasted_iota(jnp.int32, (1, tokens), 1)
        bias[:, slot * tokens : (slot + 1) * tokens] = jnp.where(
            (key <= row) & (key >= start), 0.0, MASKED
        )


def take(table, column):
    lane = lax.broadcasted_iota(jnp.int32, table.shape, 1)
    return jnp.sum(jnp.where(lane == column, table[...], 0.0), -1, keepdims=True)


def put(table, column, value):
    lane = lax.broadcasted_iota(jnp.int32, table.shape, 1)
    table[...] = jnp.where(lane == column, value, table[...])


def near_kernel(
    sizes, q_ref, do_ref, start_ref, own_ref, partner_ref,
    qs_ref, dos_ref, w_ref, u_ref, k_ref, log_ref, dot_ref,
    wide, v_s, bias, s_a, d_a, s_b, d_b, *copies,
):
    tokens, groups, heads, width, per, kept = sizes
    chunk = per * tokens
    chunks = groups // per * heads
    i = pl.program_id(0)
    first = step_rows(kept, 2 * chunk)
    slope = width**-0.5 * LOG2E
    qs, dos = (qs_ref, dos_ref) if kept else copies

    def products(c, s, d):
        rows = pl.ds(pl.multiple_of(c * chunk, chunk), chunk)
        h = c * per // groups
        s[...] = lax.dot_general(qs[rows, :], k_ref[h], ACROSS, preferred_element_type=f32)
        d[...] = lax.dot_general(dos[rows, :], v_s[h], ACROSS, preferred_element_type=f32)

    def weights(c, half, s, d):
        for g in range(per):
            rows = slice(g * tokens, (g + 1) * tokens)
            out = pl.ds(first + half * chunk + g * tokens, tokens)
            x = s[rows, :] * slope + bias[...]
            dp = d[rows, :]
            m = jnp.max(x, -1, keepdims=True)
            p = jnp.exp2(x - m)
            total = jnp.sum(p, -1, keepdims=True)
            inverse = 1.0 / total
            dot = jnp.sum(p * dp, -1, keepdims=True) * inverse
            w = p * inverse
            w_ref[out, :] = w.astype(bf16)
            u_ref[out, :] = (w * (dp - dot)).astype(bf16)
            put(log_ref, c * per + g, m + jnp.log2(total))
            put(dot_ref, c * per + g, dot)

    @pl.when(i == 0)
    def _():
        for source, split in ((q_ref, qs), (do_ref, dos)):
            wide[...] = source[...].astype(f32)
            for h in range(heads):
                for g in range(groups):
                    at = (h * groups + g) * tokens
                    split[at : at + tokens, :] = wide[
                        pl.ds(g * heads + h, tokens, stride=groups * heads), :
                    ].astype(bf16)
        split_heads((own_ref, partner_ref), k_ref, v_s, wide, tokens, heads)
        ctx = lax.axis_index("ctx")
        fill_bias(bias, start_ref, (ctx * tokens, (ctx + 1 - 2 * (ctx % 2)) * tokens), tokens)
        log_ref[...] = jnp.zeros_like(log_ref)
        dot_ref[...] = jnp.zeros_like(dot_ref)
        products(0, s_a, d_a)

    if not kept:
        both = pl.ds(pl.multiple_of(i * 2 * chunk, 2 * chunk), 2 * chunk)
        qs_ref[...] = qs[both, :]
        dos_ref[...] = dos[both, :]
    products(2 * i + 1, s_b, d_b)
    weights(2 * i, 0, s_a, d_a)
    products(jnp.minimum(2 * i + 2, chunks - 1), s_a, d_a)
    weights(2 * i + 1, 1, s_b, d_b)


def far_kernel(
    sizes, start_ref, log1_ref, dot1_ref, qs_ref, dos_ref, *refs,
):
    tokens, groups, heads, slots, width, per, kept = sizes
    pair_refs = refs[:slots]
    k_ref, ds_ref, log_ref, dot_ref = refs[slots : slots + 4]
    part_refs = refs[slots + 4 : 2 * slots + 4]
    wide, v_s, bias, w_s, dk, dv, s_a, d_a, s_b, d_b = refs[2 * slots + 4 :]
    chunk = per * tokens
    chunks = groups // per * heads
    hops = slots // 2
    i = pl.program_id(0)
    first = step_rows(kept, 2 * chunk)
    slope = width**-0.5 * LOG2E

    def products(c, s, d):
        rows = pl.ds(pl.multiple_of(c * chunk, chunk), chunk)
        h = c * per // groups
        s[...] = lax.dot_general(qs_ref[rows, :], k_ref[h], ACROSS, preferred_element_type=f32)
        d[...] = lax.dot_general(dos_ref[rows, :], v_s[h], ACROSS, preferred_element_type=f32)

    def weights(c, half, s, d):
        for g in range(per):
            rows = slice(g * tokens, (g + 1) * tokens)
            out = pl.ds(first + half * chunk + g * tokens, tokens)
            log1 = take(log1_ref, c * per + g)
            dot1 = take(dot1_ref, c * per + g)
            x = s[rows, :] * slope + bias[...]
            dp = d[rows, :]
            m = jnp.maximum(jnp.max(x, -1, keepdims=True), log1)
            p = jnp.exp2(x - m)
            before = jnp.exp2(log1 - m)
            total = jnp.sum(p, -1, keepdims=True) + before
            inverse = 1.0 / total
            dot = (jnp.sum(p * dp, -1, keepdims=True) + before * dot1) * inverse
            w = p * inverse
            w_s[half * chunk + g * tokens : half * chunk + (g + 1) * tokens, :] = w.astype(bf16)
            ds_ref[out, :] = (w * (dp - dot)).astype(bf16)
            put(log_ref, c * per + g, m + jnp.log2(total))
            put(dot_ref, c * per + g, dot)

    @pl.when(i == 0)
    def _():
        split_heads(pair_refs, k_ref, v_s, wide, tokens, heads)
        ctx = lax.axis_index("ctx")
        partner = ctx + 1 - 2 * (ctx % 2)
        starts = [(ctx - 2 * d) * tokens for d in range(1, hops + 1)]
        starts += [(partner - 2 * d) * tokens for d in range(1, hops + 1)]
        fill_bias(bias, start_ref, starts, tokens)
        log_ref[...] = jnp.zeros_like(log_ref)
        dot_ref[...] = jnp.zeros_like(dot_ref)
        dk[...] = jnp.zeros_like(dk)
        dv[...] = jnp.zeros_like(dv)
        products(0, s_a, d_a)

    products(2 * i + 1, s_b, d_b)
    weights(2 * i, 0, s_a, d_a)
    products(jnp.minimum(2 * i + 2, chunks - 1), s_a, d_a)
    weights(2 * i + 1, 1, s_b, d_b)
    both = pl.ds(pl.multiple_of(i * 2 * chunk, 2 * chunk), 2 * chunk)
    h = i * 2 * per // groups
    these = pl.ds(first, 2 * chunk)
    dk[h] += lax.dot_general(qs_ref[both, :], ds_ref[these, :], DOWN, preferred_element_type=f32)
    dv[h] += lax.dot_general(dos_ref[both, :], w_s[...], DOWN, preferred_element_type=f32)

    @pl.when(i == pl.num_programs(0) - 1)
    def _():
        join_heads(dk, dv, part_refs, wide, tokens, heads, width**-0.5)


def tail_kernel(
    sizes, log1_ref, dot1_ref, log_ref, dot_ref, k1_ref, k2_ref, qs_ref, dos_ref, w1_ref, u1_ref, ds2_ref,
    dq_ref, own_ref, partner_ref,
    wide, w_s, ds_s, dk, dv,
):
    tokens, groups, heads, width, per, kept = sizes
    chunk = per * tokens
    i = pl.program_id(0)
    scale = width**-0.5
    h = i * 2 * per // groups
    first = step_rows(kept, 2 * chunk)
    these = pl.ds(first, 2 * chunk)

    @pl.when(i == 0)
    def _():
        dk[...] = jnp.zeros_like(dk)
        dv[...] = jnp.zeros_like(dv)

    for g in range(2 * per):
        rows = slice(g * tokens, (g + 1) * tokens)
        column = i * 2 * per + g
        share = jnp.exp2(take(log1_ref, column) - take(log_ref, column))
        shift = take(dot1_ref, column) - take(dot_ref, column)
        here = pl.ds(first + g * tokens, tokens)
        w = w1_ref[here, :].astype(f32)
        w_s[rows, :] = (w * share).astype(bf16)
        ds_s[rows, :] = ((u1_ref[here, :].astype(f32) + w * shift) * share).astype(bf16)
    dk[h] += lax.dot_general(qs_ref[these, :], ds_s[...], DOWN, preferred_element_type=f32)
    dv[h] += lax.dot_general(dos_ref[these, :], w_s[...], DOWN, preferred_element_type=f32)
    dq = jnp.dot(ds_s[...], k1_ref[h], preferred_element_type=f32)
    dq += jnp.dot(ds2_ref[these, :], k2_ref[h], preferred_element_type=f32)
    dq *= scale
    group = i * 2 * per % groups
    for g in range(2 * per):
        dq_ref[pl.ds((group + g) * heads + h, tokens, stride=groups * heads), :] = dq[
            g * tokens : (g + 1) * tokens
        ]

    @pl.when(i == pl.num_programs(0) - 1)
    def _():
        join_heads(dk, dv, (own_ref, partner_ref), wide, tokens, heads, scale)


def whole(*shape):
    return pl.BlockSpec(shape, lambda i: (0,) * len(shape))


def stepped(kept, *shape):
    return VMEM if kept else pl.BlockSpec(shape, lambda i: (i, 0))


def params(kept):
    return pltpu.CompilerParams(vmem_limit_bytes=(24 if kept else 60) * 2**20)


def step_rows(kept, rows):
    if not kept:
        return 0
    return pl.multiple_of(pl.program_id(0) * rows, rows)


def near(q, do, start, own, partner, sizes):
    tokens, groups, heads, width, per, kept = sizes
    chunk = per * tokens
    rows = tokens * groups * heads
    keys = 2 * tokens
    return pl.pallas_call(
        functools.partial(near_kernel, sizes),
        grid=(rows // (2 * chunk),),
        in_specs=[VMEM] * 5,
        out_specs=[
            stepped(kept, 2 * chunk, width),
            stepped(kept, 2 * chunk, width),
            stepped(kept, 2 * chunk, keys),
            stepped(kept, 2 * chunk, keys),
            whole(heads, keys, width),
            whole(tokens, 128),
            whole(tokens, 128),
        ],
        out_shape=[
            jax.ShapeDtypeStruct((rows, width), bf16),
            jax.ShapeDtypeStruct((rows, width), bf16),
            jax.ShapeDtypeStruct((rows, keys), bf16),
            jax.ShapeDtypeStruct((rows, keys), bf16),
            jax.ShapeDtypeStruct((heads, keys, width), bf16),
            jax.ShapeDtypeStruct((tokens, 128), f32),
            jax.ShapeDtypeStruct((tokens, 128), f32),
        ],
        scratch_shapes=[
            pltpu.VMEM((rows, width), f32),
            pltpu.VMEM((heads, keys, width), bf16),
            pltpu.VMEM((tokens, keys), f32),
        ]
        + [pltpu.VMEM((chunk, keys), f32)] * 4
        + [pltpu.VMEM((rows, width), bf16)] * (0 if kept else 2),
        compiler_params=params(kept),
        cost_estimate=pl.CostEstimate(
            flops=2 * 2 * rows * (keys) * width,
            bytes_accessed=8 * rows * (keys),
            transcendentals=rows * (keys),
        ),
        name="near",
    )(q, do, start, own, partner)


def far(start, log1, dot1, qs, dos, pairs, sizes):
    tokens, groups, heads, width, per, kept = sizes
    slots = len(pairs)
    chunk = per * tokens
    rows = tokens * groups * heads
    keys = slots * tokens
    return pl.pallas_call(
        functools.partial(far_kernel, (tokens, groups, heads, slots, width, per, kept)),
        grid=(rows // (2 * chunk),),
        in_specs=[VMEM] * (5 + slots),
        out_specs=[
            whole(heads, keys, width),
            stepped(kept, 2 * chunk, keys),
            whole(tokens, 128),
            whole(tokens, 128),
        ]
        + [whole(2, tokens * heads, width)] * slots,
        out_shape=[
            jax.ShapeDtypeStruct((heads, keys, width), bf16),
            jax.ShapeDtypeStruct((rows, keys), bf16),
            jax.ShapeDtypeStruct((tokens, 128), f32),
            jax.ShapeDtypeStruct((tokens, 128), f32),
        ]
        + [jax.ShapeDtypeStruct((2, tokens * heads, width), bf16)] * slots,
        scratch_shapes=[
            pltpu.VMEM((tokens * heads, width), f32),
            pltpu.VMEM((heads, keys, width), bf16),
            pltpu.VMEM((tokens, keys), f32),
            pltpu.VMEM((2 * chunk, keys), bf16),
            pltpu.VMEM((heads, width, keys), f32),
            pltpu.VMEM((heads, width, keys), f32),
        ]
        + [pltpu.VMEM((chunk, keys), f32)] * 4,
        compiler_params=params(kept),
        cost_estimate=pl.CostEstimate(
            flops=2 * 4 * rows * (keys) * width,
            bytes_accessed=8 * rows * (keys),
            transcendentals=rows * (keys),
        ),
        name="far",
    )(start, log1, dot1, qs, dos, *pairs)


def tail(log1, dot1, log, dot, k1, k2, qs, dos, w1, u1, ds2, sizes):
    tokens, groups, heads, width, per, kept = sizes
    chunk = per * tokens
    rows = tokens * groups * heads
    near_keys, far_keys = k1.shape[1], k2.shape[1]
    return pl.pallas_call(
        functools.partial(tail_kernel, sizes),
        grid=(rows // (2 * chunk),),
        in_specs=[whole(tokens, 128)] * 4
        + [
            whole(heads, near_keys, width),
            whole(heads, far_keys, width),
            stepped(kept, 2 * chunk, width),
            stepped(kept, 2 * chunk, width),
            stepped(kept, 2 * chunk, near_keys),
            stepped(kept, 2 * chunk, near_keys),
            stepped(kept, 2 * chunk, far_keys),
        ],
        out_specs=[VMEM] * 3,
        out_shape=[
            jax.ShapeDtypeStruct((rows, width), f32),
            jax.ShapeDtypeStruct((2, tokens * heads, width), f32),
            jax.ShapeDtypeStruct((2, tokens * heads, width), bf16),
        ],
        scratch_shapes=[
            pltpu.VMEM((tokens * heads, width), f32),
            pltpu.VMEM((2 * chunk, near_keys), bf16),
            pltpu.VMEM((2 * chunk, near_keys), bf16),
            pltpu.VMEM((heads, width, near_keys), f32),
            pltpu.VMEM((heads, width, near_keys), f32),
        ],
        compiler_params=params(kept),
        cost_estimate=pl.CostEstimate(
            flops=2 * 3 * rows * (near_keys + far_keys) * width,
            bytes_accessed=8 * rows * (near_keys + far_keys),
            transcendentals=rows * (near_keys + far_keys),
        ),
        name="tail",
    )(log1, dot1, log, dot, k1, k2, qs, dos, w1, u1, ds2)


def shards(queries, keys, values, output_gradient, band_start):
    tokens, heads, groups, width = queries.shape
    count = lax.axis_size("ctx")
    reach = min(WINDOW // tokens, count - 1)
    hops = min((reach + 1) // 2, count // 2 - 1)
    own = jnp.stack([keys.reshape(tokens * heads, width), values.reshape(tokens * heads, width)], 0)
    same = [moved(own, 2 * d) for d in range(1, hops + 1)]
    partner = swapped(own)
    start = band_start.reshape(1, tokens)
    per = next(n for n in (3, 2, 1) if groups % (2 * n) == 0 and n * hops <= 4)
    kept = hops <= 2
    sizes = (tokens, groups, heads, width, per, kept)

    def flat(a):
        return a.transpose(0, 2, 1, 3).reshape(tokens * groups * heads, width)

    qs, dos, w1, u1, k1, log1, dot1 = near(
        flat(queries), flat(output_gradient), start, own, partner, sizes
    )
    *same, log1 = lax.optimization_barrier((*same, log1))
    other = [swapped(block) for block in same]
    k2, ds2, log, dot, *parts = far(start, log1, dot1, qs, dos, same + other, sizes)
    arriving = []
    for d in range(hops):
        crossed = swapped(parts[hops + d])
        both = (parts[d].astype(f32) + crossed.astype(f32)).astype(bf16)
        both, log = lax.optimization_barrier((both, log))
        arriving.append(moved(both, -2 * (d + 1)))
    dq, total, crossing = tail(log1, dot1, log, dot, k1, k2, qs, dos, w1, u1, ds2, sizes)
    crossing, *arriving = lax.optimization_barrier((crossing, *arriving))
    total = total + swapped(crossing).astype(f32)
    for part in arriving:
        total = total + part.astype(f32)
    return (
        dq.reshape(tokens, groups, heads, width).transpose(0, 2, 1, 3),
        total[0].reshape(tokens, heads, width),
        total[1].reshape(tokens, heads, width),
    )


def solution(mesh):
    rows = P(("rep", "ctx"), "kv", None, None)
    keys = P(("rep", "ctx"), "kv", None)
    return jax.shard_map(
        shards,
        mesh=mesh,
        in_specs=(rows, keys, keys, rows, P(("rep", "ctx"))),
        out_specs=(rows, keys, keys),
        check_vma=False,
    )
```

time: 57.2 us -> 53.4 us (0.934)
  waiting for transfers between devices: 16.1 us -> 4.01 us
  Pallas kernels: 26.5 us -> 36 us
  other arithmetic: 3.71 us -> 1.15 us
  local copies, waits for them, and re-layouts: 3.16 us -> 4.31 us
    ppermute x2, waiting for transfers between devices: 14.7 us -> 0.01 us  [moved(): return lax.ppermute(block, 'ctx', route)]
    pallas_call x1 -> x3, Pallas kernels: 26.5 us -> 36 us  [the longest x1 14.1 us: far(): pl.pallas_call(functools.partial(far_kernel, (tokens, groups, heads, slot...]
    unnamed x8 -> x6, local copies, waits for them, and re-layouts: 0.76 us -> 3.49 us
    ppermute x4, waiting for transfers between devices: 1.35 us -> 4.01 us  [swapped(): lax.ppermute(block, 'ctx', [(i, i ^ 1) for i in range(lax.axis_size('ctx'...]
    reshape x1 -> x0, local copies, waits for them, and re-layouts: 1.49 us -> none  [shards(): band_start.reshape(tokens, 1)]
    add x1, other arithmetic: 1.13 us -> 0.08 us  [shards(): total = total + part.astype(f32)]
    convert_element_type x1, other arithmetic: 1.02 us -> 0.07 us  [shards(): both = (parts[d].astype(f32) + crossed.astype(f32)).astype(bf16)]
    ppermute x4, starting transfers between devices: 0.58 us -> 1.25 us  [swapped(): lax.ppermute(block, 'ctx', [(i, i ^ 1) for i in range(lax.axis_size('ctx'...]
  transfers between devices with their start and end apart: 6 -> 6, of which waited for: 3 -> 3; matrix products, arithmetic and copies ran while one was open for 6% -> 0% of each run, Pallas kernels for 0% -> 41%
where the time goes in v2:
time: 53.4 us; the launch traced here: 53.1 us
  Pallas kernels  36 us (67%)
  starting transfers between devices  6.96 us (13%)
  local copies, waits for them, and re-layouts  4.31 us (8%)
  waiting for transfers between devices  4.01 us (8%)
  other arithmetic  1.15 us (2%)
  between operations  0.7 us (1%)
    pallas_call x1, Pallas kernels, far(): pl.pallas_call(functools.partial(far_kernel, (tokens, groups, heads, slot...  14.1 us
    pallas_call x1, Pallas kernels, tail(): pl.pallas_call(functools.partial(tail_kernel, sizes), grid=(rows // (2 *...  11.9 us
    pallas_call x1, Pallas kernels, near(): pl.pallas_call(functools.partial(near_kernel, sizes), grid=(rows // (2 *...  9.98 us
    ppermute x2, starting transfers between devices, moved(): return lax.ppermute(block, 'ctx', route)  5.71 us
    ppermute x4, waiting for transfers between devices, swapped(): lax.ppermute(block, 'ctx', [(i, i ^ 1) for i in range(lax.axis_size('ctx'...  4.01 us
    unnamed x6, local copies, waits for them, and re-layouts  3.49 us
    ppermute x4, starting transfers between devices, swapped(): lax.ppermute(block, 'ctx', [(i, i ^ 1) for i in range(lax.axis_size('ctx'...  1.25 us
  transfers between devices with their start and end apart: 6, of which 3 were waited for; matrix products, arithmetic and copies ran while one was open for 0% of the time, Pallas kernels for 41%

profile of v2, /device:TPU:0, one launch (start us, length us, event | category | flops | bytes accessed | tf_op | source)
XLA Modules:
  0.0 53.1 jit_solution(2916504623197671563)
XLA Ops:
  0.6 1.0 %pad_maximum_fusion.own_ref = bf16[2,512,128]{2,1,0:T(8,128)(2,1)S(1)} fusion(bf16[1,512,128]{2,1,0:T(8,128)(2,1)} %bitcast.20, bf16[1,512,128]{2,1,0:T(8,128)(2,1)} %bitcast.21), kind=kLoop, calls=%fused_computation.2 | loop fusion | flops 131072 | bytes 524288 | tf_op jit(solution)/shard_map/stack | solution.py:400
  1.6 0.5 collective-permute-start.1
  2.1 4.4 %collective-permute-start = (bf16[2,512,128]{2,1,0:T(8,128)(2,1)S(1)}, bf16[2,512,128]{2,1,0:T(8,128)(2,1)S(1)}, u32[]{:S(2)}, u32[]{:S(2)}) collective-permute-start(bf16[2,512,128]{2,1,0:T(8,128)(2,1)S(1)} %pad_maximum_fusion.own_ref), channel_id=1, source_target_pairs={{0,16},{8,24},{1,17},{9,25},{2,18},{10,26},{3,19},{11,27},{4,20},{... | collective-permute-start | bytes 786440 | tf_op jit(solution)/shard_map/ppermute | solution.py:23
  6.6 0.0 collective-permute-done.1.partner_ref
  6.6 0.0 copy-start
  6.6 1.4 %copy-done = bf16[256,2,12,128]{3,1,2,0:T(2,128)(2,1)S(1)} copy-done((bf16[256,2,12,128]{3,1,2,0:T(2,128)(2,1)S(1)}, bf16[256,2,12,128]{3,1,2,0:T(2,128)(2,1)}, u32[]{:S(2)}) %copy-start) | copy-done | bytes 1572888
  8.0 0.0 copy-start.1
  8.0 1.4 %copy-done.1 = bf16[256,2,12,128]{3,1,2,0:T(2,128)(2,1)S(1)} copy-done((bf16[256,2,12,128]{3,1,2,0:T(2,128)(2,1)S(1)}, bf16[256,2,12,128]{3,1,2,0:T(2,128)(2,1)}, u32[]{:S(2)}) %copy-start.1) | copy-done | bytes 1572888
  9.4 0.0 copy-start.2
  9.4 0.7 %copy-done.2 = s32[256]{0:T(256)S(1)} copy-done((s32[256]{0:T(256)S(1)}, s32[256]{0:T(256)}, u32[]{:S(2)}) %copy-start.2) | copy-done | bytes 1048
  10.1 10.0 %near.1 = (bf16[6144,128]{1,0:T(8,128)(2,1)S(1)}, bf16[6144,128]{1,0:T(8,128)(2,1)S(1)}, bf16[6144,512]{1,0:T(8,128)(2,1)S(1)}, bf16[6144,512]{1,0:T(8,128)(2,1)...) custom-call(bf16[6144,128]{1,0:T(8,128)(2,1)S(1)} %bitcast.14, ...), custom_call_target="tpu_custom_call" | custom-call | flops 1610612736 | bytes 25165824 | tf_op jit(solution)/shard_map/near/pallas_call | solution.py:272
  20.1 0.0 collective-permute-done.refs_0_
  20.1 0.3 collective-permute-start.2
  20.3 1.3 %collective-permute-done.2.refs_1_ = bf16[2,512,128]{2,1,0:T(8,128)(2,1)S(1)} collective-permute-done((bf16[2,512,128]{2,1,0:T(8,128)(2,1)S(1)}, bf16[2,512,128]{2,1,0:T(8,128)(2,1)S(1)}, u32[]{:S(2)}, u32[]{:S(2)}) %collective-permute-start.2) | collective-permute-done | bytes 262176 | tf_op jit(solution)/shard_map/ppermute | solution.py:27
  21.7 14.1 %far.1 = (bf16[2,512,128]{2,1,0:T(8,128)(2,1)S(1)}, bf16[6144,512]{1,0:T(8,128)(2,1)S(1)}, f32[256,128]{1,0:T(8,128)S(1)}, f32[256,128]{1,0:T(8,128)S(1)}, bf16[...) custom-call(s32[1,256]{1,0:T(1,128)S(1)} %bitcast.17, f32[256,128]{1,0:T(8,128)S(1)} %get-tuple-element.26.log1_ref, ...), custom_call_target="tpu_custom_call" | custom-call | flops 3221225472 | bytes 25165824 | tf_op jit(solution)/shard_map/far/pallas_call | solution.py:317
  35.8 0.3 collective-permute-start.3
  36.0 1.3 %collective-permute-done.3 = bf16[2,512,128]{2,1,0:T(8,128)(2,1)S(1)} collective-permute-done((bf16[2,512,128]{2,1,0:T(8,128)(2,1)S(1)}, bf16[2,512,128]{2,1,0:T(8,128)(2,1)S(1)}, u32[]{:S(2)}, u32[]{:S(2)}) %collective-permute-start.3) | collective-permute-done | bytes 262176 | tf_op jit(solution)/shard_map/ppermute | solution.py:27
  37.4 0.1 add_convert_fusion
  37.5 1.3 %collective-permute-start.4 = (bf16[2,512,128]{2,1,0:T(8,128)(2,1)S(1)}, bf16[2,512,128]{2,1,0:T(8,128)(2,1)S(1)}, u32[]{:S(2)}, u32[]{:S(2)}) collective-permute-start(bf16[2,512,128]{2,1,0:T(8,128)(2,1)S(1)} %add_convert_fusion), channel_id=1, source_target_pairs={{16,0},{24,8},{17,1},{25,9},{18,2},{26,10},{19,3},{27,11},{20,4},{... | collective-permute-start | bytes 786440 | tf_op jit(solution)/shard_map/ppermute | solution.py:23
  38.8 11.9 %tail.1 = (f32[6144,128]{1,0:T(8,128)}, f32[2,512,128]{2,1,0:T(8,128)S(1)}, bf16[2,512,128]{2,1,0:T(8,128)(2,1)S(1)}) custom-call(f32[256,128]{1,0:T(8,128)S(1)} %get-tuple-element.26.log1_ref, f32[256,128]{1,0:T(8,128)S(1)} %get-tuple-element.27.dot1_ref, f32[256,128]{1,0:T(8,128)S(1)} %get-tuple-element.34.log_ref, ...), custom_call_target="tpu_custom_call" | custom-call | flops 4831838208 | bytes 50331648 | tf_op jit(solution)/shard_map/tail/pallas_call | solution.py:359
  50.7 0.0 collective-permute-done.4
  50.7 0.2 collective-permute-start.5
  50.9 1.3 %collective-permute-done.5 = bf16[2,512,128]{2,1,0:T(8,128)(2,1)S(1)} collective-permute-done((bf16[2,512,128]{2,1,0:T(8,128)(2,1)S(1)}, bf16[2,512,128]{2,1,0:T(8,128)(2,1)S(1)}, u32[]{:S(2)}, u32[]{:S(2)}) %collective-permute-start.5) | collective-permute-done | bytes 262176 | tf_op jit(solution)/shard_map/ppermute | solution.py:27
  52.2 0.1 convert_add_fusion
  52.3 0.8 %fusion = (f32[1,512,128]{2,1,0:T(8,128)}, f32[1,512,128]{2,1,0:T(8,128)}) fusion(f32[2,512,128]{2,1,0:T(8,128)S(1)} %convert_add_fusion), kind=kLoop, calls=%fused_computation.3 | loop fusion | bytes 1048576 | tf_op jit(solution)/shard_map/slice | solution.py:431
Async XLA Ops:
  1.6 4.9 %collective-permute-start.1 = (bf16[2,512,128]{2,1,0:T(8,128)(2,1)S(1)}, bf16[2,512,128]{2,1,0:T(8,128)(2,1)S(1)}, u32[]{:S(2)}, u32[]{:S(2)}) collective-permute-start(bf16[2,512,128]{2,1,0:T(8,128)(2,1)S(1)} %pad_maximum_fusion.own_ref), channel_id=1, source_target_pairs={{0,8},{8,0},{16,24},{24,16},{1,9},{9,1},{17,25},{25,17},{2,10},{10... | collective-permute-start | bytes 786440 | tf_op jit(solution)/shard_map/ppermute | solution.py:27
  2.1 17.9 %collective-permute-start = (bf16[2,512,128]{2,1,0:T(8,128)(2,1)S(1)}, bf16[2,512,128]{2,1,0:T(8,128)(2,1)S(1)}, u32[]{:S(2)}, u32[]{:S(2)}) collective-permute-start(bf16[2,512,128]{2,1,0:T(8,128)(2,1)S(1)} %pad_maximum_fusion.own_ref), channel_id=1, source_target_pairs={{0,16},{8,24},{1,17},{9,25},{2,18},{10,26},{3,19},{11,27},{4,20},{... | collective-permute-start | bytes 786440 | tf_op jit(solution)/shard_map/ppermute | solution.py:23
  6.6 1.4 %copy-start = (bf16[256,2,12,128]{3,1,2,0:T(2,128)(2,1)S(1)}, bf16[256,2,12,128]{3,1,2,0:T(2,128)(2,1)}, u32[]{:S(2)}) copy-start(bf16[256,2,12,128]{3,1,2,0:T(2,128)(2,1)} %param.5) | copy-start | bytes 4718596
  8.0 1.4 %copy-start.1 = (bf16[256,2,12,128]{3,1,2,0:T(2,128)(2,1)S(1)}, bf16[256,2,12,128]{3,1,2,0:T(2,128)(2,1)}, u32[]{:S(2)}) copy-start(bf16[256,2,12,128]{3,1,2,0:T(2,128)(2,1)} %param.8) | copy-start | bytes 4718596
  9.4 0.7 %copy-start.2 = (s32[256]{0:T(256)S(1)}, s32[256]{0:T(256)}, u32[]{:S(2)}) copy-start(s32[256]{0:T(256)} %param.9) | copy-start | bytes 3076
  20.1 1.6 %collective-permute-start.2 = (bf16[2,512,128]{2,1,0:T(8,128)(2,1)S(1)}, bf16[2,512,128]{2,1,0:T(8,128)(2,1)S(1)}, u32[]{:S(2)}, u32[]{:S(2)}) collective-permute-start(bf16[2,512,128]{2,1,0:T(8,128)(2,1)S(1)} %collective-permute-done.refs_0_), channel_id=1, source_target_pairs={{0,8},{8,0},{16,24},{24,16},{1,9},{9,1},{17,25},{25,17},{2,10},{10... | collective-permute-start | bytes 786440 | tf_op jit(solution)/shard_map/ppermute | solution.py:27
  35.8 1.6 %collective-permute-start.3 = (bf16[2,512,128]{2,1,0:T(8,128)(2,1)S(1)}, bf16[2,512,128]{2,1,0:T(8,128)(2,1)S(1)}, u32[]{:S(2)}, u32[]{:S(2)}) collective-permute-start(bf16[2,512,128]{2,1,0:T(8,128)(2,1)S(1)} %get-tuple-element.32), channel_id=1, source_target_pairs={{0,8},{8,0},{16,24},{24,16},{1,9},{9,1},{17,25},{25,17},{2,10},{10... | collective-permute-start | bytes 786440 | tf_op jit(solution)/shard_map/ppermute | solution.py:27
  37.5 13.2 %collective-permute-start.4 = (bf16[2,512,128]{2,1,0:T(8,128)(2,1)S(1)}, bf16[2,512,128]{2,1,0:T(8,128)(2,1)S(1)}, u32[]{:S(2)}, u32[]{:S(2)}) collective-permute-start(bf16[2,512,128]{2,1,0:T(8,128)(2,1)S(1)} %add_convert_fusion), channel_id=1, source_target_pairs={{16,0},{24,8},{17,1},{25,9},{18,2},{26,10},{19,3},{27,11},{20,4},{... | collective-permute-start | bytes 786440 | tf_op jit(solution)/shard_map/ppermute | solution.py:23
  50.7 1.5 %collective-permute-start.5 = (bf16[2,512,128]{2,1,0:T(8,128)(2,1)S(1)}, bf16[2,512,128]{2,1,0:T(8,128)(2,1)S(1)}, u32[]{:S(2)}, u32[]{:S(2)}) collective-permute-start(bf16[2,512,128]{2,1,0:T(8,128)(2,1)S(1)} %get-tuple-element.45), channel_id=1, source_target_pairs={{0,8},{8,0},{16,24},{24,16},{1,9},{9,1},{17,25},{25,17},{2,10},{10... | collective-permute-start | bytes 786440 | tf_op jit(solution)/shard_map/ppermute | solution.py:27

commit v3 on v2

v3 whole, which is shorter than its diff:
```python
import functools

import jax
import jax.numpy as jnp
from jax import lax
from jax.experimental import pallas as pl
from jax.experimental.pallas import tpu as pltpu
from jax.sharding import PartitionSpec as P

WINDOW = 2048
LOG2E = 1.4426950408889634
MASKED = -1e30
f32 = jnp.float32
bf16 = jnp.bfloat16
ACROSS = (((1,), (1,)), ((), ()))
VMEM = pl.BlockSpec(memory_space=pltpu.VMEM)


def moved(block, distance):
    devices = range(lax.axis_size("ctx"))
    route = [(i - distance, i) for i in devices if i - distance in devices]
    return lax.ppermute(block, "ctx", route)


def swapped(block):
    return lax.ppermute(block, "ctx", [(i, i ^ 1) for i in range(lax.axis_size("ctx"))])


def split_heads(pair_refs, k_s, v_s, wide, tokens, heads):
    for slot, pair in enumerate(pair_refs):
        for source, split in ((0, k_s), (1, v_s)):
            wide[: tokens * heads] = pair[source].astype(f32)
            for h in range(heads):
                split[h, slot * tokens : (slot + 1) * tokens, :] = wide[
                    pl.ds(h, tokens, stride=heads), :
                ].astype(bf16)


def join_heads(dk, dv, part_refs, wide, tokens, heads, scale):
    for source, grad in ((0, dk), (1, dv)):
        for slot, part in enumerate(part_refs):
            for h in range(heads):
                block = grad[h, :, slot * tokens : (slot + 1) * tokens].T
                wide[pl.ds(h, tokens, stride=heads), :] = block * scale if source == 0 else block
            part[source] = wide[: tokens * heads].astype(part.dtype)


def fill_bias(bias, start_ref, first_keys, tokens):
    down = lax.broadcasted_iota(jnp.int32, (tokens, tokens), 0)
    along = lax.broadcasted_iota(jnp.int32, (tokens, tokens), 1)
    start = jnp.sum(
        jnp.where(down == along, start_ref[...].astype(f32), 0.0), -1, keepdims=True
    ).astype(jnp.int32)
    row = lax.axis_index("ctx") * tokens + lax.broadcasted_iota(jnp.int32, (tokens, 1), 0)
    for slot, first in enumerate(first_keys):
        key = first + lax.broadcasted_iota(jnp.int32, (1, tokens), 1)
        bias[:, slot * tokens : (slot + 1) * tokens] = jnp.where(
            (key <= row) & (key >= start), 0.0, MASKED
        )


def spread(lanes, width):
    return jnp.concatenate([lanes] * (width // lanes.shape[1]), 1)


def prep_kernel(sizes, q_ref, do_ref, qs_ref, dos_ref, wide, q_in, do_in, arrived):
    tokens, groups, heads, width, per, kept = sizes
    pieces = q_in.shape[0]
    here = tokens // pieces
    size = here * groups * heads
    loads = []
    for n in range(pieces):
        for k, (source, target) in enumerate(((q_ref, q_in), (do_ref, do_in))):
            load = pltpu.make_async_copy(
                source.at[pl.ds(n * size, size), :], target.at[n], arrived.at[n, k]
            )
            load.start()
            loads.append(load)
    for n in range(pieces):
        for k, (source, split) in enumerate(((q_in, qs_ref), (do_in, dos_ref))):
            loads[2 * n + k].wait()
            wide[2 * n + k] = source[n].astype(f32)
            for h in range(heads):
                for g in range(groups):
                    at = (h * groups + g) * tokens + n * here
                    split[at : at + here, :] = wide[
                        2 * n + k, pl.ds(g * heads + h, here, stride=groups * heads), :
                    ].astype(bf16)


def near_kernel(
    sizes, qs, dos, start_ref, own_ref, partner_ref,
    w_ref, u_ref, k_ref, log_ref, mean_ref, qt_ref, dot_ref,
    wide, v_s, bias, s_a, d_a, s_b, d_b,
):
    tokens, groups, heads, width, per, kept = sizes
    chunk = per * tokens
    chunks = groups // per * heads
    i = pl.program_id(0)
    first = step_rows(kept, 2 * chunk)
    slope = width**-0.5 * LOG2E

    def products(c, s, d):
        rows = pl.ds(pl.multiple_of(c * chunk, chunk), chunk)
        h = c * per // groups
        s[...] = lax.dot_general(qs[rows, :], k_ref[h], ACROSS, preferred_element_type=f32)
        d[...] = lax.dot_general(dos[rows, :], v_s[h], ACROSS, preferred_element_type=f32)

    def weights(c, half, s, d):
        for g in range(per):
            rows = slice(g * tokens, (g + 1) * tokens)
            out = pl.ds(first + half * chunk + g * tokens, tokens)
            x = s[rows, :] * slope + bias[...]
            dp = d[rows, :]
            m = jnp.max(x, -1, keepdims=True)
            p = jnp.exp2(x - m)
            total = jnp.sum(p, -1, keepdims=True)
            inverse = 1.0 / total
            dot = jnp.sum(p * dp, -1, keepdims=True) * inverse
            w = p * inverse
            w_ref[out, :] = w.astype(bf16)
            u_ref[out, :] = (w * (dp - dot)).astype(bf16)
            log_ref[out, :] = jnp.broadcast_to(m + jnp.log2(total), (tokens, 128))
            mean_ref[out, :] = jnp.broadcast_to(dot, (tokens, 128))

    @pl.when(i == 0)
    def _():
        split_heads((own_ref, partner_ref), k_ref, v_s, wide, tokens, heads)
        ctx = lax.axis_index("ctx")
        fill_bias(bias, start_ref, (ctx * tokens, (ctx + 1 - 2 * (ctx % 2)) * tokens), tokens)
        products(0, s_a, d_a)

    both = pl.ds(pl.multiple_of(i * 2 * chunk, 2 * chunk), 2 * chunk)
    columns = pl.ds(first, 2 * chunk)
    products(2 * i + 1, s_b, d_b)
    qt_ref[:, columns] = qs[both, :].T
    weights(2 * i, 0, s_a, d_a)
    products(jnp.minimum(2 * i + 2, chunks - 1), s_a, d_a)
    dot_ref[:, columns] = dos[both, :].T
    weights(2 * i + 1, 1, s_b, d_b)


def far_kernel(
    sizes, start_ref, log1_ref, mean1_ref, qs_ref, dos_ref, qt_ref, dot_ref, *refs,
):
    tokens, groups, heads, slots, width, per, kept = sizes
    pair_refs = refs[:slots]
    k_ref, ds_ref, share_ref, shift_ref = refs[slots : slots + 4]
    part_refs = refs[slots + 4 : 2 * slots + 4]
    wide, v_s, bias, dk, dv, s_a, d_a, s_b, d_b, w_s, *ds_s = refs[2 * slots + 4 :]
    chunk = per * tokens
    chunks = groups // per * heads
    hops = slots // 2
    i = pl.program_id(0)
    first = step_rows(kept, 2 * chunk)
    slope = width**-0.5 * LOG2E
    ctx = lax.axis_index("ctx")
    reached = ctx >= 2
    steps = groups // (2 * per)
    inside = pl.multiple_of(i % steps * 2 * chunk, 2 * chunk)

    def products(c, s, d):
        rows = pl.ds(pl.multiple_of(c * chunk, chunk), chunk)
        h = c * per // groups
        s[...] = lax.dot_general(qs_ref[rows, :], k_ref[h], ACROSS, preferred_element_type=f32)
        d[...] = lax.dot_general(dos_ref[rows, :], v_s[h], ACROSS, preferred_element_type=f32)

    def gradients():
        h = i // steps
        rows = pl.ds(pl.multiple_of(h * groups * tokens, groups * tokens), groups * tokens)
        ds = ds_ref[rows, :] if kept else ds_s[0][...]
        dk[h] = jnp.dot(qt_ref[:, rows], ds, preferred_element_type=f32)
        dv[h] = jnp.dot(dot_ref[:, rows], w_s[...], preferred_element_type=f32)

    def weights(c, half, s, d):
        for g in range(per):
            rows = slice(g * tokens, (g + 1) * tokens)
            out = pl.ds(first + half * chunk + g * tokens, tokens)
            log1 = log1_ref[out, :]
            mean1 = mean1_ref[out, :]
            x = s[rows, :] * slope + bias[...]
            dp = d[rows, :]
            m = jnp.maximum(jnp.max(x, -1, keepdims=True), log1)
            p = jnp.exp2(x - spread(m, x.shape[1]))
            before = jnp.exp2(log1 - m)
            inverse = 1.0 / (jnp.sum(p, -1, keepdims=True) + before)
            mean = (jnp.sum(p * dp, -1, keepdims=True) + before * mean1) * inverse
            w = p * spread(inverse, x.shape[1])
            ds = (w * (dp - spread(mean, x.shape[1]))).astype(bf16)
            here = pl.ds(inside + half * chunk + g * tokens, tokens)
            w_s[here, :] = w.astype(bf16)
            ds_ref[out, :] = ds
            if not kept:
                ds_s[0][here, :] = ds
            share_ref[out, :] = before * inverse
            shift_ref[out, :] = mean1 - mean

    @pl.when(reached & (i == 0))
    def _():
        split_heads(pair_refs, k_ref, v_s, wide, tokens, heads)
        partner = ctx + 1 - 2 * (ctx % 2)
        starts = [(ctx - 2 * d) * tokens for d in range(1, hops + 1)]
        starts += [(partner - 2 * d) * tokens for d in range(1, hops + 1)]
        fill_bias(bias, start_ref, starts, tokens)
        products(0, s_a, d_a)

    @pl.when(reached)
    def _():
        products(2 * i + 1, s_b, d_b)
        weights(2 * i, 0, s_a, d_a)
        products(jnp.minimum(2 * i + 2, chunks - 1), s_a, d_a)
        weights(2 * i + 1, 1, s_b, d_b)

    @pl.when(reached & (i % steps == steps - 1))
    def _():
        gradients()

    @pl.when(reached & (i == pl.num_programs(0) - 1))
    def _():
        join_heads(dk, dv, part_refs, wide, tokens, heads, width**-0.5)

    @pl.when(jnp.logical_not(reached))
    def _():
        these = pl.ds(first, 2 * chunk)
        ds_ref[these, :] = jnp.zeros((2 * chunk, ds_ref.shape[1]), bf16)
        share_ref[these, :] = jnp.ones((2 * chunk, 128), f32)
        shift_ref[these, :] = jnp.zeros((2 * chunk, 128), f32)

    @pl.when(jnp.logical_not(reached) & (i == 0))
    def _():
        k_ref[...] = jnp.zeros_like(k_ref)
        for part in part_refs:
            part[...] = jnp.zeros_like(part)


def tail_kernel(
    sizes, share_ref, shift_ref, k1_ref, k2_ref, qt_ref, dot_ref, w1_ref, u1_ref, ds2_ref,
    dq_ref, own_ref, partner_ref,
    wide, w_a, ds_a, w_b, ds_b, dk, dv,
):
    tokens, groups, heads, width, per, kept = sizes
    chunk = per * tokens
    i = pl.program_id(0)
    scale = width**-0.5
    h = i * 2 * per // groups
    first = step_rows(kept, 2 * chunk)

    @pl.when(i == 0)
    def _():
        dk[...] = jnp.zeros_like(dk)
        dv[...] = jnp.zeros_like(dv)

    def rescaled(half, w_s, ds_s):
        for g in range(per):
            rows = slice(g * tokens, (g + 1) * tokens)
            here = pl.ds(first + half * chunk + g * tokens, tokens)
            w = w1_ref[here, :].astype(f32)
            share = spread(share_ref[here, :], w.shape[1])
            shift = spread(shift_ref[here, :], w.shape[1])
            w_s[rows, :] = (w * share).astype(bf16)
            ds_s[rows, :] = ((u1_ref[here, :].astype(f32) + w * shift) * share).astype(bf16)

    def gradients(half, w_s, ds_s):
        these = pl.ds(first + half * chunk, chunk)
        dk[h] += jnp.dot(qt_ref[:, these], ds_s[...], preferred_element_type=f32)
        dv[h] += jnp.dot(dot_ref[:, these], w_s[...], preferred_element_type=f32)
        dq = jnp.dot(ds_s[...], k1_ref[h], preferred_element_type=f32)
        dq += jnp.dot(ds2_ref[these, :], k2_ref[h], preferred_element_type=f32)
        dq *= scale
        group = (i * 2 + half) * per % groups
        for g in range(per):
            dq_ref[pl.ds((group + g) * heads + h, tokens, stride=groups * heads), :] = dq[
                g * tokens : (g + 1) * tokens
            ]

    rescaled(0, w_a, ds_a)
    rescaled(1, w_b, ds_b)
    gradients(0, w_a, ds_a)
    gradients(1, w_b, ds_b)

    @pl.when(i == pl.num_programs(0) - 1)
    def _():
        join_heads(dk, dv, (own_ref, partner_ref), wide, tokens, heads, scale)


def whole(*shape):
    return pl.BlockSpec(shape, lambda i: (0,) * len(shape))


def stepped(kept, *shape):
    return VMEM if kept else pl.BlockSpec(shape, lambda i: (i, 0))


def across(kept, *shape):
    return VMEM if kept else pl.BlockSpec(shape, lambda i: (0, i))


def params(kept):
    return pltpu.CompilerParams(vmem_limit_bytes=(16 if kept else 60) * 2**20)


def step_rows(kept, rows):
    if not kept:
        return 0
    return pl.multiple_of(pl.program_id(0) * rows, rows)


def prep(q, do, sizes):
    tokens, groups, heads, width, per, kept = sizes
    rows = tokens * groups * heads
    pieces = 4
    return pl.pallas_call(
        functools.partial(prep_kernel, sizes),
        in_specs=[pl.BlockSpec(memory_space=pltpu.HBM)] * 2,
        out_specs=[VMEM] * 2,
        out_shape=[jax.ShapeDtypeStruct((rows, width), bf16)] * 2,
        scratch_shapes=[
            pltpu.VMEM((2 * pieces, rows // pieces, width), f32),
            pltpu.VMEM((pieces, rows // pieces, width), bf16),
            pltpu.VMEM((pieces, rows // pieces, width), bf16),
            pltpu.SemaphoreType.DMA((pieces, 2)),
        ],
        compiler_params=params(kept),
        name="prep",
    )(q, do)


def near(qs, dos, start, own, partner, sizes):
    tokens, groups, heads, width, per, kept = sizes
    chunk = per * tokens
    rows = tokens * groups * heads
    keys = 2 * tokens
    return pl.pallas_call(
        functools.partial(near_kernel, sizes),
        grid=(rows // (2 * chunk),),
        in_specs=[VMEM] * 5,
        out_specs=[
            stepped(kept, 2 * chunk, keys),
            stepped(kept, 2 * chunk, keys),
            whole(heads, keys, width),
            stepped(kept, 2 * chunk, 128),
            stepped(kept, 2 * chunk, 128),
            across(kept, width, 2 * chunk),
            across(kept, width, 2 * chunk),
        ],
        out_shape=[
            jax.ShapeDtypeStruct((rows, keys), bf16),
            jax.ShapeDtypeStruct((rows, keys), bf16),
            jax.ShapeDtypeStruct((heads, keys, width), bf16),
            jax.ShapeDtypeStruct((rows, 128), f32),
            jax.ShapeDtypeStruct((rows, 128), f32),
            jax.ShapeDtypeStruct((width, rows), bf16),
            jax.ShapeDtypeStruct((width, rows), bf16),
        ],
        scratch_shapes=[
            pltpu.VMEM((tokens * heads, width), f32),
            pltpu.VMEM((heads, keys, width), bf16),
            pltpu.VMEM((tokens, keys), f32),
        ]
        + [pltpu.VMEM((chunk, keys), f32)] * 4,
        compiler_params=params(kept),
        cost_estimate=pl.CostEstimate(
            flops=2 * 2 * rows * (keys) * width,
            bytes_accessed=8 * rows * (keys),
            transcendentals=rows * (keys),
        ),
        name="near",
    )(qs, dos, start, own, partner)


def far(start, log1, mean1, qs, dos, qt, dt, pairs, sizes):
    tokens, groups, heads, width, per, kept = sizes
    slots = len(pairs)
    chunk = per * tokens
    rows = tokens * groups * heads
    keys = slots * tokens
    return pl.pallas_call(
        functools.partial(far_kernel, (tokens, groups, heads, slots, width, per, kept)),
        grid=(rows // (2 * chunk),),
        in_specs=[VMEM] + [stepped(kept, 2 * chunk, 128)] * 2 + [VMEM] * (4 + slots),
        out_specs=[
            whole(heads, keys, width),
            stepped(kept, 2 * chunk, keys),
            stepped(kept, 2 * chunk, 128),
            stepped(kept, 2 * chunk, 128),
        ]
        + [whole(2, tokens * heads, width)] * slots,
        out_shape=[
            jax.ShapeDtypeStruct((heads, keys, width), bf16),
            jax.ShapeDtypeStruct((rows, keys), bf16),
            jax.ShapeDtypeStruct((rows, 128), f32),
            jax.ShapeDtypeStruct((rows, 128), f32),
        ]
        + [jax.ShapeDtypeStruct((2, tokens * heads, width), bf16)] * slots,
        scratch_shapes=[
            pltpu.VMEM((tokens * heads, width), f32),
            pltpu.VMEM((heads, keys, width), bf16),
            pltpu.VMEM((tokens, keys), f32),
            pltpu.VMEM((heads, width, keys), f32),
            pltpu.VMEM((heads, width, keys), f32),
        ]
        + [pltpu.VMEM((chunk, keys), f32)] * 4
        + [pltpu.VMEM((groups * tokens, keys), bf16)] * (1 if kept else 2),
        compiler_params=params(kept),
        cost_estimate=pl.CostEstimate(
            flops=2 * 4 * rows * (keys) * width,
            bytes_accessed=8 * rows * (keys),
            transcendentals=rows * (keys),
        ),
        input_output_aliases={1: 2, 2: 3},
        name="far",
    )(start, log1, mean1, qs, dos, qt, dt, *pairs)


def tail(share, shift, k1, k2, qt, dt, w1, u1, ds2, sizes):
    tokens, groups, heads, width, per, kept = sizes
    chunk = per * tokens
    rows = tokens * groups * heads
    near_keys, far_keys = k1.shape[1], k2.shape[1]
    return pl.pallas_call(
        functools.partial(tail_kernel, sizes),
        grid=(rows // (2 * chunk),),
        in_specs=[
            stepped(kept, 2 * chunk, 128),
            stepped(kept, 2 * chunk, 128),
            whole(heads, near_keys, width),
            whole(heads, far_keys, width),
            across(kept, width, 2 * chunk),
            across(kept, width, 2 * chunk),
            stepped(kept, 2 * chunk, near_keys),
            stepped(kept, 2 * chunk, near_keys),
            stepped(kept, 2 * chunk, far_keys),
        ],
        out_specs=[VMEM] * 3,
        out_shape=[
            jax.ShapeDtypeStruct((rows, width), f32),
            jax.ShapeDtypeStruct((2, tokens * heads, width), f32),
            jax.ShapeDtypeStruct((2, tokens * heads, width), bf16),
        ],
        scratch_shapes=[
            pltpu.VMEM((tokens * heads, width), f32),
            *[pltpu.VMEM((chunk, near_keys), bf16)] * 4,
            pltpu.VMEM((heads, width, near_keys), f32),
            pltpu.VMEM((heads, width, near_keys), f32),
        ],
        compiler_params=params(kept),
        cost_estimate=pl.CostEstimate(
            flops=2 * 3 * rows * (near_keys + far_keys) * width,
            bytes_accessed=8 * rows * (near_keys + far_keys),
            transcendentals=rows * (near_keys + far_keys),
        ),
        name="tail",
    )(share, shift, k1, k2, qt, dt, w1, u1, ds2)


def shards(queries, keys, values, output_gradient, band_start):
    tokens, heads, groups, width = queries.shape
    count = lax.axis_size("ctx")
    reach = min(WINDOW // tokens, count - 1)
    hops = min((reach + 1) // 2, count // 2 - 1)
    own = jnp.stack([keys.reshape(tokens * heads, width), values.reshape(tokens * heads, width)], 0)
    same = [moved(own, 2 * d) for d in range(1, hops + 1)]
    partner = swapped(own)
    start = band_start.reshape(1, tokens)
    per = next(n for n in (3, 2, 1) if groups % (2 * n) == 0 and n * hops <= 4)
    kept = hops <= 2
    sizes = (tokens, groups, heads, width, per, kept)

    def flat(a):
        return a.transpose(0, 2, 1, 3).reshape(tokens * groups * heads, width)

    in_hbm = [
        pltpu.with_memory_space_constraint(flat(a), pltpu.HBM) for a in (queries, output_gradient)
    ]
    qs, dos = prep(*in_hbm, sizes)
    w1, u1, k1, log1, mean1, qt, dt = near(qs, dos, start, own, partner, sizes)
    *same, log1 = lax.optimization_barrier((*same, log1))
    other = [swapped(block) for block in same]
    k2, ds2, share, shift, *parts = far(
        start, log1, mean1, qs, dos, qt, dt, same + other, sizes
    )
    arriving = []
    for d in range(hops):
        crossed = swapped(parts[hops + d])
        both = (parts[d].astype(f32) + crossed.astype(f32)).astype(bf16)
        both, share = lax.optimization_barrier((both, share))
        arriving.append(moved(both, -2 * (d + 1)))
    dq, total, crossing = tail(share, shift, k1, k2, qt, dt, w1, u1, ds2, sizes)
    crossing, *arriving = lax.optimization_barrier((crossing, *arriving))
    total = total + swapped(crossing).astype(f32)
    for part in arriving:
        total = total + part.astype(f32)
    return (
        dq.reshape(tokens, groups, heads, width).transpose(0, 2, 1, 3),
        total[0].reshape(tokens, heads, width),
        total[1].reshape(tokens, heads, width),
    )


def solution(mesh):
    rows = P(("rep", "ctx"), "kv", None, None)
    keys = P(("rep", "ctx"), "kv", None)
    return jax.shard_map(
        shards,
        mesh=mesh,
        in_specs=(rows, keys, keys, rows, P(("rep", "ctx"))),
        out_specs=(rows, keys, keys),
        check_vma=False,
    )
```

time: 53.4 us -> 43.4 us (0.81)
  Pallas kernels: 36 us -> 21.9 us
  waiting for transfers between devices: 4.01 us -> 11.8 us
  local copies, waits for them, and re-layouts: 4.31 us -> 0.83 us
    pallas_call x1, Pallas kernels: 14.1 us -> 1.08 us  [far(): pl.pallas_call(functools.partial(far_kernel, (tokens, groups, heads, slot...]
    ppermute x2, waiting for transfers between devices: 0.01 us -> 7.52 us  [moved(): return lax.ppermute(block, 'ctx', route)]
    unnamed x6 -> x2, local copies, waits for them, and re-layouts: 3.49 us -> 0.01 us
    pallas_call x1, Pallas kernels: 11.9 us -> 9.26 us  [tail(): pl.pallas_call(functools.partial(tail_kernel, sizes), grid=(rows // (2 *...]
    pallas_call x0 -> x1, Pallas kernels: none -> 2.46 us  [prep(): pl.pallas_call(functools.partial(prep_kernel, sizes), in_specs=[pl.BlockS...]
    pallas_call x1, Pallas kernels: 9.98 us -> 9.12 us  [near(): pl.pallas_call(functools.partial(near_kernel, sizes), grid=(rows // (2 *...]
  transfers between devices with their start and end apart: 6 -> 6, of which waited for: 3 -> 4; matrix products, arithmetic and copies ran while one was open for 0% -> 0% of each run, Pallas kernels for 41% -> 48%
where the time goes in v3:
time: 43.4 us; the launch traced here: 43.1 us
  Pallas kernels  21.9 us (50%)
  waiting for transfers between devices  11.8 us (27%)
  starting transfers between devices  6.72 us (15%)
  other arithmetic  1.15 us (3%)
  local copies, waits for them, and re-layouts  0.83 us (2%)
  between operations  0.72 us (2%)
    pallas_call x1, Pallas kernels, tail(): pl.pallas_call(functools.partial(tail_kernel, sizes), grid=(rows // (2 *...  9.26 us
    pallas_call x1, Pallas kernels, near(): pl.pallas_call(functools.partial(near_kernel, sizes), grid=(rows // (2 *...  9.12 us
    ppermute x2, waiting for transfers between devices, moved(): return lax.ppermute(block, 'ctx', route)  7.52 us
    ppermute x2, starting transfers between devices, moved(): return lax.ppermute(block, 'ctx', route)  5.71 us
    ppermute x4, waiting for transfers between devices, swapped(): lax.ppermute(block, 'ctx', [(i, i ^ 1) for i in range(lax.axis_size('ctx'...  4.24 us
    pallas_call x1, Pallas kernels, prep(): pl.pallas_call(functools.partial(prep_kernel, sizes), in_specs=[pl.BlockS...  2.46 us
    pallas_call x1, Pallas kernels, far(): pl.pallas_call(functools.partial(far_kernel, (tokens, groups, heads, slot...  1.08 us
    ppermute x4, starting transfers between devices, swapped(): lax.ppermute(block, 'ctx', [(i, i ^ 1) for i in range(lax.axis_size('ctx'...  1.01 us
  transfers between devices with their start and end apart: 6, of which 4 were waited for; matrix products, arithmetic and copies ran while one was open for 0% of the time, Pallas kernels for 48%

profile of v3, /device:TPU:0, one launch (start us, length us, event | category | flops | bytes accessed | tf_op | source)
XLA Modules:
  0.0 43.1 jit_solution(14742088037284498114)
XLA Ops:
  0.6 0.0 copy-start
  0.6 1.0 %pad_maximum_fusion.own_ref = bf16[2,512,128]{2,1,0:T(8,128)(2,1)S(1)} fusion(bf16[1,512,128]{2,1,0:T(8,128)(2,1)} %bitcast.20, bf16[1,512,128]{2,1,0:T(8,128)(2,1)} %bitcast.21), kind=kLoop, calls=%fused_computation.2 | loop fusion | flops 131072 | bytes 524288 | tf_op jit(solution)/shard_map/stack | solution.py:461
  1.6 0.5 %collective-permute-start.1 = (bf16[2,512,128]{2,1,0:T(8,128)(2,1)S(1)}, bf16[2,512,128]{2,1,0:T(8,128)(2,1)S(1)}, u32[]{:S(2)}, u32[]{:S(2)}) collective-permute-start(bf16[2,512,128]{2,1,0:T(8,128)(2,1)S(1)} %pad_maximum_fusion.own_ref), channel_id=1, source_target_pairs={{0,8},{8,0},{16,24},{24,16},{1,9},{9,1},{17,25},{25,17},{2,10},{10... | collective-permute-start | bytes 786440 | tf_op jit(solution)/shard_map/ppermute | solution.py:26
  2.2 4.4 %collective-permute-start = (bf16[2,512,128]{2,1,0:T(8,128)(2,1)S(1)}, bf16[2,512,128]{2,1,0:T(8,128)(2,1)S(1)}, u32[]{:S(2)}, u32[]{:S(2)}) collective-permute-start(bf16[2,512,128]{2,1,0:T(8,128)(2,1)S(1)} %pad_maximum_fusion.own_ref), channel_id=1, source_target_pairs={{0,16},{8,24},{1,17},{9,25},{2,18},{10,26},{3,19},{11,27},{4,20},{... | collective-permute-start | bytes 786440 | tf_op jit(solution)/shard_map/ppermute | solution.py:22
  6.6 2.5 %prep.1 = (bf16[6144,128]{1,0:T(8,128)(2,1)S(1)}, bf16[6144,128]{1,0:T(8,128)(2,1)S(1)}) custom-call(bf16[6144,128]{1,0:T(8,128)(2,1)} %bitcast.16, bf16[6144,128]{1,0:T(8,128)(2,1)} %bitcast.17), custom_call_target="tpu_custom_call" | custom-call | tf_op jit(solution)/shard_map/prep/pallas_call | solution.py:312
  9.1 0.0 collective-permute-done.1.partner_ref
  9.1 0.0 copy-done
  9.1 9.1 %near.1 = (bf16[6144,512]{1,0:T(8,128)(2,1)S(1)}, bf16[6144,512]{1,0:T(8,128)(2,1)S(1)}, bf16[2,512,128]{2,1,0:T(8,128)(2,1)S(1)}, f32[6144,128]{1,0:T(8,128)S(1...) custom-call(bf16[6144,128]{1,0:T(8,128)(2,1)S(1)} %get-tuple-element.27.qs.qs_ref, ...), custom_call_target="tpu_custom_call" | custom-call | flops 1610612736 | bytes 25165824 | tf_op jit(solution)/shard_map/near/pallas_call | solution.py:333
  18.2 0.0 collective-permute-done.refs_0_
  18.2 0.2 collective-permute-start.2
  18.5 1.4 %collective-permute-done.2.refs_1_ = bf16[2,512,128]{2,1,0:T(8,128)(2,1)S(1)} collective-permute-done((bf16[2,512,128]{2,1,0:T(8,128)(2,1)S(1)}, bf16[2,512,128]{2,1,0:T(8,128)(2,1)S(1)}, u32[]{:S(2)}, u32[]{:S(2)}) %collective-permute-start.2) | collective-permute-done | bytes 262176 | tf_op jit(solution)/shard_map/ppermute | solution.py:26
  19.8 1.1 %far.1 = (bf16[2,512,128]{2,1,0:T(8,128)(2,1)S(1)}, bf16[6144,512]{1,0:T(8,128)(2,1)S(1)}, f32[6144,128]{1,0:T(8,128)S(1)}, f32[6144,128]{1,0:T(8,128)S(1)}, bf1...) custom-call(s32[1,256]{1,0:T(1,128)S(1)} %bitcast.15, ...), custom_call_target="tpu_custom_call", output_to_operand_aliasing={{2}: (1, {}), {3}: (2, {})} | custom-call | flops 3221225472 | bytes 25165824 | tf_op jit(solution)/shard_map/far/pallas_call | solution.py:377
  20.9 0.2 collective-permute-start.3
  21.1 1.4 %collective-permute-done.3 = bf16[2,512,128]{2,1,0:T(8,128)(2,1)S(1)} collective-permute-done((bf16[2,512,128]{2,1,0:T(8,128)(2,1)S(1)}, bf16[2,512,128]{2,1,0:T(8,128)(2,1)S(1)}, u32[]{:S(2)}, u32[]{:S(2)}) %collective-permute-start.3) | collective-permute-done | bytes 262176 | tf_op jit(solution)/shard_map/ppermute | solution.py:26
  22.5 0.1 add_convert_fusion
  22.6 1.3 %collective-permute-start.4 = (bf16[2,512,128]{2,1,0:T(8,128)(2,1)S(1)}, bf16[2,512,128]{2,1,0:T(8,128)(2,1)S(1)}, u32[]{:S(2)}, u32[]{:S(2)}) collective-permute-start(bf16[2,512,128]{2,1,0:T(8,128)(2,1)S(1)} %add_convert_fusion), channel_id=1, source_target_pairs={{16,0},{24,8},{17,1},{25,9},{18,2},{26,10},{19,3},{27,11},{20,4},{... | collective-permute-start | bytes 786440 | tf_op jit(solution)/shard_map/ppermute | solution.py:22
  23.9 9.3 %tail.1 = (f32[6144,128]{1,0:T(8,128)}, f32[2,512,128]{2,1,0:T(8,128)S(1)}, bf16[2,512,128]{2,1,0:T(8,128)(2,1)S(1)}) custom-call(f32[6144,128]{1,0:T(8,128)S(1)} %get-tuple-element.38.share_ref, f32[6144,128]{1,0:T(8,128)S(1)} %get-tuple-element.39.shift_ref, bf16[2,512,128]{2,1,0:T(8,128)(2,1)S(1)} %get-tuple-element.40.k1_ref, ...), custom_call_target="tpu_custom_call" | custom-call | flops 4831838208 | bytes 50331648 | tf_op jit(solution)/shard_map/tail/pallas_call | solution.py:420
  33.1 7.5 %collective-permute-done.4 = bf16[2,512,128]{2,1,0:T(8,128)(2,1)S(1)} collective-permute-done((bf16[2,512,128]{2,1,0:T(8,128)(2,1)S(1)}, bf16[2,512,128]{2,1,0:T(8,128)(2,1)S(1)}, u32[]{:S(2)}, u32[]{:S(2)}) %collective-permute-start.4) | collective-permute-done | bytes 262176 | tf_op jit(solution)/shard_map/ppermute | solution.py:22
  40.7 0.0 collective-permute-start.5
  40.7 1.5 %collective-permute-done.5 = bf16[2,512,128]{2,1,0:T(8,128)(2,1)S(1)} collective-permute-done((bf16[2,512,128]{2,1,0:T(8,128)(2,1)S(1)}, bf16[2,512,128]{2,1,0:T(8,128)(2,1)S(1)}, u32[]{:S(2)}, u32[]{:S(2)}) %collective-permute-start.5) | collective-permute-done | bytes 262176 | tf_op jit(solution)/shard_map/ppermute | solution.py:26
  42.2 0.1 convert_add_fusion
  42.3 0.8 %fusion = (f32[1,512,128]{2,1,0:T(8,128)}, f32[1,512,128]{2,1,0:T(8,128)}) fusion(f32[2,512,128]{2,1,0:T(8,128)S(1)} %convert_add_fusion), kind=kLoop, calls=%fused_computation.3 | loop fusion | bytes 1048576 | tf_op jit(solution)/shard_map/slice | solution.py:496
Async XLA Ops:
  0.6 8.4 %copy-start = (s32[256]{0:T(256)S(1)}, s32[256]{0:T(256)}, u32[]{:S(2)}) copy-start(s32[256]{0:T(256)} %param.9) | copy-start | bytes 3076
  1.6 7.4 %collective-permute-start.1 = (bf16[2,512,128]{2,1,0:T(8,128)(2,1)S(1)}, bf16[2,512,128]{2,1,0:T(8,128)(2,1)S(1)}, u32[]{:S(2)}, u32[]{:S(2)}) collective-permute-start(bf16[2,512,128]{2,1,0:T(8,128)(2,1)S(1)} %pad_maximum_fusion.own_ref), channel_id=1, source_target_pairs={{0,8},{8,0},{16,24},{24,16},{1,9},{9,1},{17,25},{25,17},{2,10},{10... | collective-permute-start | bytes 786440 | tf_op jit(solution)/shard_map/ppermute | solution.py:26
  2.2 16.0 %collective-permute-start = (bf16[2,512,128]{2,1,0:T(8,128)(2,1)S(1)}, bf16[2,512,128]{2,1,0:T(8,128)(2,1)S(1)}, u32[]{:S(2)}, u32[]{:S(2)}) collective-permute-start(bf16[2,512,128]{2,1,0:T(8,128)(2,1)S(1)} %pad_maximum_fusion.own_ref), channel_id=1, source_target_pairs={{0,16},{8,24},{1,17},{9,25},{2,18},{10,26},{3,19},{11,27},{4,20},{... | collective-permute-start | bytes 786440 | tf_op jit(solution)/shard_map/ppermute | solution.py:22
  18.2 1.6 %collective-permute-start.2 = (bf16[2,512,128]{2,1,0:T(8,128)(2,1)S(1)}, bf16[2,512,128]{2,1,0:T(8,128)(2,1)S(1)}, u32[]{:S(2)}, u32[]{:S(2)}) collective-permute-start(bf16[2,512,128]{2,1,0:T(8,128)(2,1)S(1)} %collective-permute-done.refs_0_), channel_id=1, source_target_pairs={{0,8},{8,0},{16,24},{24,16},{1,9},{9,1},{17,25},{25,17},{2,10},{10... | collective-permute-start | bytes 786440 | tf_op jit(solution)/shard_map/ppermute | solution.py:26
  20.9 1.6 %collective-permute-start.3 = (bf16[2,512,128]{2,1,0:T(8,128)(2,1)S(1)}, bf16[2,512,128]{2,1,0:T(8,128)(2,1)S(1)}, u32[]{:S(2)}, u32[]{:S(2)}) collective-permute-start(bf16[2,512,128]{2,1,0:T(8,128)(2,1)S(1)} %get-tuple-element.36), channel_id=1, source_target_pairs={{0,8},{8,0},{16,24},{24,16},{1,9},{9,1},{17,25},{25,17},{2,10},{10... | collective-permute-start | bytes 786440 | tf_op jit(solution)/shard_map/ppermute | solution.py:26
  22.6 18.1 %collective-permute-start.4 = (bf16[2,512,128]{2,1,0:T(8,128)(2,1)S(1)}, bf16[2,512,128]{2,1,0:T(8,128)(2,1)S(1)}, u32[]{:S(2)}, u32[]{:S(2)}) collective-permute-start(bf16[2,512,128]{2,1,0:T(8,128)(2,1)S(1)} %add_convert_fusion), channel_id=1, source_target_pairs={{16,0},{24,8},{17,1},{25,9},{18,2},{26,10},{19,3},{27,11},{20,4},{... | collective-permute-start | bytes 786440 | tf_op jit(solution)/shard_map/ppermute | solution.py:22
  40.7 1.5 %collective-permute-start.5 = (bf16[2,512,128]{2,1,0:T(8,128)(2,1)S(1)}, bf16[2,512,128]{2,1,0:T(8,128)(2,1)S(1)}, u32[]{:S(2)}, u32[]{:S(2)}) collective-permute-start(bf16[2,512,128]{2,1,0:T(8,128)(2,1)S(1)} %get-tuple-element.49), channel_id=1, source_target_pairs={{0,8},{8,0},{16,24},{24,16},{1,9},{9,1},{17,25},{25,17},{2,10},{10... | collective-permute-start | bytes 786440 | tf_op jit(solution)/shard_map/ppermute | solution.py:26

commit v4 on v3

v4 whole, which is shorter than its diff:
```python
import functools

import jax
import jax.numpy as jnp
from jax import lax
from jax.experimental import pallas as pl
from jax.experimental.pallas import tpu as pltpu
from jax.sharding import PartitionSpec as P

WINDOW = 2048
LOG2E = 1.4426950408889634
MASKED = -1e30
f32 = jnp.float32
bf16 = jnp.bfloat16
ACROSS = (((1,), (1,)), ((), ()))
VMEM = pl.BlockSpec(memory_space=pltpu.VMEM)


def moved(block, distance):
    devices = range(lax.axis_size("ctx"))
    route = [(i - distance, i) for i in devices if i - distance in devices]
    return lax.ppermute(block, "ctx", route)


def swapped(block):
    return lax.ppermute(block, "ctx", [(i, i ^ 1) for i in range(lax.axis_size("ctx"))])


def split_heads(pair_refs, k_s, v_s, tokens, heads):
    for slot, pair in enumerate(pair_refs):
        for h in range(heads):
            rows = slice(h * tokens, (h + 1) * tokens)
            k_s[h, slot * tokens : (slot + 1) * tokens, :] = pair[0, rows, :]
            v_s[h, slot * tokens : (slot + 1) * tokens, :] = pair[1, rows, :]


def join_heads(dk, dv, part_refs, tokens, heads, scale):
    for source, grad in ((0, dk), (1, dv)):
        for slot, part in enumerate(part_refs):
            for h in range(heads):
                block = grad[h, :, slot * tokens : (slot + 1) * tokens].T
                if source == 0:
                    block *= scale
                part[source, h * tokens : (h + 1) * tokens, :] = block.astype(part.dtype)


def pack_kernel(heads, k_ref, v_ref, pair_ref, narrow, wide, arrived):
    tokens = k_ref.shape[0] // heads
    loads = [
        pltpu.make_async_copy(ref, narrow.at[source], arrived.at[source])
        for source, ref in ((0, k_ref), (1, v_ref))
    ]
    for load in loads:
        load.start()
    for source in range(2):
        loads[source].wait()
        wide[source] = narrow[source].astype(f32)
        for h in range(heads):
            pair_ref[source, h * tokens : (h + 1) * tokens, :] = wide[
                source, pl.ds(h, tokens, stride=heads), :
            ].astype(bf16)


def finish_kernel(heads, own_ref, crossed_k_ref, crossed_v_ref, *refs):
    tokens = own_ref.shape[1] // heads
    for source, crossed in ((0, crossed_k_ref), (1, crossed_v_ref)):
        for h in range(heads):
            rows = slice(h * tokens, (h + 1) * tokens)
            total = own_ref[source, rows, :] + crossed[rows, :].astype(f32)
            for arrived in refs[:-2]:
                total += arrived[source, rows, :].astype(f32)
            refs[source - 2][pl.ds(h, tokens, stride=heads), :] = total


def fill_bias(bias, start_ref, first_keys, tokens):
    down = lax.broadcasted_iota(jnp.int32, (tokens, tokens), 0)
    along = lax.broadcasted_iota(jnp.int32, (tokens, tokens), 1)
    start = jnp.sum(
        jnp.where(down == along, start_ref[...].astype(f32), 0.0), -1, keepdims=True
    ).astype(jnp.int32)
    row = lax.axis_index("ctx") * tokens + lax.broadcasted_iota(jnp.int32, (tokens, 1), 0)
    for slot, first in enumerate(first_keys):
        key = first + lax.broadcasted_iota(jnp.int32, (1, tokens), 1)
        bias[:, slot * tokens : (slot + 1) * tokens] = jnp.where(
            (key <= row) & (key >= start), 0.0, MASKED
        )


def spread(lanes, width):
    return jnp.concatenate([lanes] * (width // lanes.shape[1]), 1)


def prep_kernel(sizes, q_ref, do_ref, qs_ref, dos_ref, wide, q_in, do_in, arrived):
    tokens, groups, heads, width, here, kept = sizes
    pieces = q_in.shape[0]
    size = tokens // pieces * groups * heads
    blocks = tokens // here
    loads = []
    for n in range(pieces):
        for k, (source, target) in enumerate(((q_ref, q_in), (do_ref, do_in))):
            load = pltpu.make_async_copy(
                source.at[pl.ds(n * size, size), :], target.at[n], arrived.at[n, k]
            )
            load.start()
            loads.append(load)
    for n in range(pieces):
        for k, (source, split) in enumerate(((q_in, qs_ref), (do_in, dos_ref))):
            loads[2 * n + k].wait()
            wide[2 * n + k] = source[n].astype(f32)
            for h in range(heads):
                for b in range(blocks // pieces):
                    for g in range(groups):
                        at = ((h * blocks + n * (blocks // pieces) + b) * groups + g) * here
                        begin = (b * here * groups + g) * heads + h
                        split[at : at + here, :] = wide[
                            2 * n + k, pl.ds(begin, here, stride=groups * heads), :
                        ].astype(bf16)


def near_kernel(
    sizes, qs, dos, start_ref, own_ref, partner_ref,
    w_ref, u_ref, k_ref, log_ref, mean_ref, qt_ref, dot_ref,
    v_s, bias, s_a, d_a, s_b, d_b,
):
    tokens, groups, heads, width, here, kept = sizes
    chunk = here * groups
    blocks = tokens // here
    chunks = blocks * heads
    i = pl.program_id(0)
    first = step_rows(kept, 2 * chunk)
    slope = width**-0.5 * LOG2E
    lower, every = tokens + tokens // 2, 2 * tokens
    early = i % (blocks // 2) < blocks // 4

    def products(c, s, d, keys):
        rows = pl.ds(pl.multiple_of(c * chunk, chunk), chunk)
        h = c // blocks
        s[:, :keys] = lax.dot_general(qs[rows, :], k_ref[h, :keys], ACROSS, preferred_element_type=f32)
        d[:, :keys] = lax.dot_general(dos[rows, :], v_s[h, :keys], ACROSS, preferred_element_type=f32)

    def weights(c, half, s, d, keys):
        size = chunk // 3
        band = bias[pl.ds(pl.multiple_of(c % blocks * here, here), here), :keys]
        band = jnp.concatenate([band] * (size // here), 0)
        for row in range(0, chunk, size):
            rows = slice(row, row + size)
            out = pl.ds(first + half * chunk + row, size)
            x = s[rows, :keys] * slope + band
            dp = d[rows, :keys]
            m = jnp.max(x, -1, keepdims=True)
            p = jnp.exp2(x - m)
            total = jnp.sum(p, -1, keepdims=True)
            inverse = 1.0 / total
            dot = jnp.sum(p * dp, -1, keepdims=True) * inverse
            w = p * inverse
            w_ref[out, :keys] = w.astype(bf16)
            u_ref[out, :keys] = (w * (dp - dot)).astype(bf16)
            log_ref[out, :] = jnp.broadcast_to(m + jnp.log2(total), (size, 128))
            mean_ref[out, :] = jnp.broadcast_to(dot, (size, 128))

    @pl.when(i == 0)
    def _():
        split_heads((partner_ref, own_ref), k_ref, v_s, tokens, heads)
        ctx = lax.axis_index("ctx")
        fill_bias(bias, start_ref, ((ctx + 1 - 2 * (ctx % 2)) * tokens, ctx * tokens), tokens)
        products(0, s_a, d_a, lower)

    both = pl.ds(pl.multiple_of(i * 2 * chunk, 2 * chunk), 2 * chunk)
    columns = pl.ds(first, 2 * chunk)

    def step(keys, next_keys):
        products(2 * i + 1, s_b, d_b, keys)
        qt_ref[:, columns] = qs[both, :].T
        weights(2 * i, 0, s_a, d_a, keys)
        products(jnp.minimum(2 * i + 2, chunks - 1), s_a, d_a, next_keys)
        dot_ref[:, columns] = dos[both, :].T
        weights(2 * i + 1, 1, s_b, d_b, keys)

    @pl.when(early)
    def _():
        step(lower, every)

    @pl.when(jnp.logical_not(early))
    def _():
        step(every, lower if blocks == 4 else every)


def far_kernel(
    sizes, start_ref, log1_ref, mean1_ref, qs_ref, dos_ref, qt_ref, dot_ref, *refs,
):
    tokens, groups, heads, slots, width, here, kept = sizes
    pair_refs = refs[:slots]
    k_ref, ds_ref, share_ref, shift_ref = refs[slots : slots + 4]
    part_refs = refs[slots + 4 : 2 * slots + 4]
    v_s, bias, dk, dv, s_a, d_a, s_b, d_b, w_s = refs[2 * slots + 4 :]
    chunk = here * groups
    blocks = tokens // here
    chunks = blocks * heads
    hops = slots // 2
    i = pl.program_id(0)
    first = step_rows(kept, 2 * chunk)
    slope = width**-0.5 * LOG2E
    ctx = lax.axis_index("ctx")
    reached = ctx >= 2
    steps = blocks // 2
    inside = pl.multiple_of(i % steps * 2 * chunk, 2 * chunk) if kept else 0

    def products(c, s, d):
        rows = pl.ds(pl.multiple_of(c * chunk, chunk), chunk)
        h = c // blocks
        s[...] = lax.dot_general(qs_ref[rows, :], k_ref[h], ACROSS, preferred_element_type=f32)
        d[...] = lax.dot_general(dos_ref[rows, :], v_s[h], ACROSS, preferred_element_type=f32)

    def gradients(count):
        h = i // steps
        rows = pl.ds(pl.multiple_of((i - count + 1) * 2 * chunk, 2 * chunk), count * 2 * chunk)
        ds = ds_ref[rows, :] if kept else ds_ref[...]
        dk_part = jnp.dot(qt_ref[:, rows], ds, preferred_element_type=f32)
        dv_part = jnp.dot(dot_ref[:, rows], w_s[...], preferred_element_type=f32)
        if kept:
            dk[h] = dk_part
            dv[h] = dv_part
        else:
            dk[h] += dk_part
            dv[h] += dv_part

    def weights(c, half, s, d):
        size = chunk // 3
        band = bias[pl.ds(pl.multiple_of(c % blocks * here, here), here), :]
        band = jnp.concatenate([band] * (size // here), 0)
        for row in range(0, chunk, size):
            rows = slice(row, row + size)
            out = pl.ds(first + half * chunk + row, size)
            log1 = log1_ref[out, :]
            mean1 = mean1_ref[out, :]
            x = s[rows, :] * slope + band
            dp = d[rows, :]
            m = jnp.maximum(jnp.max(x, -1, keepdims=True), log1)
            p = jnp.exp2(x - spread(m, x.shape[1]))
            before = jnp.exp2(log1 - m)
            inverse = 1.0 / (jnp.sum(p, -1, keepdims=True) + before)
            mean = (jnp.sum(p * dp, -1, keepdims=True) + before * mean1) * inverse
            w = p * spread(inverse, x.shape[1])
            ds = (w * (dp - spread(mean, x.shape[1]))).astype(bf16)
            there = pl.ds(inside + half * chunk + row, size)
            w_s[there, :] = w.astype(bf16)
            ds_ref[out, :] = ds
            share_ref[out, :] = before * inverse
            shift_ref[out, :] = mean1 - mean

    @pl.when(reached & (i == 0))
    def _():
        split_heads(pair_refs, k_ref, v_s, tokens, heads)
        partner = ctx + 1 - 2 * (ctx % 2)
        starts = [(ctx - 2 * d) * tokens for d in range(1, hops + 1)]
        starts += [(partner - 2 * d) * tokens for d in range(1, hops + 1)]
        fill_bias(bias, start_ref, starts, tokens)
        if not kept:
            dk[...] = jnp.zeros_like(dk)
            dv[...] = jnp.zeros_like(dv)
        products(0, s_a, d_a)

    @pl.when(reached)
    def _():
        products(2 * i + 1, s_b, d_b)
        weights(2 * i, 0, s_a, d_a)
        products(jnp.minimum(2 * i + 2, chunks - 1), s_a, d_a)
        weights(2 * i + 1, 1, s_b, d_b)

    if kept:
        pl.when(reached & (i % steps == steps - 1))(lambda: gradients(steps))
    else:
        pl.when(reached)(lambda: gradients(1))

    @pl.when(reached & (i == pl.num_programs(0) - 1))
    def _():
        join_heads(dk, dv, part_refs, tokens, heads, width**-0.5)

    @pl.when(jnp.logical_not(reached))
    def _():
        these = pl.ds(first, 2 * chunk)
        ds_ref[these, :] = jnp.zeros((2 * chunk, ds_ref.shape[1]), bf16)
        share_ref[these, :] = jnp.ones((2 * chunk, 128), f32)
        shift_ref[these, :] = jnp.zeros((2 * chunk, 128), f32)

    @pl.when(jnp.logical_not(reached) & (i == 0))
    def _():
        k_ref[...] = jnp.zeros_like(k_ref)
        for part in part_refs:
            part[...] = jnp.zeros_like(part)


def tail_kernel(
    sizes, k1_ref, k2_ref, share_ref, shift_ref, w1_ref, u1_ref, ds2_ref, *refs,
):
    tokens, groups, heads, width, here, kept = sizes
    qt_refs, dot_refs = refs[:heads], refs[heads : 2 * heads]
    dq_ref, own_ref, partner_ref, dk, dv = refs[2 * heads : 2 * heads + 5]
    scratch = refs[2 * heads + 5 :]
    chunk = here * groups
    i = pl.program_id(0)
    scale = width**-0.5
    first = step_rows(kept, chunk)

    @pl.when(i == 0)
    def _():
        dk[...] = jnp.zeros_like(dk)
        dv[...] = jnp.zeros_like(dv)

    def rescaled(h, w_s, ds_s, keys):
        size = 64 if chunk % 64 == 0 else chunk
        for row in range(0, chunk, size):
            rows = pl.ds(first + row, size)
            w = w1_ref[h, rows, :keys].astype(f32)
            share = spread(share_ref[h, rows, :], w.shape[1])
            shift = spread(shift_ref[h, rows, :], w.shape[1])
            w_s[row : row + size, :keys] = (w * share).astype(bf16)
            ds_s[row : row + size, :keys] = (
                (u1_ref[h, rows, :keys].astype(f32) + w * shift) * share
            ).astype(bf16)

    def gradients(h, w_s, ds_s, keys):
        columns = pl.ds((h * tokens * groups if kept else 0) + first, chunk)
        ds = ds_s[:, :keys]
        dk[h, :, :keys] += jnp.dot(qt_refs[h][:, columns], ds, preferred_element_type=f32)
        dv[h, :, :keys] += jnp.dot(
            dot_refs[h][:, columns], w_s[:, :keys], preferred_element_type=f32
        )
        dq = jnp.dot(ds, k1_ref[h, :keys], preferred_element_type=f32)
        dq += jnp.dot(ds2_ref[h, pl.ds(first, chunk), :], k2_ref[h], preferred_element_type=f32)
        dq *= scale
        for g in range(groups):
            dq_ref[pl.ds(g * heads + h, here, stride=groups * heads), :] = dq[
                g * here : (g + 1) * here
            ]

    def step(keys):
        for h in range(heads):
            rescaled(h, scratch[2 * h], scratch[2 * h + 1], keys)
        for h in range(heads):
            gradients(h, scratch[2 * h], scratch[2 * h + 1], keys)

    half = pl.num_programs(0) // 2
    pl.when(i < half)(lambda: step(tokens + tokens // 2))
    pl.when(i >= half)(lambda: step(2 * tokens))

    @pl.when(i == pl.num_programs(0) - 1)
    def _():
        join_heads(dk, dv, (partner_ref, own_ref), tokens, heads, scale)


def pack(keys, values, heads):
    return pl.pallas_call(
        functools.partial(pack_kernel, heads),
        in_specs=[pl.BlockSpec(memory_space=pltpu.HBM)] * 2,
        out_specs=VMEM,
        out_shape=jax.ShapeDtypeStruct((2, *keys.shape), bf16),
        scratch_shapes=[
            pltpu.VMEM((2, *keys.shape), bf16),
            pltpu.VMEM((2, *keys.shape), f32),
            pltpu.SemaphoreType.DMA((2,)),
        ],
        compiler_params=params(True, 4),
        name="pack",
    )(keys, values)


def finish(own, crossed, arrived, heads):
    return pl.pallas_call(
        functools.partial(finish_kernel, heads),
        in_specs=[VMEM] * (3 + len(arrived)),
        out_specs=[VMEM] * 2,
        out_shape=[jax.ShapeDtypeStruct(own.shape[1:], f32)] * 2,
        compiler_params=params(True, 8),
        name="finish",
    )(own, *crossed, *arrived)


def whole(*shape):
    return pl.BlockSpec(shape, lambda i: (0,) * len(shape))


def stepped(kept, *shape):
    return VMEM if kept else pl.BlockSpec(shape, lambda i: (i, 0))


def across(kept, *shape):
    return VMEM if kept else pl.BlockSpec(shape, lambda i: (0, i))


def params(kept, megabytes=16):
    return pltpu.CompilerParams(vmem_limit_bytes=(megabytes if kept else 60) * 2**20)


def step_rows(kept, rows):
    if not kept:
        return 0
    return pl.multiple_of(pl.program_id(0) * rows, rows)


def prep(q, do, sizes):
    tokens, groups, heads, width, here, kept = sizes
    rows = tokens * groups * heads
    pieces = 4
    return pl.pallas_call(
        functools.partial(prep_kernel, sizes),
        in_specs=[pl.BlockSpec(memory_space=pltpu.HBM)] * 2,
        out_specs=[VMEM] * 2,
        out_shape=[jax.ShapeDtypeStruct((rows, width), bf16)] * 2,
        scratch_shapes=[
            pltpu.VMEM((2 * pieces, rows // pieces, width), f32),
            pltpu.VMEM((pieces, rows // pieces, width), bf16),
            pltpu.VMEM((pieces, rows // pieces, width), bf16),
            pltpu.SemaphoreType.DMA((pieces, 2)),
        ],
        compiler_params=params(kept),
        name="prep",
    )(q, do)


def near(qs, dos, start, own, partner, sizes):
    tokens, groups, heads, width, here, kept = sizes
    chunk = here * groups
    rows = tokens * groups * heads
    keys = 2 * tokens
    return pl.pallas_call(
        functools.partial(near_kernel, sizes),
        grid=(rows // (2 * chunk),),
        in_specs=[VMEM] * 5,
        out_specs=[
            stepped(kept, 2 * chunk, keys),
            stepped(kept, 2 * chunk, keys),
            whole(heads, keys, width),
            stepped(kept, 2 * chunk, 128),
            stepped(kept, 2 * chunk, 128),
            across(kept, width, 2 * chunk),
            across(kept, width, 2 * chunk),
        ],
        out_shape=[
            jax.ShapeDtypeStruct((rows, keys), bf16),
            jax.ShapeDtypeStruct((rows, keys), bf16),
            jax.ShapeDtypeStruct((heads, keys, width), bf16),
            jax.ShapeDtypeStruct((rows, 128), f32),
            jax.ShapeDtypeStruct((rows, 128), f32),
            jax.ShapeDtypeStruct((width, rows), bf16),
            jax.ShapeDtypeStruct((width, rows), bf16),
        ],
        scratch_shapes=[
            pltpu.VMEM((heads, keys, width), bf16),
            pltpu.VMEM((tokens, keys), f32),
        ]
        + [pltpu.VMEM((chunk, keys), f32)] * 4,
        compiler_params=params(kept),
        cost_estimate=pl.CostEstimate(
            flops=2 * 2 * rows * (keys) * width,
            bytes_accessed=8 * rows * (keys),
            transcendentals=rows * (keys),
        ),
        name="near",
    )(qs, dos, start, own, partner)


def far(start, log1, mean1, qs, dos, qt, dt, pairs, sizes):
    tokens, groups, heads, width, here, kept = sizes
    slots = len(pairs)
    chunk = here * groups
    rows = tokens * groups * heads
    keys = slots * tokens
    return pl.pallas_call(
        functools.partial(far_kernel, (tokens, groups, heads, slots, width, here, kept)),
        grid=(rows // (2 * chunk),),
        in_specs=[VMEM] + [stepped(kept, 2 * chunk, 128)] * 2 + [VMEM] * (4 + slots),
        out_specs=[
            whole(heads, keys, width),
            stepped(kept, 2 * chunk, keys),
            stepped(kept, 2 * chunk, 128),
            stepped(kept, 2 * chunk, 128),
        ]
        + [whole(2, tokens * heads, width)] * slots,
        out_shape=[
            jax.ShapeDtypeStruct((heads, keys, width), bf16),
            jax.ShapeDtypeStruct((rows, keys), bf16),
            jax.ShapeDtypeStruct((rows, 128), f32),
            jax.ShapeDtypeStruct((rows, 128), f32),
        ]
        + [jax.ShapeDtypeStruct((2, tokens * heads, width), bf16)] * slots,
        scratch_shapes=[
            pltpu.VMEM((heads, keys, width), bf16),
            pltpu.VMEM((tokens, keys), f32),
            pltpu.VMEM((heads, width, keys), f32),
            pltpu.VMEM((heads, width, keys), f32),
        ]
        + [pltpu.VMEM((chunk, keys), f32)] * 4
        + [pltpu.VMEM((groups * tokens if kept else 2 * chunk, keys), bf16)],
        compiler_params=params(kept),
        cost_estimate=pl.CostEstimate(
            flops=2 * 4 * rows * (keys) * width,
            bytes_accessed=8 * rows * (keys),
            transcendentals=rows * (keys),
        ),
        input_output_aliases={1: 2, 2: 3},
        name="far",
    )(start, log1, mean1, qs, dos, qt, dt, *pairs)


def tail(share, shift, k1, k2, qt, dt, w1, u1, ds2, sizes):
    tokens, groups, heads, width, here, kept = sizes
    chunk = here * groups
    rows = tokens * groups * heads
    blocks = tokens // here
    near_keys, far_keys = k1.shape[1], k2.shape[1]

    def both(columns):
        if kept:
            return VMEM
        return pl.BlockSpec((heads, chunk, columns), lambda i: (0, i, 0))

    def turned(h):
        if kept:
            return VMEM
        return pl.BlockSpec((width, chunk), lambda i: (0, h * blocks + i))

    def by_head(a):
        return a.reshape(heads, rows // heads, a.shape[1])

    return pl.pallas_call(
        functools.partial(tail_kernel, sizes),
        grid=(blocks,),
        in_specs=[
            whole(heads, near_keys, width),
            whole(heads, far_keys, width),
            both(128),
            both(128),
            both(near_keys),
            both(near_keys),
            both(far_keys),
        ]
        + [turned(h) for h in range(heads)] * 2,
        out_specs=[pl.BlockSpec((chunk * heads, width), lambda i: (i, 0)), VMEM, VMEM],
        out_shape=[
            jax.ShapeDtypeStruct((rows, width), f32),
            jax.ShapeDtypeStruct((2, tokens * heads, width), f32),
            jax.ShapeDtypeStruct((2, tokens * heads, width), bf16),
        ],
        scratch_shapes=[
            pltpu.VMEM((heads, width, near_keys), f32),
            pltpu.VMEM((heads, width, near_keys), f32),
            *[pltpu.VMEM((chunk, near_keys), bf16)] * (2 * heads),
        ],
        compiler_params=params(kept, 14),
        cost_estimate=pl.CostEstimate(
            flops=6 * rows * (near_keys + far_keys) * width,
            bytes_accessed=8 * rows * (near_keys + far_keys),
            transcendentals=rows * (near_keys + far_keys),
        ),
        name="tail",
    )(
        k1,
        k2,
        *[by_head(a) for a in (share, shift, w1, u1, ds2)],
        *[qt] * heads,
        *[dt] * heads,
    )


def shards(queries, keys, values, output_gradient, band_start):
    tokens, heads, groups, width = queries.shape
    count = lax.axis_size("ctx")
    reach = min(WINDOW // tokens, count - 1)
    hops = min((reach + 1) // 2, count // 2 - 1)

    def in_hbm(a):
        return pltpu.with_memory_space_constraint(a, pltpu.HBM)

    own = pack(
        in_hbm(keys.reshape(tokens * heads, width)),
        in_hbm(values.reshape(tokens * heads, width)),
        heads,
    )
    same = [moved(own, 2 * d) for d in range(1, hops + 1)]
    partner = swapped(own)
    start = band_start.reshape(1, tokens)
    kept = hops <= 2
    here = tokens // (4 if kept else 8)
    sizes = (tokens, groups, heads, width, here, kept)

    def flat(a):
        return a.transpose(0, 2, 1, 3).reshape(tokens * groups * heads, width)

    qs, dos = prep(in_hbm(flat(queries)), in_hbm(flat(output_gradient)), sizes)
    w1, u1, k1, log1, mean1, qt, dt = near(qs, dos, start, own, partner, sizes)
    *same, log1 = lax.optimization_barrier((*same, log1))
    other = [swapped(block) for block in same]
    k2, ds2, share, shift, *parts = far(
        start, log1, mean1, qs, dos, qt, dt, same + other, sizes
    )
    arriving = []
    for d in range(hops):
        crossed = swapped(parts[hops + d])
        both = (parts[d].astype(f32) + crossed.astype(f32)).astype(bf16)
        both, share = lax.optimization_barrier((both, share))
        arriving.append(moved(both, -2 * (d + 1)))
    dq, total, crossing = tail(share, shift, k1, k2, qt, dt, w1, u1, ds2, sizes)
    crossed = [swapped(half) for half in crossing]
    dk, dv = finish(total, crossed, arriving, heads)
    return (
        dq.reshape(tokens, groups, heads, width).transpose(0, 2, 1, 3),
        dk.reshape(tokens, heads, width),
        dv.reshape(tokens, heads, width),
    )


def solution(mesh):
    rows = P(("rep", "ctx"), "kv", None, None)
    keys = P(("rep", "ctx"), "kv", None)
    return jax.shard_map(
        shards,
        mesh=mesh,
        in_specs=(rows, keys, keys, rows, P(("rep", "ctx"))),
        out_specs=(rows, keys, keys),
        check_vma=False,
    )
```

time: 43.4 us -> 41.8 us (0.963)
  the two profiles are of different devices: /device:TPU:0 before, /device:TPU:27 now
where the time goes in v4:
time: 41.8 us; the launch traced here: 41.6 us
  Pallas kernels  32.5 us (78%)
  starting transfers between devices  4.37 us (10%)
  waiting for transfers between devices  3.94 us (9%)
  between operations  0.72 us (2%)
    pallas_call x1, Pallas kernels, far(): pl.pallas_call(functools.partial(far_kernel, (tokens, groups, heads, slot...  11.5 us
    pallas_call x1, Pallas kernels, tail(): pl.pallas_call(functools.partial(tail_kernel, sizes), grid=(blocks,), in_...  8.85 us
    pallas_call x1, Pallas kernels, near(): pl.pallas_call(functools.partial(near_kernel, sizes), grid=(rows // (2 *...  7.83 us
    ppermute x5, waiting for transfers between devices, swapped(): lax.ppermute(block, 'ctx', [(i, i ^ 1) for i in range(lax.axis_size('ctx'...  3.94 us
    ppermute x2, starting transfers between devices, moved(): return lax.ppermute(block, 'ctx', route)  2.77 us
    pallas_call x1, Pallas kernels, prep(): pl.pallas_call(functools.partial(prep_kernel, sizes), in_specs=[pl.BlockS...  2.46 us
    ppermute x5, starting transfers between devices, swapped(): lax.ppermute(block, 'ctx', [(i, i ^ 1) for i in range(lax.axis_size('ctx'...  1.61 us
    pallas_call x1, Pallas kernels, pack(): pl.pallas_call(functools.partial(pack_kernel, heads), in_specs=[pl.BlockS...  1.02 us
  transfers between devices with their start and end apart: 7, of which 4 were waited for; matrix products, arithmetic and copies ran while one was open for 0% of the time, Pallas kernels for 46%

profile of v4, /device:TPU:27, one launch (start us, length us, event | category | flops | bytes accessed | tf_op | source)
XLA Modules:
  0.0 41.6 jit_solution(1967217938920493392)
XLA Ops:
  0.6 0.0 copy-start
  0.6 1.0 %pack.1.own_ref = bf16[2,512,128]{2,1,0:T(8,128)(2,1)S(1)} custom-call(bf16[512,128]{1,0:T(8,128)(2,1)} %bitcast.32, bf16[512,128]{1,0:T(8,128)(2,1)} %bitcast.33), custom_call_target="tpu_custom_call" | custom-call | tf_op jit(solution)/shard_map/pack/pallas_call | solution.py:353
  1.7 0.7 %collective-permute-start = (bf16[2,512,128]{2,1,0:T(8,128)(2,1)S(1)}, bf16[2,512,128]{2,1,0:T(8,128)(2,1)S(1)}, u32[]{:S(2)}, u32[]{:S(2)}) collective-permute-start(bf16[2,512,128]{2,1,0:T(8,128)(2,1)S(1)} %pack.1.own_ref), channel_id=1, source_target_pairs={{0,8},{8,0},{16,24},{24,16},{1,9},{9,1},{17,25},{25,17},{2,10},{10... | collective-permute-start | bytes 786440 | tf_op jit(solution)/shard_map/ppermute | solution.py:26
  2.4 1.3 %collective-permute-start.1 = (bf16[2,512,128]{2,1,0:T(8,128)(2,1)S(1)}, bf16[2,512,128]{2,1,0:T(8,128)(2,1)S(1)}, u32[]{:S(2)}, u32[]{:S(2)}) collective-permute-start(bf16[2,512,128]{2,1,0:T(8,128)(2,1)S(1)} %pack.1.own_ref), channel_id=1, source_target_pairs={{0,16},{8,24},{1,17},{9,25},{2,18},{10,26},{3,19},{11,27},{4,20},{... | collective-permute-start | bytes 786440 | tf_op jit(solution)/shard_map/ppermute | solution.py:22
  3.7 2.5 %prep.1 = (bf16[6144,128]{1,0:T(8,128)(2,1)S(1)}, bf16[6144,128]{1,0:T(8,128)(2,1)S(1)}) custom-call(bf16[6144,128]{1,0:T(8,128)(2,1)} %bitcast.30, bf16[6144,128]{1,0:T(8,128)(2,1)} %bitcast.31), custom_call_target="tpu_custom_call" | custom-call | tf_op jit(solution)/shard_map/prep/pallas_call | solution.py:405
  6.2 0.0 collective-permute-done.partner_ref
  6.2 0.0 copy-done
  6.2 7.8 %near.1 = (bf16[6144,512]{1,0:T(8,128)(2,1)S(1)}, bf16[6144,512]{1,0:T(8,128)(2,1)S(1)}, bf16[2,512,128]{2,1,0:T(8,128)(2,1)S(1)}, f32[6144,128]{1,0:T(8,128)S(1...) custom-call(bf16[6144,128]{1,0:T(8,128)(2,1)S(1)} %get-tuple-element.27.qs.qs_ref, ...), custom_call_target="tpu_custom_call" | custom-call | flops 1610612736 | bytes 25165824 | tf_op jit(solution)/shard_map/near/pallas_call | solution.py:426
  14.0 0.0 collective-permute-done.1.refs_0_
  14.0 0.1 collective-permute-start.2
  14.1 1.5 %collective-permute-done.2.refs_1_ = bf16[2,512,128]{2,1,0:T(8,128)(2,1)S(1)} collective-permute-done((bf16[2,512,128]{2,1,0:T(8,128)(2,1)S(1)}, bf16[2,512,128]{2,1,0:T(8,128)(2,1)S(1)}, u32[]{:S(2)}, u32[]{:S(2)}) %collective-permute-start.2) | collective-permute-done | bytes 262176 | tf_op jit(solution)/shard_map/ppermute | solution.py:26
  15.6 11.5 %far.1 = (bf16[2,512,128]{2,1,0:T(8,128)(2,1)S(1)}, bf16[6144,512]{1,0:T(8,128)(2,1)S(1)}, f32[6144,128]{1,0:T(8,128)S(1)}, f32[6144,128]{1,0:T(8,128)S(1)}, bf1...) custom-call(s32[1,256]{1,0:T(1,128)S(1)} %bitcast.29, ...), custom_call_target="tpu_custom_call", output_to_operand_aliasing={{2}: (1, {}), {3}: (2, {})} | custom-call | flops 3221225472 | bytes 25165824 | tf_op jit(solution)/shard_map/far/pallas_call | solution.py:469
  27.1 0.2 collective-permute-start.3
  27.3 1.4 %collective-permute-done.3 = bf16[2,512,128]{2,1,0:T(8,128)(2,1)S(1)} collective-permute-done((bf16[2,512,128]{2,1,0:T(8,128)(2,1)S(1)}, bf16[2,512,128]{2,1,0:T(8,128)(2,1)S(1)}, u32[]{:S(2)}, u32[]{:S(2)}) %collective-permute-start.3) | collective-permute-done | bytes 262176 | tf_op jit(solution)/shard_map/ppermute | solution.py:26
  28.7 0.1 add_convert_fusion
  28.8 1.5 %collective-permute-start.6 = (bf16[2,512,128]{2,1,0:T(8,128)(2,1)S(1)}, bf16[2,512,128]{2,1,0:T(8,128)(2,1)S(1)}, u32[]{:S(2)}, u32[]{:S(2)}) collective-permute-start(bf16[2,512,128]{2,1,0:T(8,128)(2,1)S(1)} %add_convert_fusion), channel_id=1, source_target_pairs={{16,0},{24,8},{17,1},{25,9},{18,2},{26,10},{19,3},{27,11},{20,4},{... | collective-permute-start | bytes 786440 | tf_op jit(solution)/shard_map/ppermute | solution.py:22
  30.3 8.8 %tail.1 = (f32[6144,128]{1,0:T(8,128)}, f32[2,512,128]{2,1,0:T(8,128)S(1)}, bf16[2,512,128]{2,1,0:T(8,128)(2,1)S(1)}) custom-call(bf16[2,512,128]{2,1,0:T(8,128)(2,1)S(1)} %get-tuple-element.29.k1_ref, bf16[2,512,128]{2,1,0:T(8,128)(2,1)S(1)} %get-tuple-element.36.k2_ref, f32[2,3072,128]{2,1,0:T(8,128)S(1)} %bitcast.23, f32[2,3072,128]{2,1,0:T(8,128)S(1)} %bitcast.24, ...), custom_call_target="tpu_custom_call" | custom-call | flops 4831838208 | bytes 50331648 | tf_op jit(solution)/shard_map/tail/pallas_call | solution.py:526
  39.2 0.2 collective-permute-start.5
  39.4 0.4 collective-permute-start.4
  39.8 0.8 %collective-permute-done.5.crossed_v_ref = bf16[512,128]{1,0:T(8,128)(2,1)S(1)} collective-permute-done((bf16[512,128]{1,0:T(8,128)(2,1)S(1)}, bf16[512,128]{1,0:T(8,128)(2,1)S(1)}, u32[]{:S(2)}, u32[]{:S(2)}) %collective-permute-start.5) | collective-permute-done | bytes 131104 | tf_op jit(solution)/shard_map/ppermute | solution.py:26
  40.6 0.2 collective-permute-done.4.crossed_k_ref
  40.8 0.0 collective-permute-done.6.refs_0_
  40.8 0.8 %finish.1 = (f32[512,128]{1,0:T(8,128)}, f32[512,128]{1,0:T(8,128)}) custom-call(f32[2,512,128]{2,1,0:T(8,128)S(1)} %get-tuple-element.46.own_ref, bf16[512,128]{1,0:T(8,128)(2,1)S(1)} %collective-permute-done.4.crossed_k_ref, bf16[512,128]{1,0:T(8,128)(2,1)S(1)} %collective-permute-done.5.crossed_v_ref, bf16[2,512,128]{2,1,0:T(8,128)(2,1)S(1)} %collective-permute-done.6.refs_0_), custom_call_target="tpu_custom_call" | custom-call | tf_op jit(solution)/shard_map/finish/pallas_call | solution.py:369
  (1 shorter events, 0.0 us)
Async XLA Ops:
  0.6 5.5 %copy-start = (s32[256]{0:T(256)S(1)}, s32[256]{0:T(256)}, u32[]{:S(2)}) copy-start(s32[256]{0:T(256)} %param.9) | copy-start | bytes 3076
  1.7 4.5 %collective-permute-start = (bf16[2,512,128]{2,1,0:T(8,128)(2,1)S(1)}, bf16[2,512,128]{2,1,0:T(8,128)(2,1)S(1)}, u32[]{:S(2)}, u32[]{:S(2)}) collective-permute-start(bf16[2,512,128]{2,1,0:T(8,128)(2,1)S(1)} %pack.1.own_ref), channel_id=1, source_target_pairs={{0,8},{8,0},{16,24},{24,16},{1,9},{9,1},{17,25},{25,17},{2,10},{10... | collective-permute-start | bytes 786440 | tf_op jit(solution)/shard_map/ppermute | solution.py:26
  2.4 11.6 %collective-permute-start.1 = (bf16[2,512,128]{2,1,0:T(8,128)(2,1)S(1)}, bf16[2,512,128]{2,1,0:T(8,128)(2,1)S(1)}, u32[]{:S(2)}, u32[]{:S(2)}) collective-permute-start(bf16[2,512,128]{2,1,0:T(8,128)(2,1)S(1)} %pack.1.own_ref), channel_id=1, source_target_pairs={{0,16},{8,24},{1,17},{9,25},{2,18},{10,26},{3,19},{11,27},{4,20},{... | collective-permute-start | bytes 786440 | tf_op jit(solution)/shard_map/ppermute | solution.py:22
  14.0 1.6 %collective-permute-start.2 = (bf16[2,512,128]{2,1,0:T(8,128)(2,1)S(1)}, bf16[2,512,128]{2,1,0:T(8,128)(2,1)S(1)}, u32[]{:S(2)}, u32[]{:S(2)}) collective-permute-start(bf16[2,512,128]{2,1,0:T(8,128)(2,1)S(1)} %collective-permute-done.1.refs_0_), channel_id=1, source_target_pairs={{0,8},{8,0},{16,24},{24,16},{1,9},{9,1},{17,25},{25,17},{2,10},{10... | collective-permute-start | bytes 786440 | tf_op jit(solution)/shard_map/ppermute | solution.py:26
  27.1 1.6 %collective-permute-start.3 = (bf16[2,512,128]{2,1,0:T(8,128)(2,1)S(1)}, bf16[2,512,128]{2,1,0:T(8,128)(2,1)S(1)}, u32[]{:S(2)}, u32[]{:S(2)}) collective-permute-start(bf16[2,512,128]{2,1,0:T(8,128)(2,1)S(1)} %get-tuple-element.38), channel_id=1, source_target_pairs={{0,8},{8,0},{16,24},{24,16},{1,9},{9,1},{17,25},{25,17},{2,10},{10... | collective-permute-start | bytes 786440 | tf_op jit(solution)/shard_map/ppermute | solution.py:26
  28.8 12.0 %collective-permute-start.6 = (bf16[2,512,128]{2,1,0:T(8,128)(2,1)S(1)}, bf16[2,512,128]{2,1,0:T(8,128)(2,1)S(1)}, u32[]{:S(2)}, u32[]{:S(2)}) collective-permute-start(bf16[2,512,128]{2,1,0:T(8,128)(2,1)S(1)} %add_convert_fusion), channel_id=1, source_target_pairs={{16,0},{24,8},{17,1},{25,9},{18,2},{26,10},{19,3},{27,11},{20,4},{... | collective-permute-start | bytes 786440 | tf_op jit(solution)/shard_map/ppermute | solution.py:22
  39.2 1.4 %collective-permute-start.5 = (bf16[512,128]{1,0:T(8,128)(2,1)S(1)}, bf16[512,128]{1,0:T(8,128)(2,1)S(1)}, u32[]{:S(2)}, u32[]{:S(2)}) collective-permute-start(bf16[512,128]{1,0:T(8,128)(2,1)S(1)} %get-tuple-element.51), channel_id=1, source_target_pairs={{0,8},{8,0},{16,24},{24,16},{1,9},{9,1},{17,25},{25,17},{2,10},{10... | collective-permute-start | bytes 393224 | tf_op jit(solution)/shard_map/ppermute | solution.py:26
  39.4 1.4 %collective-permute-start.4 = (bf16[512,128]{1,0:T(8,128)(2,1)S(1)}, bf16[512,128]{1,0:T(8,128)(2,1)S(1)}, u32[]{:S(2)}, u32[]{:S(2)}) collective-permute-start(bf16[512,128]{1,0:T(8,128)(2,1)S(1)} %get-tuple-element.52), channel_id=1, source_target_pairs={{0,8},{8,0},{16,24},{24,16},{1,9},{9,1},{17,25},{25,17},{2,10},{10... | collective-permute-start | bytes 393224 | tf_op jit(solution)/shard_map/ppermute | solution.py:26

commit v5 on v4

--- a/solution.py
+++ b/solution.py
@@ -290,13 +290,21 @@
             part[...] = jnp.zeros_like(part)
 
 
+def ahead_kernel(k_ref, ds_ref, dq_ref):
+    heads = k_ref.shape[0]
+    each = ds_ref.shape[0] // heads
+    for h in range(heads):
+        rows = slice(h * each, h * each + (each if h < heads - 1 else each // 2))
+        dq_ref[rows, :] = jnp.dot(ds_ref[rows, :], k_ref[h], preferred_element_type=f32)
+
+
 def tail_kernel(
     sizes, k1_ref, k2_ref, share_ref, shift_ref, w1_ref, u1_ref, ds2_ref, *refs,
 ):
     tokens, groups, heads, width, here, kept = sizes
     qt_refs, dot_refs = refs[:heads], refs[heads : 2 * heads]
-    dq_ref, own_ref, partner_ref, dk, dv = refs[2 * heads : 2 * heads + 5]
-    scratch = refs[2 * heads + 5 :]
+    ahead_ref = refs[2 * heads]
+    dq_ref, own_ref, partner_ref, dk, dv, *scratch = refs[2 * heads + (1 if kept else 0) :]
     chunk = here * groups
     i = pl.program_id(0)
     scale = width**-0.5
@@ -327,7 +335,12 @@
             dot_refs[h][:, columns], w_s[:, :keys], preferred_element_type=f32
         )
         dq = jnp.dot(ds, k1_ref[h, :keys], preferred_element_type=f32)
-        dq += jnp.dot(ds2_ref[h, pl.ds(first, chunk), :], k2_ref[h], preferred_element_type=f32)
+        if kept and (h < heads - 1 or keys < 2 * tokens):
+            dq += ahead_ref[pl.ds(h * groups * tokens + first, chunk), :]
+        else:
+            dq += jnp.dot(
+                ds2_ref[h, pl.ds(first, chunk), :], k2_ref[h], preferred_element_type=f32
+            )
         dq *= scale
         for g in range(groups):
             dq_ref[pl.ds(g * heads + h, here, stride=groups * heads), :] = dq[
@@ -503,7 +516,19 @@
     )(start, log1, mean1, qs, dos, qt, dt, *pairs)
 
 
-def tail(share, shift, k1, k2, qt, dt, w1, u1, ds2, sizes):
+def ahead(k2, ds2):
+    heads, _, width = k2.shape
+    return pl.pallas_call(
+        ahead_kernel,
+        in_specs=[VMEM] * 2,
+        out_specs=VMEM,
+        out_shape=jax.ShapeDtypeStruct((ds2.shape[0] - ds2.shape[0] // (2 * heads), width), f32),
+        compiler_params=params(True, 4),
+        name="ahead",
+    )(k2, ds2)
+
+
+def tail(share, shift, k1, k2, qt, dt, w1, u1, ds2, early, sizes):
     tokens, groups, heads, width, here, kept = sizes
     chunk = here * groups
     rows = tokens * groups * heads
@@ -535,7 +560,8 @@
             both(near_keys),
             both(far_keys),
         ]
-        + [turned(h) for h in range(heads)] * 2,
+        + [turned(h) for h in range(heads)] * 2
+        + [VMEM] * len(early),
         out_specs=[pl.BlockSpec((chunk * heads, width), lambda i: (i, 0)), VMEM, VMEM],
         out_shape=[
             jax.ShapeDtypeStruct((rows, width), f32),
@@ -560,6 +586,7 @@
         *[by_head(a) for a in (share, shift, w1, u1, ds2)],
         *[qt] * heads,
         *[dt] * heads,
+        *early,
     )
 
 
@@ -594,13 +621,16 @@
     k2, ds2, share, shift, *parts = far(
         start, log1, mean1, qs, dos, qt, dt, same + other, sizes
     )
+    early = [ahead(k2, ds2)] if kept else []
     arriving = []
     for d in range(hops):
         crossed = swapped(parts[hops + d])
         both = (parts[d].astype(f32) + crossed.astype(f32)).astype(bf16)
-        both, share = lax.optimization_barrier((both, share))
+        both, share, early = lax.optimization_barrier((both, share, early))
         arriving.append(moved(both, -2 * (d + 1)))
-    dq, total, crossing = tail(share, shift, k1, k2, qt, dt, w1, u1, ds2, sizes)
+    dq, total, crossing = tail(
+        share, shift, k1, k2, qt, dt, w1, u1, ds2, early, sizes
+    )
     crossed = [swapped(half) for half in crossing]
     dk, dv = finish(total, crossed, arriving, heads)
     return (

time: 41.8 us -> 40.8 us (0.976)
  the two profiles are of different devices: /device:TPU:27 before, /device:TPU:0 now
where the time goes in v5:
time: 40.8 us; the launch traced here: 40.3 us
  Pallas kernels  22.1 us (54%)
  waiting for transfers between devices  9.81 us (24%)
  starting transfers between devices  7.53 us (18%)
  between operations  0.74 us (2%)
    pallas_call x1, Pallas kernels, near(): pl.pallas_call(functools.partial(near_kernel, sizes), grid=(rows // (2 *...  7.84 us
    pallas_call x1, Pallas kernels, tail(): pl.pallas_call(functools.partial(tail_kernel, sizes), grid=(blocks,), in_...  7.5 us
    ppermute x2, waiting for transfers between devices, moved(): return lax.ppermute(block, 'ctx', route)  7.33 us
    ppermute x2, starting transfers between devices, moved(): return lax.ppermute(block, 'ctx', route)  5.89 us
    ppermute x5, waiting for transfers between devices, swapped(): lax.ppermute(block, 'ctx', [(i, i ^ 1) for i in range(lax.axis_size('ctx'...  2.47 us
    pallas_call x1, Pallas kernels, prep(): pl.pallas_call(functools.partial(prep_kernel, sizes), in_specs=[pl.BlockS...  2.46 us
    ppermute x5, starting transfers between devices, swapped(): lax.ppermute(block, 'ctx', [(i, i ^ 1) for i in range(lax.axis_size('ctx'...  1.64 us
    pallas_call x1, Pallas kernels, ahead(): pl.pallas_call(ahead_kernel, in_specs=[VMEM] * 2, out_specs=VMEM, out_sha...  1.38 us
  transfers between devices with their start and end apart: 7, of which 4 were waited for; matrix products, arithmetic and copies ran while one was open for 0% of the time, Pallas kernels for 48%

profile of v5, /device:TPU:0, one launch (start us, length us, event | category | flops | bytes accessed | tf_op | source)
XLA Modules:
  0.0 40.3 jit_solution(3616085369278658773)
XLA Ops:
  0.6 0.0 copy-start
  0.6 1.0 %pack.1.own_ref = bf16[2,512,128]{2,1,0:T(8,128)(2,1)S(1)} custom-call(bf16[512,128]{1,0:T(8,128)(2,1)} %bitcast.32, bf16[512,128]{1,0:T(8,128)(2,1)} %bitcast.33), custom_call_target="tpu_custom_call" | custom-call | tf_op jit(solution)/shard_map/pack/pallas_call | solution.py:366
  1.7 0.5 %collective-permute-start = (bf16[2,512,128]{2,1,0:T(8,128)(2,1)S(1)}, bf16[2,512,128]{2,1,0:T(8,128)(2,1)S(1)}, u32[]{:S(2)}, u32[]{:S(2)}) collective-permute-start(bf16[2,512,128]{2,1,0:T(8,128)(2,1)S(1)} %pack.1.own_ref), channel_id=1, source_target_pairs={{0,8},{8,0},{16,24},{24,16},{1,9},{9,1},{17,25},{25,17},{2,10},{10... | collective-permute-start | bytes 786440 | tf_op jit(solution)/shard_map/ppermute | solution.py:26
  2.2 4.4 %collective-permute-start.1 = (bf16[2,512,128]{2,1,0:T(8,128)(2,1)S(1)}, bf16[2,512,128]{2,1,0:T(8,128)(2,1)S(1)}, u32[]{:S(2)}, u32[]{:S(2)}) collective-permute-start(bf16[2,512,128]{2,1,0:T(8,128)(2,1)S(1)} %pack.1.own_ref), channel_id=1, source_target_pairs={{0,16},{8,24},{1,17},{9,25},{2,18},{10,26},{3,19},{11,27},{4,20},{... | collective-permute-start | bytes 786440 | tf_op jit(solution)/shard_map/ppermute | solution.py:22
  6.6 2.5 %prep.1 = (bf16[6144,128]{1,0:T(8,128)(2,1)S(1)}, bf16[6144,128]{1,0:T(8,128)(2,1)S(1)}) custom-call(bf16[6144,128]{1,0:T(8,128)(2,1)} %bitcast.30, bf16[6144,128]{1,0:T(8,128)(2,1)} %bitcast.31), custom_call_target="tpu_custom_call" | custom-call | tf_op jit(solution)/shard_map/prep/pallas_call | solution.py:418
  9.1 0.0 collective-permute-done.partner_ref
  9.1 0.0 copy-done
  9.1 7.8 %near.1 = (bf16[6144,512]{1,0:T(8,128)(2,1)S(1)}, bf16[6144,512]{1,0:T(8,128)(2,1)S(1)}, bf16[2,512,128]{2,1,0:T(8,128)(2,1)S(1)}, f32[6144,128]{1,0:T(8,128)S(1...) custom-call(bf16[6144,128]{1,0:T(8,128)(2,1)S(1)} %get-tuple-element.28.qs.qs_ref, ...), custom_call_target="tpu_custom_call" | custom-call | flops 1610612736 | bytes 25165824 | tf_op jit(solution)/shard_map/near/pallas_call | solution.py:439
  17.0 0.0 collective-permute-done.1.refs_0_
  17.0 0.3 collective-permute-start.2
  17.2 1.3 %collective-permute-done.2.refs_1_ = bf16[2,512,128]{2,1,0:T(8,128)(2,1)S(1)} collective-permute-done((bf16[2,512,128]{2,1,0:T(8,128)(2,1)S(1)}, bf16[2,512,128]{2,1,0:T(8,128)(2,1)S(1)}, u32[]{:S(2)}, u32[]{:S(2)}) %collective-permute-start.2) | collective-permute-done | bytes 262176 | tf_op jit(solution)/shard_map/ppermute | solution.py:26
  18.6 1.1 %far.1 = (bf16[2,512,128]{2,1,0:T(8,128)(2,1)S(1)}, bf16[6144,512]{1,0:T(8,128)(2,1)S(1)}, f32[6144,128]{1,0:T(8,128)S(1)}, f32[6144,128]{1,0:T(8,128)S(1)}, bf1...) custom-call(s32[1,256]{1,0:T(1,128)S(1)} %bitcast.29, ...), custom_call_target="tpu_custom_call", output_to_operand_aliasing={{2}: (1, {}), {3}: (2, {})} | custom-call | flops 3221225472 | bytes 25165824 | tf_op jit(solution)/shard_map/far/pallas_call | solution.py:482
  19.7 0.3 collective-permute-start.3
  19.9 1.4 %ahead.1.refs_4_ = f32[4608,128]{1,0:T(8,128)S(1)} custom-call(bf16[2,512,128]{2,1,0:T(8,128)(2,1)S(1)} %get-tuple-element.37.k_ref.k2_ref, bf16[6144,512]{1,0:T(8,128)(2,1)S(1)} %get-tuple-element.41.ds_ref), custom_call_target="tpu_custom_call" | custom-call | tf_op jit(solution)/shard_map/ahead/pallas_call | solution.py:521
  21.3 0.0 collective-permute-done.3
  21.3 0.1 add_convert_fusion
  21.4 1.5 %collective-permute-start.6 = (bf16[2,512,128]{2,1,0:T(8,128)(2,1)S(1)}, bf16[2,512,128]{2,1,0:T(8,128)(2,1)S(1)}, u32[]{:S(2)}, u32[]{:S(2)}) collective-permute-start(bf16[2,512,128]{2,1,0:T(8,128)(2,1)S(1)} %add_convert_fusion), channel_id=1, source_target_pairs={{16,0},{24,8},{17,1},{25,9},{18,2},{26,10},{19,3},{27,11},{20,4},{... | collective-permute-start | bytes 786440 | tf_op jit(solution)/shard_map/ppermute | solution.py:22
  22.9 7.5 %tail.1 = (f32[6144,128]{1,0:T(8,128)}, f32[2,512,128]{2,1,0:T(8,128)S(1)}, bf16[2,512,128]{2,1,0:T(8,128)(2,1)S(1)}) custom-call(bf16[2,512,128]{2,1,0:T(8,128)(2,1)S(1)} %get-tuple-element.30.k1_ref, bf16[2,512,128]{2,1,0:T(8,128)(2,1)S(1)} %get-tuple-element.37.k_ref.k2_ref, f32[2,3072,128]{2,1,0:T(8,128)S(1)} %bitcast.24, f32[2,3072,128]{2,1,0:T(8,128)S(1)} %bitcast.25, ...), custom_call_target="tpu_custom_call" | custom-call | flops 4831838208 | bytes 50331648 | tf_op jit(solution)/shard_map/tail/pallas_call | solution.py:551
  30.4 0.4 collective-permute-start.5
  30.8 0.2 collective-permute-start.4
  31.0 0.8 %collective-permute-done.5.crossed_v_ref = bf16[512,128]{1,0:T(8,128)(2,1)S(1)} collective-permute-done((bf16[512,128]{1,0:T(8,128)(2,1)S(1)}, bf16[512,128]{1,0:T(8,128)(2,1)S(1)}, u32[]{:S(2)}, u32[]{:S(2)}) %collective-permute-start.5) | collective-permute-done | bytes 131104 | tf_op jit(solution)/shard_map/ppermute | solution.py:26
  31.8 0.3 collective-permute-done.4.crossed_k_ref
  32.1 7.3 %collective-permute-done.6.refs_0_ = bf16[2,512,128]{2,1,0:T(8,128)(2,1)S(1)} collective-permute-done((bf16[2,512,128]{2,1,0:T(8,128)(2,1)S(1)}, bf16[2,512,128]{2,1,0:T(8,128)(2,1)S(1)}, u32[]{:S(2)}, u32[]{:S(2)}) %collective-permute-start.6) | collective-permute-done | bytes 262176 | tf_op jit(solution)/shard_map/ppermute | solution.py:22
  39.5 0.8 %finish.1 = (f32[512,128]{1,0:T(8,128)}, f32[512,128]{1,0:T(8,128)}) custom-call(f32[2,512,128]{2,1,0:T(8,128)S(1)} %get-tuple-element.48.own_ref, bf16[512,128]{1,0:T(8,128)(2,1)S(1)} %collective-permute-done.4.crossed_k_ref, bf16[512,128]{1,0:T(8,128)(2,1)S(1)} %collective-permute-done.5.crossed_v_ref, bf16[2,512,128]{2,1,0:T(8,128)(2,1)S(1)} %collective-permute-done.6.refs_0_), custom_call_target="tpu_custom_call" | custom-call | tf_op jit(solution)/shard_map/finish/pallas_call | solution.py:382
  (1 shorter events, 0.0 us)
Async XLA Ops:
  0.6 8.5 %copy-start = (s32[256]{0:T(256)S(1)}, s32[256]{0:T(256)}, u32[]{:S(2)}) copy-start(s32[256]{0:T(256)} %param.9) | copy-start | bytes 3076
  1.7 7.4 %collective-permute-start = (bf16[2,512,128]{2,1,0:T(8,128)(2,1)S(1)}, bf16[2,512,128]{2,1,0:T(8,128)(2,1)S(1)}, u32[]{:S(2)}, u32[]{:S(2)}) collective-permute-start(bf16[2,512,128]{2,1,0:T(8,128)(2,1)S(1)} %pack.1.own_ref), channel_id=1, source_target_pairs={{0,8},{8,0},{16,24},{24,16},{1,9},{9,1},{17,25},{25,17},{2,10},{10... | collective-permute-start | bytes 786440 | tf_op jit(solution)/shard_map/ppermute | solution.py:26
  2.2 14.8 %collective-permute-start.1 = (bf16[2,512,128]{2,1,0:T(8,128)(2,1)S(1)}, bf16[2,512,128]{2,1,0:T(8,128)(2,1)S(1)}, u32[]{:S(2)}, u32[]{:S(2)}) collective-permute-start(bf16[2,512,128]{2,1,0:T(8,128)(2,1)S(1)} %pack.1.own_ref), channel_id=1, source_target_pairs={{0,16},{8,24},{1,17},{9,25},{2,18},{10,26},{3,19},{11,27},{4,20},{... | collective-permute-start | bytes 786440 | tf_op jit(solution)/shard_map/ppermute | solution.py:22
  17.0 1.6 %collective-permute-start.2 = (bf16[2,512,128]{2,1,0:T(8,128)(2,1)S(1)}, bf16[2,512,128]{2,1,0:T(8,128)(2,1)S(1)}, u32[]{:S(2)}, u32[]{:S(2)}) collective-permute-start(bf16[2,512,128]{2,1,0:T(8,128)(2,1)S(1)} %collective-permute-done.1.refs_0_), channel_id=1, source_target_pairs={{0,8},{8,0},{16,24},{24,16},{1,9},{9,1},{17,25},{25,17},{2,10},{10... | collective-permute-start | bytes 786440 | tf_op jit(solution)/shard_map/ppermute | solution.py:26
  19.7 1.7 %collective-permute-start.3 = (bf16[2,512,128]{2,1,0:T(8,128)(2,1)S(1)}, bf16[2,512,128]{2,1,0:T(8,128)(2,1)S(1)}, u32[]{:S(2)}, u32[]{:S(2)}) collective-permute-start(bf16[2,512,128]{2,1,0:T(8,128)(2,1)S(1)} %get-tuple-element.39), channel_id=1, source_target_pairs={{0,8},{8,0},{16,24},{24,16},{1,9},{9,1},{17,25},{25,17},{2,10},{10... | collective-permute-start | bytes 786440 | tf_op jit(solution)/shard_map/ppermute | solution.py:26
  21.4 18.0 %collective-permute-start.6 = (bf16[2,512,128]{2,1,0:T(8,128)(2,1)S(1)}, bf16[2,512,128]{2,1,0:T(8,128)(2,1)S(1)}, u32[]{:S(2)}, u32[]{:S(2)}) collective-permute-start(bf16[2,512,128]{2,1,0:T(8,128)(2,1)S(1)} %add_convert_fusion), channel_id=1, source_target_pairs={{16,0},{24,8},{17,1},{25,9},{18,2},{26,10},{19,3},{27,11},{20,4},{... | collective-permute-start | bytes 786440 | tf_op jit(solution)/shard_map/ppermute | solution.py:22
  30.4 1.4 %collective-permute-start.5 = (bf16[512,128]{1,0:T(8,128)(2,1)S(1)}, bf16[512,128]{1,0:T(8,128)(2,1)S(1)}, u32[]{:S(2)}, u32[]{:S(2)}) collective-permute-start(bf16[512,128]{1,0:T(8,128)(2,1)S(1)} %get-tuple-element.53), channel_id=1, source_target_pairs={{0,8},{8,0},{16,24},{24,16},{1,9},{9,1},{17,25},{25,17},{2,10},{10... | collective-permute-start | bytes 393224 | tf_op jit(solution)/shard_map/ppermute | solution.py:26
  30.8 1.3 %collective-permute-start.4 = (bf16[512,128]{1,0:T(8,128)(2,1)S(1)}, bf16[512,128]{1,0:T(8,128)(2,1)S(1)}, u32[]{:S(2)}, u32[]{:S(2)}) collective-permute-start(bf16[512,128]{1,0:T(8,128)(2,1)S(1)} %get-tuple-element.54), channel_id=1, source_target_pairs={{0,8},{8,0},{16,24},{24,16},{1,9},{9,1},{17,25},{25,17},{2,10},{10... | collective-permute-start | bytes 393224 | tf_op jit(solution)/shard_map/ppermute | solution.py:26

commit v6 on v5

--- a/solution.py
+++ b/solution.py
@@ -203,7 +203,6 @@
     ctx = lax.axis_index("ctx")
     reached = ctx >= 2
     steps = blocks // 2
-    inside = pl.multiple_of(i % steps * 2 * chunk, 2 * chunk) if kept else 0
 
     def products(c, s, d):
         rows = pl.ds(pl.multiple_of(c * chunk, chunk), chunk)
@@ -211,20 +210,25 @@
         s[...] = lax.dot_general(qs_ref[rows, :], k_ref[h], ACROSS, preferred_element_type=f32)
         d[...] = lax.dot_general(dos_ref[rows, :], v_s[h], ACROSS, preferred_element_type=f32)
 
-    def gradients(count):
+    def head_gradients(h):
+        rows = slice(h * groups * tokens, (h + 1) * groups * tokens)
+        grads = (
+            jnp.dot(qt_ref[:, rows], ds_ref[rows, :], preferred_element_type=f32) * width**-0.5,
+            jnp.dot(dot_ref[:, rows], w_s[rows, :], preferred_element_type=f32),
+        )
+        for source, grad in enumerate(grads):
+            for slot, part in enumerate(part_refs):
+                part[source, h * tokens : (h + 1) * tokens, :] = grad[
+                    :, slot * tokens : (slot + 1) * tokens
+                ].T.astype(bf16)
+
+    def step_gradients():
         h = i // steps
-        rows = pl.ds(pl.multiple_of((i - count + 1) * 2 * chunk, 2 * chunk), count * 2 * chunk)
-        ds = ds_ref[rows, :] if kept else ds_ref[...]
-        dk_part = jnp.dot(qt_ref[:, rows], ds, preferred_element_type=f32)
-        dv_part = jnp.dot(dot_ref[:, rows], w_s[...], preferred_element_type=f32)
-        if kept:
-            dk[h] = dk_part
-            dv[h] = dv_part
-        else:
-            dk[h] += dk_part
-            dv[h] += dv_part
-
-    def weights(c, half, s, d):
+        rows = pl.ds(pl.multiple_of(i * 2 * chunk, 2 * chunk), 2 * chunk)
+        dk[h] += jnp.dot(qt_ref[:, rows], ds_ref[...], preferred_element_type=f32)
+        dv[h] += jnp.dot(dot_ref[:, rows], w_s[...], preferred_element_type=f32)
+
+    def weights(c, half, s, d, first):
         size = chunk // 3
         band = bias[pl.ds(pl.multiple_of(c % blocks * here, here), here), :]
         band = jnp.concatenate([band] * (size // here), 0)
@@ -242,7 +246,7 @@
             mean = (jnp.sum(p * dp, -1, keepdims=True) + before * mean1) * inverse
             w = p * spread(inverse, x.shape[1])
             ds = (w * (dp - spread(mean, x.shape[1]))).astype(bf16)
-            there = pl.ds(inside + half * chunk + row, size)
+            there = out if kept else pl.ds(half * chunk + row, size)
             w_s[there, :] = w.astype(bf16)
             ds_ref[out, :] = ds
             share_ref[out, :] = before * inverse
@@ -260,21 +264,42 @@
             dv[...] = jnp.zeros_like(dv)
         products(0, s_a, d_a)
 
-    @pl.when(reached)
-    def _():
+    def step(i, first):
         products(2 * i + 1, s_b, d_b)
-        weights(2 * i, 0, s_a, d_a)
+        weights(2 * i, 0, s_a, d_a, first)
         products(jnp.minimum(2 * i + 2, chunks - 1), s_a, d_a)
-        weights(2 * i + 1, 1, s_b, d_b)
+        weights(2 * i + 1, 1, s_b, d_b, first)
 
     if kept:
-        pl.when(reached & (i % steps == steps - 1))(lambda: gradients(steps))
+        ends = [steps * h for h in range(1, heads)]
+        plain = reached
+        for end in ends:
+            plain &= i != end
+
+        @pl.when(plain)
+        def _():
+            step(i, first)
+
+        for h, end in enumerate(ends):
+
+            @pl.when(reached & (i == end))
+            def _():
+                head_gradients(h)
+                step(end, end * 2 * chunk)
+
+        @pl.when(reached & (i == pl.num_programs(0) - 1))
+        def _():
+            head_gradients(heads - 1)
     else:
-        pl.when(reached)(lambda: gradients(1))
-
-    @pl.when(reached & (i == pl.num_programs(0) - 1))
-    def _():
-        join_heads(dk, dv, part_refs, tokens, heads, width**-0.5)
+
+        @pl.when(reached)
+        def _():
+            step(i, first)
+            step_gradients()
+
+        @pl.when(reached & (i == pl.num_programs(0) - 1))
+        def _():
+            join_heads(dk, dv, part_refs, tokens, heads, width**-0.5)
 
     @pl.when(jnp.logical_not(reached))
     def _():
@@ -426,7 +451,7 @@
             pltpu.VMEM((pieces, rows // pieces, width), bf16),
             pltpu.SemaphoreType.DMA((pieces, 2)),
         ],
-        compiler_params=params(kept),
+        compiler_params=params(kept, 12),
         name="prep",
     )(q, do)
 
@@ -463,7 +488,7 @@
             pltpu.VMEM((tokens, keys), f32),
         ]
         + [pltpu.VMEM((chunk, keys), f32)] * 4,
-        compiler_params=params(kept),
+        compiler_params=params(kept, 12),
         cost_estimate=pl.CostEstimate(
             flops=2 * 2 * rows * (keys) * width,
             bytes_accessed=8 * rows * (keys),
@@ -504,8 +529,8 @@
             pltpu.VMEM((heads, width, keys), f32),
         ]
         + [pltpu.VMEM((chunk, keys), f32)] * 4
-        + [pltpu.VMEM((groups * tokens if kept else 2 * chunk, keys), bf16)],
-        compiler_params=params(kept),
+        + [pltpu.VMEM((rows if kept else 2 * chunk, keys), bf16)],
+        compiler_params=params(kept, 16),
         cost_estimate=pl.CostEstimate(
             flops=2 * 4 * rows * (keys) * width,
             bytes_accessed=8 * rows * (keys),
@@ -573,7 +598,7 @@
             pltpu.VMEM((heads, width, near_keys), f32),
             *[pltpu.VMEM((chunk, near_keys), bf16)] * (2 * heads),
         ],
-        compiler_params=params(kept, 14),
+        compiler_params=params(kept, 12),
         cost_estimate=pl.CostEstimate(
             flops=6 * rows * (near_keys + far_keys) * width,
             bytes_accessed=8 * rows * (near_keys + far_keys),

time: 40.8 us -> 39.7 us (0.973)
  waiting for transfers between devices: 9.81 us -> 8.99 us
    ppermute x2, waiting for transfers between devices: 7.33 us -> 6.52 us  [moved(): return lax.ppermute(block, 'ctx', route)]
  transfers between devices with their start and end apart: 7 -> 7, of which waited for: 4 -> 4; matrix products, arithmetic and copies ran while one was open for 0% -> 0% of each run, Pallas kernels for 48% -> 49%
where the time goes in v6:
time: 39.7 us; the launch traced here: 39.3 us
  Pallas kernels  22.1 us (56%)
  waiting for transfers between devices  8.99 us (23%)
  starting transfers between devices  7.35 us (19%)
  between operations  0.74 us (2%)
    pallas_call x1, Pallas kernels, near(): pl.pallas_call(functools.partial(near_kernel, sizes), grid=(rows // (2 *...  7.76 us
    pallas_call x1, Pallas kernels, tail(): pl.pallas_call(functools.partial(tail_kernel, sizes), grid=(blocks,), in_...  7.59 us
    ppermute x2, waiting for transfers between devices, moved(): return lax.ppermute(block, 'ctx', route)  6.52 us
    ppermute x2, starting transfers between devices, moved(): return lax.ppermute(block, 'ctx', route)  5.71 us
    ppermute x5, waiting for transfers between devices, swapped(): lax.ppermute(block, 'ctx', [(i, i ^ 1) for i in range(lax.axis_size('ctx'...  2.48 us
    pallas_call x1, Pallas kernels, prep(): pl.pallas_call(functools.partial(prep_kernel, sizes), in_specs=[pl.BlockS...  2.46 us
    ppermute x5, starting transfers between devices, swapped(): lax.ppermute(block, 'ctx', [(i, i ^ 1) for i in range(lax.axis_size('ctx'...  1.64 us
    pallas_call x1, Pallas kernels, ahead(): pl.pallas_call(ahead_kernel, in_specs=[VMEM] * 2, out_specs=VMEM, out_sha...  1.39 us
  transfers between devices with their start and end apart: 7, of which 4 were waited for; matrix products, arithmetic and copies ran while one was open for 0% of the time, Pallas kernels for 49%

profile of v6, /device:TPU:0, one launch (start us, length us, event | category | flops | bytes accessed | tf_op | source)
XLA Modules:
  0.0 39.3 jit_solution(7681931216982609523)
XLA Ops:
  0.6 0.0 copy-start
  0.6 1.0 %pack.1.own_ref = bf16[2,512,128]{2,1,0:T(8,128)(2,1)S(1)} custom-call(bf16[512,128]{1,0:T(8,128)(2,1)} %bitcast.32, bf16[512,128]{1,0:T(8,128)(2,1)} %bitcast.33), custom_call_target="tpu_custom_call" | custom-call | tf_op jit(solution)/shard_map/pack/pallas_call | solution.py:391
  1.7 0.5 %collective-permute-start = (bf16[2,512,128]{2,1,0:T(8,128)(2,1)S(1)}, bf16[2,512,128]{2,1,0:T(8,128)(2,1)S(1)}, u32[]{:S(2)}, u32[]{:S(2)}) collective-permute-start(bf16[2,512,128]{2,1,0:T(8,128)(2,1)S(1)} %pack.1.own_ref), channel_id=1, source_target_pairs={{0,8},{8,0},{16,24},{24,16},{1,9},{9,1},{17,25},{25,17},{2,10},{10... | collective-permute-start | bytes 786440 | tf_op jit(solution)/shard_map/ppermute | solution.py:26
  2.2 4.4 %collective-permute-start.1 = (bf16[2,512,128]{2,1,0:T(8,128)(2,1)S(1)}, bf16[2,512,128]{2,1,0:T(8,128)(2,1)S(1)}, u32[]{:S(2)}, u32[]{:S(2)}) collective-permute-start(bf16[2,512,128]{2,1,0:T(8,128)(2,1)S(1)} %pack.1.own_ref), channel_id=1, source_target_pairs={{0,16},{8,24},{1,17},{9,25},{2,18},{10,26},{3,19},{11,27},{4,20},{... | collective-permute-start | bytes 786440 | tf_op jit(solution)/shard_map/ppermute | solution.py:22
  6.6 2.5 %prep.1 = (bf16[6144,128]{1,0:T(8,128)(2,1)S(1)}, bf16[6144,128]{1,0:T(8,128)(2,1)S(1)}) custom-call(bf16[6144,128]{1,0:T(8,128)(2,1)} %bitcast.30, bf16[6144,128]{1,0:T(8,128)(2,1)} %bitcast.31), custom_call_target="tpu_custom_call" | custom-call | tf_op jit(solution)/shard_map/prep/pallas_call | solution.py:443
  9.1 0.0 collective-permute-done.partner_ref
  9.1 0.0 copy-done
  9.1 7.8 %near.1 = (bf16[6144,512]{1,0:T(8,128)(2,1)S(1)}, bf16[6144,512]{1,0:T(8,128)(2,1)S(1)}, bf16[2,512,128]{2,1,0:T(8,128)(2,1)S(1)}, f32[6144,128]{1,0:T(8,128)S(1...) custom-call(bf16[6144,128]{1,0:T(8,128)(2,1)S(1)} %get-tuple-element.28.qs.qs_ref, ...), custom_call_target="tpu_custom_call" | custom-call | flops 1610612736 | bytes 25165824 | tf_op jit(solution)/shard_map/near/pallas_call | solution.py:464
  16.9 0.0 collective-permute-done.1.refs_0_
  16.9 0.3 collective-permute-start.2
  17.2 1.3 %collective-permute-done.2.refs_1_ = bf16[2,512,128]{2,1,0:T(8,128)(2,1)S(1)} collective-permute-done((bf16[2,512,128]{2,1,0:T(8,128)(2,1)S(1)}, bf16[2,512,128]{2,1,0:T(8,128)(2,1)S(1)}, u32[]{:S(2)}, u32[]{:S(2)}) %collective-permute-start.2) | collective-permute-done | bytes 262176 | tf_op jit(solution)/shard_map/ppermute | solution.py:26
  18.5 1.1 %far.1 = (bf16[2,512,128]{2,1,0:T(8,128)(2,1)S(1)}, bf16[6144,512]{1,0:T(8,128)(2,1)S(1)}, f32[6144,128]{1,0:T(8,128)S(1)}, f32[6144,128]{1,0:T(8,128)S(1)}, bf1...) custom-call(s32[1,256]{1,0:T(1,128)S(1)} %bitcast.29, ...), custom_call_target="tpu_custom_call", output_to_operand_aliasing={{2}: (1, {}), {3}: (2, {})} | custom-call | flops 3221225472 | bytes 25165824 | tf_op jit(solution)/shard_map/far/pallas_call | solution.py:507
  19.6 0.3 collective-permute-start.3
  19.8 1.4 %ahead.1.refs_4_ = f32[4608,128]{1,0:T(8,128)S(1)} custom-call(bf16[2,512,128]{2,1,0:T(8,128)(2,1)S(1)} %get-tuple-element.37.k_ref.k2_ref, bf16[6144,512]{1,0:T(8,128)(2,1)S(1)} %get-tuple-element.41.ds_ref), custom_call_target="tpu_custom_call" | custom-call | tf_op jit(solution)/shard_map/ahead/pallas_call | solution.py:546
  21.2 0.0 collective-permute-done.3
  21.2 0.1 add_convert_fusion
  21.3 1.3 %collective-permute-start.6 = (bf16[2,512,128]{2,1,0:T(8,128)(2,1)S(1)}, bf16[2,512,128]{2,1,0:T(8,128)(2,1)S(1)}, u32[]{:S(2)}, u32[]{:S(2)}) collective-permute-start(bf16[2,512,128]{2,1,0:T(8,128)(2,1)S(1)} %add_convert_fusion), channel_id=1, source_target_pairs={{16,0},{24,8},{17,1},{25,9},{18,2},{26,10},{19,3},{27,11},{20,4},{... | collective-permute-start | bytes 786440 | tf_op jit(solution)/shard_map/ppermute | solution.py:22
  22.6 7.6 %tail.1 = (f32[6144,128]{1,0:T(8,128)}, f32[2,512,128]{2,1,0:T(8,128)S(1)}, bf16[2,512,128]{2,1,0:T(8,128)(2,1)S(1)}) custom-call(bf16[2,512,128]{2,1,0:T(8,128)(2,1)S(1)} %get-tuple-element.30.k1_ref, bf16[2,512,128]{2,1,0:T(8,128)(2,1)S(1)} %get-tuple-element.37.k_ref.k2_ref, f32[2,3072,128]{2,1,0:T(8,128)S(1)} %bitcast.24, f32[2,3072,128]{2,1,0:T(8,128)S(1)} %bitcast.25, ...), custom_call_target="tpu_custom_call" | custom-call | flops 4831838208 | bytes 50331648 | tf_op jit(solution)/shard_map/tail/pallas_call | solution.py:576
  30.2 0.4 collective-permute-start.5
  30.6 0.2 collective-permute-start.4
  30.8 0.8 %collective-permute-done.5.crossed_v_ref = bf16[512,128]{1,0:T(8,128)(2,1)S(1)} collective-permute-done((bf16[512,128]{1,0:T(8,128)(2,1)S(1)}, bf16[512,128]{1,0:T(8,128)(2,1)S(1)}, u32[]{:S(2)}, u32[]{:S(2)}) %collective-permute-start.5) | collective-permute-done | bytes 131104 | tf_op jit(solution)/shard_map/ppermute | solution.py:26
  31.6 0.3 collective-permute-done.4.crossed_k_ref
  32.0 6.5 %collective-permute-done.6.refs_0_ = bf16[2,512,128]{2,1,0:T(8,128)(2,1)S(1)} collective-permute-done((bf16[2,512,128]{2,1,0:T(8,128)(2,1)S(1)}, bf16[2,512,128]{2,1,0:T(8,128)(2,1)S(1)}, u32[]{:S(2)}, u32[]{:S(2)}) %collective-permute-start.6) | collective-permute-done | bytes 262176 | tf_op jit(solution)/shard_map/ppermute | solution.py:22
  38.5 0.8 %finish.1 = (f32[512,128]{1,0:T(8,128)}, f32[512,128]{1,0:T(8,128)}) custom-call(f32[2,512,128]{2,1,0:T(8,128)S(1)} %get-tuple-element.48.own_ref, bf16[512,128]{1,0:T(8,128)(2,1)S(1)} %collective-permute-done.4.crossed_k_ref, bf16[512,128]{1,0:T(8,128)(2,1)S(1)} %collective-permute-done.5.crossed_v_ref, bf16[2,512,128]{2,1,0:T(8,128)(2,1)S(1)} %collective-permute-done.6.refs_0_), custom_call_target="tpu_custom_call" | custom-call | tf_op jit(solution)/shard_map/finish/pallas_call | solution.py:407
  (1 shorter events, 0.0 us)
Async XLA Ops:
  0.6 8.5 %copy-start = (s32[256]{0:T(256)S(1)}, s32[256]{0:T(256)}, u32[]{:S(2)}) copy-start(s32[256]{0:T(256)} %param.9) | copy-start | bytes 3076
  1.7 7.4 %collective-permute-start = (bf16[2,512,128]{2,1,0:T(8,128)(2,1)S(1)}, bf16[2,512,128]{2,1,0:T(8,128)(2,1)S(1)}, u32[]{:S(2)}, u32[]{:S(2)}) collective-permute-start(bf16[2,512,128]{2,1,0:T(8,128)(2,1)S(1)} %pack.1.own_ref), channel_id=1, source_target_pairs={{0,8},{8,0},{16,24},{24,16},{1,9},{9,1},{17,25},{25,17},{2,10},{10... | collective-permute-start | bytes 786440 | tf_op jit(solution)/shard_map/ppermute | solution.py:26
  2.2 14.7 %collective-permute-start.1 = (bf16[2,512,128]{2,1,0:T(8,128)(2,1)S(1)}, bf16[2,512,128]{2,1,0:T(8,128)(2,1)S(1)}, u32[]{:S(2)}, u32[]{:S(2)}) collective-permute-start(bf16[2,512,128]{2,1,0:T(8,128)(2,1)S(1)} %pack.1.own_ref), channel_id=1, source_target_pairs={{0,16},{8,24},{1,17},{9,25},{2,18},{10,26},{3,19},{11,27},{4,20},{... | collective-permute-start | bytes 786440 | tf_op jit(solution)/shard_map/ppermute | solution.py:22
  16.9 1.6 %collective-permute-start.2 = (bf16[2,512,128]{2,1,0:T(8,128)(2,1)S(1)}, bf16[2,512,128]{2,1,0:T(8,128)(2,1)S(1)}, u32[]{:S(2)}, u32[]{:S(2)}) collective-permute-start(bf16[2,512,128]{2,1,0:T(8,128)(2,1)S(1)} %collective-permute-done.1.refs_0_), channel_id=1, source_target_pairs={{0,8},{8,0},{16,24},{24,16},{1,9},{9,1},{17,25},{25,17},{2,10},{10... | collective-permute-start | bytes 786440 | tf_op jit(solution)/shard_map/ppermute | solution.py:26
  19.6 1.7 %collective-permute-start.3 = (bf16[2,512,128]{2,1,0:T(8,128)(2,1)S(1)}, bf16[2,512,128]{2,1,0:T(8,128)(2,1)S(1)}, u32[]{:S(2)}, u32[]{:S(2)}) collective-permute-start(bf16[2,512,128]{2,1,0:T(8,128)(2,1)S(1)} %get-tuple-element.39), channel_id=1, source_target_pairs={{0,8},{8,0},{16,24},{24,16},{1,9},{9,1},{17,25},{25,17},{2,10},{10... | collective-permute-start | bytes 786440 | tf_op jit(solution)/shard_map/ppermute | solution.py:26
  21.3 17.1 %collective-permute-start.6 = (bf16[2,512,128]{2,1,0:T(8,128)(2,1)S(1)}, bf16[2,512,128]{2,1,0:T(8,128)(2,1)S(1)}, u32[]{:S(2)}, u32[]{:S(2)}) collective-permute-start(bf16[2,512,128]{2,1,0:T(8,128)(2,1)S(1)} %add_convert_fusion), channel_id=1, source_target_pairs={{16,0},{24,8},{17,1},{25,9},{18,2},{26,10},{19,3},{27,11},{20,4},{... | collective-permute-start | bytes 786440 | tf_op jit(solution)/shard_map/ppermute | solution.py:22
  30.2 1.4 %collective-permute-start.5 = (bf16[512,128]{1,0:T(8,128)(2,1)S(1)}, bf16[512,128]{1,0:T(8,128)(2,1)S(1)}, u32[]{:S(2)}, u32[]{:S(2)}) collective-permute-start(bf16[512,128]{1,0:T(8,128)(2,1)S(1)} %get-tuple-element.53), channel_id=1, source_target_pairs={{0,8},{8,0},{16,24},{24,16},{1,9},{9,1},{17,25},{25,17},{2,10},{10... | collective-permute-start | bytes 393224 | tf_op jit(solution)/shard_map/ppermute | solution.py:26
  30.6 1.3 %collective-permute-start.4 = (bf16[512,128]{1,0:T(8,128)(2,1)S(1)}, bf16[512,128]{1,0:T(8,128)(2,1)S(1)}, u32[]{:S(2)}, u32[]{:S(2)}) collective-permute-start(bf16[512,128]{1,0:T(8,128)(2,1)S(1)} %get-tuple-element.54), channel_id=1, source_target_pairs={{0,8},{8,0},{16,24},{24,16},{1,9},{9,1},{17,25},{25,17},{2,10},{10... | collective-permute-start | bytes 393224 | tf_op jit(solution)/shard_map/ppermute | solution.py:26

commit v7 on v6

--- a/solution.py
+++ b/solution.py
@@ -139,7 +139,7 @@
         d[:, :keys] = lax.dot_general(dos[rows, :], v_s[h, :keys], ACROSS, preferred_element_type=f32)
 
     def weights(c, half, s, d, keys):
-        size = chunk // 3
+        size = chunk // (2 if kept else 3)
         band = bias[pl.ds(pl.multiple_of(c % blocks * here, here), here), :keys]
         band = jnp.concatenate([band] * (size // here), 0)
         for row in range(0, chunk, size):
@@ -229,7 +229,7 @@
         dv[h] += jnp.dot(dot_ref[:, rows], w_s[...], preferred_element_type=f32)
 
     def weights(c, half, s, d, first):
-        size = chunk // 3
+        size = chunk // (2 if kept else 3)
         band = bias[pl.ds(pl.multiple_of(c % blocks * here, here), here), :]
         band = jnp.concatenate([band] * (size // here), 0)
         for row in range(0, chunk, size):

time: 39.7 us -> 39.4 us (level)
  no operation moved by 1% of the time
where the time goes in v7:
time: 39.4 us; the launch traced here: 39 us
  Pallas kernels  22 us (56%)
  waiting for transfers between devices  8.87 us (23%)
  starting transfers between devices  7.37 us (19%)
  between operations  0.74 us (2%)
    pallas_call x1, Pallas kernels, tail(): pl.pallas_call(functools.partial(tail_kernel, sizes), grid=(blocks,), in_...  7.58 us
    pallas_call x1, Pallas kernels, near(): pl.pallas_call(functools.partial(near_kernel, sizes), grid=(rows // (2 *...  7.57 us
    ppermute x2, waiting for transfers between devices, moved(): return lax.ppermute(block, 'ctx', route)  6.41 us
    ppermute x2, starting transfers between devices, moved(): return lax.ppermute(block, 'ctx', route)  5.71 us
    ppermute x5, waiting for transfers between devices, swapped(): lax.ppermute(block, 'ctx', [(i, i ^ 1) for i in range(lax.axis_size('ctx'...  2.46 us
    pallas_call x1, Pallas kernels, prep(): pl.pallas_call(functools.partial(prep_kernel, sizes), in_specs=[pl.BlockS...  2.46 us
    ppermute x5, starting transfers between devices, swapped(): lax.ppermute(block, 'ctx', [(i, i ^ 1) for i in range(lax.axis_size('ctx'...  1.65 us
    pallas_call x1, Pallas kernels, ahead(): pl.pallas_call(ahead_kernel, in_specs=[VMEM] * 2, out_specs=VMEM, out_sha...  1.39 us
  transfers between devices with their start and end apart: 7, of which 4 were waited for; matrix products, arithmetic and copies ran while one was open for 0% of the time, Pallas kernels for 49%

profile of v7, /device:TPU:0, one launch (start us, length us, event | category | flops | bytes accessed | tf_op | source)
XLA Modules:
  0.0 39.0 jit_solution(6987979065342570818)
XLA Ops:
  0.6 0.0 copy-start
  0.6 1.0 %pack.1.own_ref = bf16[2,512,128]{2,1,0:T(8,128)(2,1)S(1)} custom-call(bf16[512,128]{1,0:T(8,128)(2,1)} %bitcast.32, bf16[512,128]{1,0:T(8,128)(2,1)} %bitcast.33), custom_call_target="tpu_custom_call" | custom-call | tf_op jit(solution)/shard_map/pack/pallas_call | solution.py:391
  1.7 0.5 %collective-permute-start = (bf16[2,512,128]{2,1,0:T(8,128)(2,1)S(1)}, bf16[2,512,128]{2,1,0:T(8,128)(2,1)S(1)}, u32[]{:S(2)}, u32[]{:S(2)}) collective-permute-start(bf16[2,512,128]{2,1,0:T(8,128)(2,1)S(1)} %pack.1.own_ref), channel_id=1, source_target_pairs={{0,8},{8,0},{16,24},{24,16},{1,9},{9,1},{17,25},{25,17},{2,10},{10... | collective-permute-start | bytes 786440 | tf_op jit(solution)/shard_map/ppermute | solution.py:26
  2.2 4.4 %collective-permute-start.1 = (bf16[2,512,128]{2,1,0:T(8,128)(2,1)S(1)}, bf16[2,512,128]{2,1,0:T(8,128)(2,1)S(1)}, u32[]{:S(2)}, u32[]{:S(2)}) collective-permute-start(bf16[2,512,128]{2,1,0:T(8,128)(2,1)S(1)} %pack.1.own_ref), channel_id=1, source_target_pairs={{0,16},{8,24},{1,17},{9,25},{2,18},{10,26},{3,19},{11,27},{4,20},{... | collective-permute-start | bytes 786440 | tf_op jit(solution)/shard_map/ppermute | solution.py:22
  6.6 2.5 %prep.1 = (bf16[6144,128]{1,0:T(8,128)(2,1)S(1)}, bf16[6144,128]{1,0:T(8,128)(2,1)S(1)}) custom-call(bf16[6144,128]{1,0:T(8,128)(2,1)} %bitcast.30, bf16[6144,128]{1,0:T(8,128)(2,1)} %bitcast.31), custom_call_target="tpu_custom_call" | custom-call | tf_op jit(solution)/shard_map/prep/pallas_call | solution.py:443
  9.1 0.0 collective-permute-done.partner_ref
  9.1 0.0 copy-done
  9.1 7.6 %near.1 = (bf16[6144,512]{1,0:T(8,128)(2,1)S(1)}, bf16[6144,512]{1,0:T(8,128)(2,1)S(1)}, bf16[2,512,128]{2,1,0:T(8,128)(2,1)S(1)}, f32[6144,128]{1,0:T(8,128)S(1...) custom-call(bf16[6144,128]{1,0:T(8,128)(2,1)S(1)} %get-tuple-element.28.qs.qs_ref, ...), custom_call_target="tpu_custom_call" | custom-call | flops 1610612736 | bytes 25165824 | tf_op jit(solution)/shard_map/near/pallas_call | solution.py:464
  16.7 0.0 collective-permute-done.1.refs_0_
  16.7 0.3 collective-permute-start.2
  17.0 1.3 %collective-permute-done.2.refs_1_ = bf16[2,512,128]{2,1,0:T(8,128)(2,1)S(1)} collective-permute-done((bf16[2,512,128]{2,1,0:T(8,128)(2,1)S(1)}, bf16[2,512,128]{2,1,0:T(8,128)(2,1)S(1)}, u32[]{:S(2)}, u32[]{:S(2)}) %collective-permute-start.2) | collective-permute-done | bytes 262176 | tf_op jit(solution)/shard_map/ppermute | solution.py:26
  18.3 1.1 %far.1 = (bf16[2,512,128]{2,1,0:T(8,128)(2,1)S(1)}, bf16[6144,512]{1,0:T(8,128)(2,1)S(1)}, f32[6144,128]{1,0:T(8,128)S(1)}, f32[6144,128]{1,0:T(8,128)S(1)}, bf1...) custom-call(s32[1,256]{1,0:T(1,128)S(1)} %bitcast.29, ...), custom_call_target="tpu_custom_call", output_to_operand_aliasing={{2}: (1, {}), {3}: (2, {})} | custom-call | flops 3221225472 | bytes 25165824 | tf_op jit(solution)/shard_map/far/pallas_call | solution.py:507
  19.4 0.3 collective-permute-start.3
  19.7 1.4 %ahead.1.refs_4_ = f32[4608,128]{1,0:T(8,128)S(1)} custom-call(bf16[2,512,128]{2,1,0:T(8,128)(2,1)S(1)} %get-tuple-element.37.k_ref.k2_ref, bf16[6144,512]{1,0:T(8,128)(2,1)S(1)} %get-tuple-element.41.ds_ref), custom_call_target="tpu_custom_call" | custom-call | tf_op jit(solution)/shard_map/ahead/pallas_call | solution.py:546
  21.1 0.0 collective-permute-done.3
  21.1 0.1 add_convert_fusion
  21.1 1.3 %collective-permute-start.6 = (bf16[2,512,128]{2,1,0:T(8,128)(2,1)S(1)}, bf16[2,512,128]{2,1,0:T(8,128)(2,1)S(1)}, u32[]{:S(2)}, u32[]{:S(2)}) collective-permute-start(bf16[2,512,128]{2,1,0:T(8,128)(2,1)S(1)} %add_convert_fusion), channel_id=1, source_target_pairs={{16,0},{24,8},{17,1},{25,9},{18,2},{26,10},{19,3},{27,11},{20,4},{... | collective-permute-start | bytes 786440 | tf_op jit(solution)/shard_map/ppermute | solution.py:22
  22.4 7.6 %tail.1 = (f32[6144,128]{1,0:T(8,128)}, f32[2,512,128]{2,1,0:T(8,128)S(1)}, bf16[2,512,128]{2,1,0:T(8,128)(2,1)S(1)}) custom-call(bf16[2,512,128]{2,1,0:T(8,128)(2,1)S(1)} %get-tuple-element.30.k1_ref, bf16[2,512,128]{2,1,0:T(8,128)(2,1)S(1)} %get-tuple-element.37.k_ref.k2_ref, f32[2,3072,128]{2,1,0:T(8,128)S(1)} %bitcast.24, f32[2,3072,128]{2,1,0:T(8,128)S(1)} %bitcast.25, ...), custom_call_target="tpu_custom_call" | custom-call | flops 4831838208 | bytes 50331648 | tf_op jit(solution)/shard_map/tail/pallas_call | solution.py:576
  30.0 0.4 collective-permute-start.5
  30.4 0.2 collective-permute-start.4
  30.6 0.8 %collective-permute-done.5.crossed_v_ref = bf16[512,128]{1,0:T(8,128)(2,1)S(1)} collective-permute-done((bf16[512,128]{1,0:T(8,128)(2,1)S(1)}, bf16[512,128]{1,0:T(8,128)(2,1)S(1)}, u32[]{:S(2)}, u32[]{:S(2)}) %collective-permute-start.5) | collective-permute-done | bytes 131104 | tf_op jit(solution)/shard_map/ppermute | solution.py:26
  31.5 0.3 collective-permute-done.4.crossed_k_ref
  31.8 6.4 %collective-permute-done.6.refs_0_ = bf16[2,512,128]{2,1,0:T(8,128)(2,1)S(1)} collective-permute-done((bf16[2,512,128]{2,1,0:T(8,128)(2,1)S(1)}, bf16[2,512,128]{2,1,0:T(8,128)(2,1)S(1)}, u32[]{:S(2)}, u32[]{:S(2)}) %collective-permute-start.6) | collective-permute-done | bytes 262176 | tf_op jit(solution)/shard_map/ppermute | solution.py:22
  38.2 0.8 %finish.1 = (f32[512,128]{1,0:T(8,128)}, f32[512,128]{1,0:T(8,128)}) custom-call(f32[2,512,128]{2,1,0:T(8,128)S(1)} %get-tuple-element.48.own_ref, bf16[512,128]{1,0:T(8,128)(2,1)S(1)} %collective-permute-done.4.crossed_k_ref, bf16[512,128]{1,0:T(8,128)(2,1)S(1)} %collective-permute-done.5.crossed_v_ref, bf16[2,512,128]{2,1,0:T(8,128)(2,1)S(1)} %collective-permute-done.6.refs_0_), custom_call_target="tpu_custom_call" | custom-call | tf_op jit(solution)/shard_map/finish/pallas_call | solution.py:407
  (1 shorter events, 0.0 us)
Async XLA Ops:
  0.6 8.5 %copy-start = (s32[256]{0:T(256)S(1)}, s32[256]{0:T(256)}, u32[]{:S(2)}) copy-start(s32[256]{0:T(256)} %param.9) | copy-start | bytes 3076
  1.7 7.4 %collective-permute-start = (bf16[2,512,128]{2,1,0:T(8,128)(2,1)S(1)}, bf16[2,512,128]{2,1,0:T(8,128)(2,1)S(1)}, u32[]{:S(2)}, u32[]{:S(2)}) collective-permute-start(bf16[2,512,128]{2,1,0:T(8,128)(2,1)S(1)} %pack.1.own_ref), channel_id=1, source_target_pairs={{0,8},{8,0},{16,24},{24,16},{1,9},{9,1},{17,25},{25,17},{2,10},{10... | collective-permute-start | bytes 786440 | tf_op jit(solution)/shard_map/ppermute | solution.py:26
  2.2 14.5 %collective-permute-start.1 = (bf16[2,512,128]{2,1,0:T(8,128)(2,1)S(1)}, bf16[2,512,128]{2,1,0:T(8,128)(2,1)S(1)}, u32[]{:S(2)}, u32[]{:S(2)}) collective-permute-start(bf16[2,512,128]{2,1,0:T(8,128)(2,1)S(1)} %pack.1.own_ref), channel_id=1, source_target_pairs={{0,16},{8,24},{1,17},{9,25},{2,18},{10,26},{3,19},{11,27},{4,20},{... | collective-permute-start | bytes 786440 | tf_op jit(solution)/shard_map/ppermute | solution.py:22
  16.7 1.6 %collective-permute-start.2 = (bf16[2,512,128]{2,1,0:T(8,128)(2,1)S(1)}, bf16[2,512,128]{2,1,0:T(8,128)(2,1)S(1)}, u32[]{:S(2)}, u32[]{:S(2)}) collective-permute-start(bf16[2,512,128]{2,1,0:T(8,128)(2,1)S(1)} %collective-permute-done.1.refs_0_), channel_id=1, source_target_pairs={{0,8},{8,0},{16,24},{24,16},{1,9},{9,1},{17,25},{25,17},{2,10},{10... | collective-permute-start | bytes 786440 | tf_op jit(solution)/shard_map/ppermute | solution.py:26
  19.4 1.7 %collective-permute-start.3 = (bf16[2,512,128]{2,1,0:T(8,128)(2,1)S(1)}, bf16[2,512,128]{2,1,0:T(8,128)(2,1)S(1)}, u32[]{:S(2)}, u32[]{:S(2)}) collective-permute-start(bf16[2,512,128]{2,1,0:T(8,128)(2,1)S(1)} %get-tuple-element.39), channel_id=1, source_target_pairs={{0,8},{8,0},{16,24},{24,16},{1,9},{9,1},{17,25},{25,17},{2,10},{10... | collective-permute-start | bytes 786440 | tf_op jit(solution)/shard_map/ppermute | solution.py:26
  21.1 17.0 %collective-permute-start.6 = (bf16[2,512,128]{2,1,0:T(8,128)(2,1)S(1)}, bf16[2,512,128]{2,1,0:T(8,128)(2,1)S(1)}, u32[]{:S(2)}, u32[]{:S(2)}) collective-permute-start(bf16[2,512,128]{2,1,0:T(8,128)(2,1)S(1)} %add_convert_fusion), channel_id=1, source_target_pairs={{16,0},{24,8},{17,1},{25,9},{18,2},{26,10},{19,3},{27,11},{20,4},{... | collective-permute-start | bytes 786440 | tf_op jit(solution)/shard_map/ppermute | solution.py:22
  30.0 1.4 %collective-permute-start.5 = (bf16[512,128]{1,0:T(8,128)(2,1)S(1)}, bf16[512,128]{1,0:T(8,128)(2,1)S(1)}, u32[]{:S(2)}, u32[]{:S(2)}) collective-permute-start(bf16[512,128]{1,0:T(8,128)(2,1)S(1)} %get-tuple-element.53), channel_id=1, source_target_pairs={{0,8},{8,0},{16,24},{24,16},{1,9},{9,1},{17,25},{25,17},{2,10},{10... | collective-permute-start | bytes 393224 | tf_op jit(solution)/shard_map/ppermute | solution.py:26
  30.4 1.3 %collective-permute-start.4 = (bf16[512,128]{1,0:T(8,128)(2,1)S(1)}, bf16[512,128]{1,0:T(8,128)(2,1)S(1)}, u32[]{:S(2)}, u32[]{:S(2)}) collective-permute-start(bf16[512,128]{1,0:T(8,128)(2,1)S(1)} %get-tuple-element.54), channel_id=1, source_target_pairs={{0,8},{8,0},{16,24},{24,16},{1,9},{9,1},{17,25},{25,17},{2,10},{10... | collective-permute-start | bytes 393224 | tf_op jit(solution)/shard_map/ppermute | solution.py:26
